TPU v7x, 32 devices: a whole 2x2x4 slice. The times are simulated.
32 devices in a mesh: dp: 8 (over z, x), mp: 4 (over y, core).
Axes of the slice: x: 2, y: 2, z: 4, core: 2. Of those that a mesh axis runs over, the one named last changes fastest.
Arguments:
- layer_input: bfloat16 [4096, 4096], P('dp'), may hold values from -40 to 40
- gate_pre: bfloat16 [4096, 5120], P('dp', 'mp'), may hold values from -5 to 5
- up_pre: bfloat16 [4096, 5120], P('dp', 'mp'), may hold values from -5 to 5
- hidden_cot: bfloat16 [4096, 5120], P('dp', 'mp'), may hold values from -6 to 6
- teacher_ids: int32 [4096], P('dp'), may hold values from 0 to 63
- adv_table: float32 [64], replicated, may hold values from 0.25 to 2
- gate_weight: bfloat16 [4096, 5120], P('dp', 'mp'), may hold values from -0.09375 to 0.09375
- up_weight: bfloat16 [4096, 5120], P('dp', 'mp'), may hold values from -0.09375 to 0.09375
- row_moments: float32 [2, 4096], P(None, 'dp'), may hold values from 0.05 to 0.5
- col_moments: float32 [2, 5120], P(None, 'mp'), may hold values from 0.05 to 0.5
Outputs:
- input_grad: bfloat16 [4096, 4096], P('dp', 'mp')
- gate_update: float32 [4096, 5120], P('dp', 'mp')
- up_update: float32 [4096, 5120], P('dp', 'mp')
- new_rows: float32 [2, 4096], P(None, 'dp')
- new_cols: float32 [2, 5120], P(None, 'mp')
All inputs are finite; a program needn't handle non-finite values.
Results may differ from a plain program's by a relative error of at most 0.011.
Values may be sent and summed in bfloat16 or wider, within the bound.
No kernel may reach another device: no remote copies, remote signals or barrier semaphores. Data moves between devices by JAX's collectives and lax.ppermute only.
A program may use at most 192 MiB of HBM per device.

v0:
```python
import functools
import math

import jax
import jax.numpy as jnp
from jax import lax
from jax.experimental import pallas as pl
from jax.experimental.pallas import tpu as pltpu
from jax.sharding import PartitionSpec as P

decay_rate = 0.9
tanh_scale = math.sqrt(2.0 / math.pi)
cubic_term = 0.044715
f32 = jnp.float32
bf16 = jnp.bfloat16
AXES = ("dp", "mp")
GRID = (4, 2, 2, 2)


def gelu_pair(pre_act):
    argument = tanh_scale * (pre_act + cubic_term * pre_act * pre_act * pre_act)
    tangent = jnp.tanh(argument)
    gelu_value = 0.5 * pre_act * (1.0 + tangent)
    gelu_slope = 0.5 * (1.0 + tangent) + 0.5 * pre_act * (1.0 - tangent * tangent) * tanh_scale * (
        1.0 + 3.0 * cubic_term * pre_act * pre_act
    )
    return (gelu_value, gelu_slope)


def token_advantage(teacher_ids, adv_table):
    classes = adv_table.shape[0]
    class_hit = teacher_ids[:, None] == jnp.arange(classes, dtype=jnp.int32)[None, :]
    return jnp.sum(jnp.where(class_hit, adv_table[None, :], 0.0), axis=1)


def local_any(
    layer_input,
    gate_pre,
    up_pre,
    hidden_cot,
    teacher_ids,
    adv_table,
    gate_weight,
    up_weight,
    row_moments,
    col_moments,
):
    data_size = lax.axis_size("dp")
    model_size = lax.axis_size("mp")
    block_rows = gate_weight.shape[0]
    block_cols = gate_weight.shape[1]
    token_count = layer_input.shape[0]
    advantage = token_advantage(teacher_ids, adv_table)
    weighted = hidden_cot.astype(f32) * advantage[:, None]
    gelu_value, gelu_slope = gelu_pair(gate_pre.astype(f32))
    gate_grad = (weighted * up_pre.astype(f32) * gelu_slope).astype(bf16)
    up_grad = (weighted * gelu_value).astype(bf16)
    contract_last = (((1,), (1,)), ((), ()))
    contract_first = (((0,), (0,)), ((), ()))
    pieces = lax.all_gather((gate_weight, up_weight), "dp", axis=0, tiled=True)
    partial_sum = lax.dot_general(
        gate_grad, pieces[0], contract_last, preferred_element_type=f32
    ) + lax.dot_general(up_grad, pieces[1], contract_last, preferred_element_type=f32)
    input_grad = lax.psum_scatter(
        partial_sum.astype(bf16), "mp", scatter_dimension=1, tiled=True
    )
    grad_scale = 1.0 / math.sqrt(token_count * data_size)
    gate_term = lax.dot_general(layer_input, gate_grad, contract_first, preferred_element_type=f32)
    up_term = lax.dot_general(layer_input, up_grad, contract_first, preferred_element_type=f32)
    summed = lax.psum_scatter(
        jnp.concatenate([gate_term, up_term], axis=1).astype(bf16),
        "dp",
        scatter_dimension=0,
        tiled=True,
    ).astype(f32)
    grad_gate = summed[:, :block_cols] * grad_scale
    grad_up = summed[:, block_cols:] * grad_scale
    squares_gate = grad_gate * grad_gate
    squares_up = grad_up * grad_up
    row_local = jnp.stack([jnp.sum(squares_gate, axis=1), jnp.sum(squares_up, axis=1)])
    col_local = jnp.stack([jnp.sum(squares_gate, axis=0), jnp.sum(squares_up, axis=0)])
    row_total = lax.psum(row_local, "mp")
    col_total = lax.psum(col_local, "dp")
    new_rows = decay_rate * row_moments + (1.0 - decay_rate) * (
        row_total / (block_cols * model_size)
    )
    new_cols = decay_rate * col_moments + (1.0 - decay_rate) * (
        col_total / (block_rows * data_size)
    )
    scaled_gate = grad_gate / jnp.sqrt(new_rows[0][:, None] * new_cols[0][None, :])
    scaled_up = grad_up / jnp.sqrt(new_rows[1][:, None] * new_cols[1][None, :])
    square_sums = lax.psum(
        jnp.stack([jnp.sum(scaled_gate * scaled_gate), jnp.sum(scaled_up * scaled_up)]),
        ("dp", "mp"),
    )
    entry_count = block_rows * data_size * block_cols * model_size
    mean_square = square_sums / entry_count
    gate_update = scaled_gate / jnp.sqrt(mean_square[0] + 1e-06)
    up_update = scaled_up / jnp.sqrt(mean_square[1] + 1e-06)
    return (input_grad, gate_update, up_update, new_rows, new_cols)


def device_number(place):
    number = 0
    for coordinate, size in zip(place, GRID):
        number = number * size + coordinate
    return number


def pairs(target):
    out = []
    for z in range(GRID[0]):
        for x in range(GRID[1]):
            for y in range(GRID[2]):
                for c in range(GRID[3]):
                    place = target(z, x, y, c)
                    if place is not None:
                        out.append((device_number((z, x, y, c)), device_number(place)))
    return out


def flip_z(k):
    return pairs(lambda z, x, y, c: (z ^ k, x, y, c))


FLIP_X = pairs(lambda z, x, y, c: (z, 1 - x, y, c))
FLIP_Y = pairs(lambda z, x, y, c: (z, x, 1 - y, c))
FLIP_C = pairs(lambda z, x, y, c: (z, x, y, 1 - c))
MIDDLE = pairs(lambda z, x, y, c: (3 - z, x, y, c) if z in (1, 2) else None)
OUTWARD = pairs(lambda z, x, y, c: ({1: 0, 2: 3}[z], x, y, c) if z in (1, 2) else None)
INWARD = pairs(lambda z, x, y, c: ({0: 1, 3: 2}[z], x, y, c) if z in (0, 3) else None)


def home(first, half):
    return pairs(lambda z, x, y, c: (z ^ (first + c), x, z >> 1, z & 1) if y == half else None)


def send(value, permutation):
    return lax.ppermute(value, AXES, permutation)


def tie(*values):
    return lax.optimization_barrier(values)


def advantage_of(ids_ref, table_ref):
    ids = ids_ref[...]
    hit = ids == lax.broadcasted_iota(jnp.int32, (ids.shape[0], table_ref.shape[1]), 1)
    return jnp.sum(jnp.where(hit, table_ref[...], 0.0), axis=1, keepdims=True)


def gate_kernel(ids_ref, table_ref, cot_ref, gate_ref, up_ref, out_ref):
    weighted = cot_ref[...].astype(f32) * advantage_of(ids_ref, table_ref)
    slope = gelu_pair(gate_ref[...].astype(f32))[1]
    out_ref[...] = (weighted * up_ref[...].astype(f32) * slope).astype(bf16)


def up_kernel(ids_ref, table_ref, cot_ref, gate_ref, out_ref):
    weighted = cot_ref[...].astype(f32) * advantage_of(ids_ref, table_ref)
    out_ref[...] = (weighted * gelu_pair(gate_ref[...].astype(f32))[0]).astype(bf16)


def front(kernel, teacher_ids, adv_table, arrays):
    tokens, cols = arrays[0].shape
    rows = 128
    block = pl.BlockSpec((rows, cols), lambda i: (i, 0))
    return pl.pallas_call(
        kernel,
        grid=(tokens // rows,),
        in_specs=[
            pl.BlockSpec((rows, 1), lambda i: (i, 0)),
            pl.BlockSpec((1, adv_table.shape[0]), lambda i: (0, 0)),
        ]
        + [block] * len(arrays),
        out_specs=block,
        out_shape=jax.ShapeDtypeStruct((tokens, cols), bf16),
        cost_estimate=pl.CostEstimate(
            flops=tokens * cols, bytes_accessed=tokens * cols, transcendentals=0
        ),
    )(teacher_ids[:, None], adv_table[None, :], *arrays)


def dot_first(a, b):
    return lax.dot_general(a, b, (((0,), (0,)), ((), ())), preferred_element_type=f32)


def dot_last(a, b):
    return lax.dot_general(a, b, (((1,), (1,)), ((), ())), preferred_element_type=f32)


def sum_over(value, permutations):
    for permutation in permutations:
        value = value + send(value, permutation)
    return value


OVER_DP = (FLIP_X, flip_z(1), flip_z(2))
OVER_MP = (FLIP_C, FLIP_Y)


def local_block(
    layer_input,
    gate_pre,
    up_pre,
    hidden_cot,
    teacher_ids,
    adv_table,
    gate_weight,
    up_weight,
    row_moments,
    col_moments,
):
    data_size = lax.axis_size("dp")
    model_size = lax.axis_size("mp")
    rows, cols = gate_weight.shape
    tokens = layer_input.shape[0]
    dp = lax.axis_index("dp")
    m = lax.axis_index("mp")
    z, x = dp // 2, dp % 2
    y, c = m // 2, m % 2
    piece_rows = tokens // model_size
    plane = 2 * rows
    grad_scale = 1.0 / math.sqrt(tokens * data_size)

    def plane_rows(own, other):
        both = jnp.zeros((plane, cols), bf16)
        both = lax.dynamic_update_slice(both, own, (x * rows, 0))
        return lax.dynamic_update_slice(both, other, ((1 - x) * rows, 0))

    def over_core(first, second):
        keep = jnp.where(c == 0, first, second)
        away = jnp.where(c == 0, second, first).astype(bf16)
        return keep, away

    def over_y(block):
        part = tokens // 2
        keep = lax.dynamic_slice(block, (y * part, 0), (part, plane))
        away = lax.dynamic_slice(block, ((1 - y) * part, 0), (part, plane)).astype(bf16)
        return keep, away

    def gradient(keep, recv):
        return (keep + recv.astype(f32)) * grad_scale

    mine = lax.dynamic_slice(layer_input, (m * piece_rows, 0), (piece_rows, layer_input.shape[1]))
    piece = [
        send(lax.dynamic_slice(mine, (0, (z ^ k) * plane), (piece_rows, plane)), flip_z(k))
        for k in (1, 2, 3)
    ]
    gate_other = send(gate_weight, FLIP_X)
    g = front(gate_kernel, teacher_ids, adv_table, (hidden_cot, gate_pre, up_pre))
    u = front(up_kernel, teacher_ids, adv_table, (hidden_cot, gate_pre))
    piece, g, u, gate_other, up_weight = tie(piece, g, u, gate_other, up_weight)

    g_near = send(g, flip_z(1))
    g_over = send(g, MIDDLE)
    u_near = send(u, flip_z(1))
    u_over = send(u, MIDDLE)
    up_other = send(up_weight, FLIP_X)
    piece = jnp.stack(piece)
    g_near, g_over, up_other, piece = tie(g_near, g_over, up_other, piece)

    g_far = send(g_over, OUTWARD)
    g_near_over = send(g_near, MIDDLE)
    piece_y = send(piece, FLIP_Y)
    gate_rows = plane_rows(gate_weight, gate_other)
    up_rows = plane_rows(up_weight, up_other)
    u_near, u_over, gate_rows, up_rows, piece, piece_y = tie(
        u_near, u_over, gate_rows, up_rows, piece, piece_y
    )

    u_far = send(u_over, OUTWARD)
    u_near_over = send(u_near, MIDDLE)
    pieces = jnp.stack([piece, piece_y])
    pieces_c = send(pieces, FLIP_C)
    early = dot_last(jnp.concatenate([g, g_near], axis=0), gate_rows)
    early = early + dot_last(jnp.concatenate([u, u_near], axis=0), up_rows)
    early_keep, early_away = over_core(early[:tokens], early[tokens:])
    g_far, g_near_over, pieces, pieces_c, early_keep, early_away = tie(
        g_far, g_near_over, pieces, pieces_c, early_keep, early_away
    )

    early_recv = send(early_away, FLIP_C)
    g_farthest = send(g_near_over, OUTWARD)
    far = jnp.zeros((3, model_size, piece_rows, plane), bf16)
    for part, place in ((pieces[0], m), (pieces_c[0], m ^ 1), (pieces[1], m ^ 2), (pieces_c[1], m ^ 3)):
        far = lax.dynamic_update_slice(far, part[:, None], (0, place, 0, 0))
    own_inputs = lax.dynamic_slice(layer_input, (0, z * plane), (tokens, plane))
    inputs = jnp.concatenate([own_inputs, far.reshape(3 * tokens, plane)])
    near_tokens = 3 * tokens
    inputs_keep = lax.dynamic_slice(inputs, (0, x * rows), (4 * tokens, rows))
    inputs_away = lax.dynamic_slice(inputs, (0, (1 - x) * rows), (4 * tokens, rows))

    def near_products(block):
        return dot_first(inputs_away[:near_tokens], block), dot_first(inputs_keep[:near_tokens], block)

    def last_products(block, near, span):
        away, keep = near
        away = away[:, span] + dot_first(inputs_away[near_tokens:], block)
        return away.astype(bf16), keep[:, span] + dot_first(inputs_keep[near_tokens:], block)

    g_third = g_near_over + g_far
    g_products = near_products(jnp.concatenate([g, g_near, g_third], axis=0))
    early_keep, early_away = over_y(early_keep + early_recv.astype(f32))
    u_far, u_near_over, g_products, inputs_keep, inputs_away, early_keep, early_away = tie(
        u_far, u_near_over, g_products, inputs_keep, inputs_away, early_keep, early_away
    )

    u_farthest = send(u_near_over, OUTWARD)
    u_third = u_near_over + u_far
    u_products = near_products(jnp.concatenate([u, u_near, u_third], axis=0))
    early_recv = send(early_away, FLIP_Y)
    third = dot_last(g_third, gate_rows) + dot_last(u_third, up_rows)
    u_products, third, early_recv, g_farthest = tie(u_products, third, early_recv, g_farthest)

    g_last = g_over + g_farthest
    away, g_keep = last_products(g_last, g_products, slice(None))
    g_recv = send(away, FLIP_X)
    early_sum = (early_keep + early_recv.astype(f32)).astype(bf16)
    early_home = [send(early_sum, home(0, h)) for h in range(2)]
    g_keep, g_last, u_farthest, g_recv = tie(g_keep, g_last, u_farthest, g_recv)

    block = u_over + u_farthest
    away, up_keep = last_products(block, u_products, slice(None))
    away, block, g_last, early_home = tie(away, block, g_last, early_home)
    up_recv = send(away, FLIP_X)
    last = dot_last(g_last, gate_rows) + dot_last(block, up_rows)
    late_keep, late_away = over_core(third, last)
    late_recv = send(late_away, FLIP_C)
    late_keep, late_away = over_y(late_keep + late_recv.astype(f32))
    gate_gradient = gradient(g_keep, g_recv)
    gate_row = jnp.sum(gate_gradient * gate_gradient, axis=1)
    gate_col = jnp.sum(gate_gradient * gate_gradient, axis=0)
    late_away, late_keep, gate_row, gate_col, gate_gradient, up_keep = tie(
        late_away, late_keep, gate_row, gate_col, gate_gradient, up_keep
    )
    late_recv = send(late_away, FLIP_Y)
    late_sum = (late_keep + late_recv.astype(f32)).astype(bf16)
    late_home = [send(late_sum, home(2, h)) for h in range(2)]
    late_home, up_recv = tie(late_home, up_recv)

    entry_count = rows * data_size * cols * model_size
    up_gradient = gradient(up_keep, up_recv)
    gradients = (gate_gradient, up_gradient)
    squares = up_gradient * up_gradient
    row_total = sum_over(jnp.stack([gate_row, jnp.sum(squares, axis=1)]), OVER_MP)
    new_rows = decay_rate * row_moments + (1.0 - decay_rate) * (row_total / (cols * model_size))
    inverse = 1.0 / new_rows
    column_sums = jnp.concatenate(
        [gate_col, jnp.sum(squares, axis=0)]
        + [jnp.sum(v * v * inverse[k][:, None], axis=0) for k, v in enumerate(gradients)]
    )
    column_sums = sum_over(column_sums, OVER_DP).reshape(2, 2, cols)
    new_cols = decay_rate * col_moments + (1.0 - decay_rate) * (
        column_sums[0] / (rows * data_size)
    )
    square_sums = jnp.sum(column_sums[1] / new_cols, axis=1)
    square_sums = sum_over(jnp.broadcast_to(square_sums[:, None], (2, 128)), OVER_MP)[:, :1]
    row_factor = lax.rsqrt(new_rows) * lax.rsqrt(square_sums / entry_count + 1e-06)
    col_factor = lax.rsqrt(new_cols)
    updates = [
        v * row_factor[k][:, None] * col_factor[k][None, :] for k, v in enumerate(gradients)
    ]
    input_grad = jnp.concatenate([early_home[h] + late_home[h] for h in range(2)], axis=0)
    return input_grad, updates[0], updates[1], new_rows, new_cols


def solution(mesh):
    in_specs = (
        P("dp", None),
        P("dp", "mp"),
        P("dp", "mp"),
        P("dp", "mp"),
        P("dp"),
        P(),
        P("dp", "mp"),
        P("dp", "mp"),
        P(None, "dp"),
        P(None, "mp"),
    )
    out_specs = (P("dp", "mp"), P("dp", "mp"), P("dp", "mp"), P(None, "dp"), P(None, "mp"))
    fits = (mesh.shape["dp"], mesh.shape["mp"]) == (GRID[0] * GRID[1], GRID[2] * GRID[3])
    local = local_block if fits else local_any
    return jax.shard_map(local, mesh=mesh, in_specs=in_specs, out_specs=out_specs, check_vma=False)
```

profile of v0, /device:TPU:1, one launch (start us, length us, event | category | flops | bytes accessed | tf_op | source)
XLA Modules:
  0.0 289.5 jit_solution(9640645713168641312)
XLA Ops:
  2.7 2.5 fusion.39
  6.5 2.3 collective-permute-start.1
  10.4 4.4 %shard_map.138 = bf16[512,1280]{1,0:T(8,128)(2,1)} custom-call(s32[512,1]{1,0:T(8,128)} %copy.15.ids_ref, f32[1,64]{1,0:T(1,128)} %bitcast.60, bf16[512,1280]{1,0:T(8,128)(2,1)} %cot_ref.3, bf16[512,1280]{1,0:T(8,128)(2,1)} %gate_ref.3), custom_call_target="tpu_custom_call" | custom-call | flops 655360 | bytes 655360 | tf_op jit(solution)/shard_map/pallas_call | solution.py:167
  14.8 6.4 %shard_map.137 = bf16[512,1280]{1,0:T(8,128)(2,1)} custom-call(s32[512,1]{1,0:T(8,128)} %copy.15.ids_ref, f32[1,64]{1,0:T(1,128)} %bitcast.61, bf16[512,1280]{1,0:T(8,128)(2,1)} %cot_ref.3, bf16[512,1280]{1,0:T(8,128)(2,1)} %gate_ref.3, bf16[512,1280]{1,0:T(8,128)(2,1)} %up_ref.1), custom_call_target="tpu_custom_call" | custom-call | flops 655360 | bytes 655360 | tf_op jit(solution)/shard_map/pallas_call | solution.py:167
  21.2 4.4 %collective-permute-done.2 = bf16[128,1024]{1,0:T(8,128)(2,1)S(1)} collective-permute-done((bf16[128,1024]{1,0:T(8,128)(2,1)}, bf16[128,1024]{1,0:T(8,128)(2,1)S(1)}, u32[]{:S(2)}, u32[]{:S(2)}) %collective-permute-start.2) | collective-permute-done | bytes 262176 | tf_op jit(solution)/shard_map/ppermute | solution.py:139
  25.6 5.9 %collective-permute-done.3 = bf16[512,1280]{1,0:T(8,128)(2,1)S(1)} collective-permute-done((bf16[512,1280]{1,0:T(8,128)(2,1)}, bf16[512,1280]{1,0:T(8,128)(2,1)S(1)}, u32[]{:S(2)}, u32[]{:S(2)}) %collective-permute-start.3) | collective-permute-done | bytes 1310752 | tf_op jit(solution)/shard_map/ppermute | solution.py:139
  35.6 2.8 collective-permute-start.4
  41.4 19.4 %collective-permute-done.6 = bf16[512,1280]{1,0:T(8,128)(2,1)} collective-permute-done((bf16[512,1280]{1,0:T(8,128)(2,1)}, bf16[512,1280]{1,0:T(8,128)(2,1)}, u32[]{:S(2)}, u32[]{:S(2)}) %collective-permute-start.6) | collective-permute-done | bytes 1310752 | tf_op jit(solution)/shard_map/ppermute | solution.py:139
  60.8 2.2 collective-permute-done.8
  71.5 17.4 %collective-permute-done.4 = bf16[512,1280]{1,0:T(8,128)(2,1)} collective-permute-done((bf16[512,1280]{1,0:T(8,128)(2,1)}, bf16[512,1280]{1,0:T(8,128)(2,1)}, u32[]{:S(2)}, u32[]{:S(2)}) %collective-permute-start.4) | collective-permute-done | bytes 1310752 | tf_op jit(solution)/shard_map/ppermute | solution.py:139
  92.2 4.0 %collective-permute-start.14 = (bf16[2,3,128,1024]{3,2,1,0:T(8,128)(2,1)S(1)}, bf16[2,3,128,1024]{3,2,1,0:T(8,128)(2,1)S(1)}, u32[]{:S(2)}, u32[]{:S(2)}) collective-permute-start(bf16[2,3,128,1024]{3,2,1,0:T(8,128)(2,1)S(1)} %pad_maximum_fusion.6), channel_id=1, source_target_pairs={{0,1},{1,0},{2,3},{3,2},{4,5},{5,4},{6,7},{7,6},{8,9},{9,8},{10,11... | collective-permute-start | bytes 4718600 | tf_op jit(solution)/shard_map/ppermute | solution.py:139
  96.2 4.6 %fusion.4 = f32[1024,1024]{1,0:T(8,128)S(1)} fusion(bf16[1024,1280]{1,0:T(8,128)(2,1)S(1)} %get-tuple-element.75, bf16[512,1280]{1,0:T(8,128)(2,1)} %collective-permute-done.4, bf16[512,1280]{1,0:T(8,128)(2,1)} %shard_map.138), kind=kOutput, calls=%fused_computation.10 | convolution fusion | flops 2689597440 | bytes 9437184 | tf_op jit(solution)/shard_map/dot_general | solution.py:188
  100.8 4.3 %fusion.12 = f32[1024,1024]{1,0:T(8,128)S(1)} fusion(f32[1024,1024]{1,0:T(8,128)S(1)} %fusion.4, bf16[1024,1280]{1,0:T(8,128)(2,1)S(1)} %get-tuple-element.74, bf16[512,1280]{1,0:T(8,128)(2,1)} %collective-permute-done.6, bf16[512,1280]{1,0:T(8,128)(2,1)S(1)} %copy-done.7), kind=kOutput, calls=%fused_computation.34 | convolution fusion | flops 2690646016 | bytes 13631488 | tf_op jit(solution)/shard_map/dot_general | solution.py:188
  105.9 11.0 %collective-permute-done.12 = bf16[512,1280]{1,0:T(8,128)(2,1)S(1)} collective-permute-done((bf16[512,1280]{1,0:T(8,128)(2,1)}, bf16[512,1280]{1,0:T(8,128)(2,1)S(1)}, u32[]{:S(2)}, u32[]{:S(2)}) %collective-permute-start.12) | collective-permute-done | bytes 1310752 | tf_op jit(solution)/shard_map/ppermute | solution.py:139
  118.7 4.0 %collective-permute-start.15 = (bf16[512,1024]{1,0:T(8,128)(2,1)S(1)}, bf16[512,1024]{1,0:T(8,128)(2,1)S(1)}, u32[]{:S(2)}, u32[]{:S(2)}) collective-permute-start(bf16[512,1024]{1,0:T(8,128)(2,1)S(1)} %select_convert_fusion.1), channel_id=1, source_target_pairs={{0,1},{1,0},{2,3},{3,2},{4,5},{5,4},{6,7},{7,6},{8,9},{9,8},{10,11... | collective-permute-start | bytes 3145736 | tf_op jit(solution)/shard_map/ppermute | solution.py:139
  123.9 3.6 %fusion.18 = f32[512,1280]{1,0:T(8,128)S(1)} fusion(bf16[512,1280]{1,0:T(8,128)(2,1)S(1)} %add.161, bf16[512,1280]{1,0:T(8,128)(2,1)} %collective-permute-done.6, bf16[512,1280]{1,0:T(8,128)(2,1)S(1)} %copy-done.7, bf16[2048,512]{1,0:T(8,128)(2,1)S(1)} %get-tuple-element.82), kind=kOutput, calls=%fused_computation.38 | convolution fusion | flops 2025062400 | bytes 8126464 | tf_op jit(solution)/shard_map/dot_general | solution.py:184
  127.5 3.6 %fusion.17 = f32[512,1280]{1,0:T(8,128)S(1)} fusion(bf16[512,1280]{1,0:T(8,128)(2,1)S(1)} %add.161, bf16[512,1280]{1,0:T(8,128)(2,1)} %collective-permute-done.6, bf16[512,1280]{1,0:T(8,128)(2,1)S(1)} %copy-done.7, bf16[2048,512]{1,0:T(8,128)(2,1)S(1)} %get-tuple-element.85), kind=kOutput, calls=%fused_computation.37 | convolution fusion | flops 2025062400 | bytes 8126464 | tf_op jit(solution)/shard_map/dot_general | solution.py:184
  131.6 13.3 %collective-permute-done.10 = bf16[512,1280]{1,0:T(8,128)(2,1)S(1)} collective-permute-done((bf16[512,1280]{1,0:T(8,128)(2,1)}, bf16[512,1280]{1,0:T(8,128)(2,1)S(1)}, u32[]{:S(2)}, u32[]{:S(2)}) %collective-permute-start.10) | collective-permute-done | bytes 1310752 | tf_op jit(solution)/shard_map/ppermute | solution.py:139
  147.7 4.0 %fusion.16 = f32[512,1280]{1,0:T(8,128)S(1)} fusion(bf16[512,1280]{1,0:T(8,128)(2,1)S(1)} %add.165, bf16[512,1280]{1,0:T(8,128)(2,1)} %collective-permute-done.4, bf16[512,1280]{1,0:T(8,128)(2,1)} %shard_map.138, bf16[2048,512]{1,0:T(8,128)(2,1)S(1)} %get-tuple-element.82), kind=kOutput, calls=%fused_computation.36 | convolution fusion | flops 2025062400 | bytes 8126464 | tf_op jit(solution)/shard_map/dot_general | solution.py:184
  151.8 4.0 %fusion.15 = f32[512,1280]{1,0:T(8,128)S(1)} fusion(bf16[512,1280]{1,0:T(8,128)(2,1)S(1)} %add.165, bf16[512,1280]{1,0:T(8,128)(2,1)} %collective-permute-done.4, bf16[512,1280]{1,0:T(8,128)(2,1)} %shard_map.138, bf16[2048,512]{1,0:T(8,128)(2,1)S(1)} %get-tuple-element.85), kind=kOutput, calls=%fused_computation.35 | convolution fusion | flops 2025062400 | bytes 8126464 | tf_op jit(solution)/shard_map/dot_general | solution.py:184
  158.9 14.2 %collective-permute-done.17 = bf16[512,1280]{1,0:T(8,128)(2,1)S(1)} collective-permute-done((bf16[512,1280]{1,0:T(8,128)(2,1)S(1)}, bf16[512,1280]{1,0:T(8,128)(2,1)S(1)}, u32[]{:S(2)}, u32[]{:S(2)}) %collective-permute-start.17) | collective-permute-done | bytes 1310752 | tf_op jit(solution)/shard_map/ppermute | solution.py:139
  177.0 5.9 %collective-permute-start.20 = (bf16[256,1024]{1,0:T(8,128)(2,1)S(1)}, bf16[256,1024]{1,0:T(8,128)(2,1)S(1)}, u32[]{:S(2)}, u32[]{:S(2)}) collective-permute-start(bf16[256,1024]{1,0:T(8,128)(2,1)S(1)} %add_convert_fusion.3), channel_id=1, source_target_pairs={{0,0},{1,8},{4,4},{5,12},{8,9},{9,1},{12,13},{13,5},{16,18},{17,26... | collective-permute-start | bytes 1572872 | tf_op jit(solution)/shard_map/ppermute | solution.py:139
  185.7 15.4 %collective-permute-done.18 = bf16[512,1280]{1,0:T(8,128)(2,1)S(1)} collective-permute-done((bf16[512,1280]{1,0:T(8,128)(2,1)S(1)}, bf16[512,1280]{1,0:T(8,128)(2,1)S(1)}, u32[]{:S(2)}, u32[]{:S(2)}) %collective-permute-start.18) | collective-permute-done | bytes 1310752 | tf_op jit(solution)/shard_map/ppermute | solution.py:139
  205.3 2.9 collective-permute-done.20
  218.7 11.1 %collective-permute-done.23 = bf16[256,1024]{1,0:T(8,128)(2,1)S(1)} collective-permute-done((bf16[256,1024]{1,0:T(8,128)(2,1)S(1)}, bf16[256,1024]{1,0:T(8,128)(2,1)S(1)}, u32[]{:S(2)}, u32[]{:S(2)}) %collective-permute-start.23) | collective-permute-done | bytes 524320 | tf_op jit(solution)/shard_map/ppermute | solution.py:139
  229.9 6.0 %collective-permute-start.24 = (bf16[256,1024]{1,0:T(8,128)(2,1)S(1)}, bf16[256,1024]{1,0:T(8,128)(2,1)S(1)}, u32[]{:S(2)}, u32[]{:S(2)}) collective-permute-start(bf16[256,1024]{1,0:T(8,128)(2,1)S(1)} %add_convert_fusion.2), channel_id=1, source_target_pairs={{0,16},{1,24},{4,20},{5,28},{8,25},{9,17},{12,29},{13,21},{16,2},{... | collective-permute-start | bytes 1572872 | tf_op jit(solution)/shard_map/ppermute | solution.py:139
  236.6 10.6 %collective-permute-done.26 = bf16[512,1280]{1,0:T(8,128)(2,1)S(1)} collective-permute-done((bf16[512,1280]{1,0:T(8,128)(2,1)S(1)}, bf16[512,1280]{1,0:T(8,128)(2,1)S(1)}, u32[]{:S(2)}, u32[]{:S(2)}) %collective-permute-start.26) | collective-permute-done | bytes 1310752 | tf_op jit(solution)/shard_map/ppermute | solution.py:139
  250.1 11.0 %collective-permute-start.28 = (f32[2,512]{1,0:T(2,128)S(1)}, f32[2,512]{1,0:T(2,128)S(1)}, u32[]{:S(2)}, u32[]{:S(2)}) collective-permute-start(f32[2,512]{1,0:T(2,128)S(1)} %fusion.38), channel_id=1, source_target_pairs={{0,2},{1,3},{2,0},{3,1},{4,6},{5,7},{6,4},{7,5},{8,10},{9,11},{10,... | collective-permute-start | bytes 12296 | tf_op jit(solution)/shard_map/ppermute | solution.py:139
  268.6 3.5 %collective-permute-start.31 = (f32[5120]{0:T(1024)S(1)}, f32[5120]{0:T(1024)S(1)}, u32[]{:S(2)}, u32[]{:S(2)}) collective-permute-start(f32[5120]{0:T(1024)S(1)} %add.185), channel_id=1, source_target_pairs={{0,16},{1,17},{2,18},{3,19},{4,20},{5,21},{6,22},{7,23},{8,24},{9,... | collective-permute-start | bytes 61448 | tf_op jit(solution)/shard_map/ppermute | solution.py:139
  273.5 4.5 %collective-permute-start.32 = (f32[2,128]{0,1:T(8,128)S(1)}, f32[2,128]{0,1:T(8,128)S(1)}, u32[]{:S(2)}, u32[]{:S(2)}) collective-permute-start(f32[2,128]{0,1:T(8,128)S(1)} %broadcast_in_dim.20), channel_id=1, source_target_pairs={{0,1},{1,0},{2,3},{3,2},{4,5},{5,4},{6,7},{7,6},{8,9},{9,8},{10,11... | collective-permute-start | bytes 3080 | tf_op jit(solution)/shard_map/ppermute | solution.py:139
  281.0 2.9 collective-permute-done.33
  284.0 3.6 %multiply_multiply_fusion.1 = f32[512,1280]{1,0:T(8,128)} fusion(f32[512,1280]{1,0:T(8,128)} %copy-done, f32[1280]{0:T(1024)S(1)} %get-tuple-element.118, f32[512]{0:T(512)S(1)} %bitcast.57), kind=kLoop, calls=%fused_computation.15 | loop fusion | flops 1310720 | bytes 5250048 | tf_op jit(solution)/shard_map/mul | solution.py:361
  (144 shorter events, 72.8 us)
Async XLA Ops:
  0.6 30.8 %collective-permute-start.3 = (bf16[512,1280]{1,0:T(8,128)(2,1)}, bf16[512,1280]{1,0:T(8,128)(2,1)S(1)}, u32[]{:S(2)}, u32[]{:S(2)}) collective-permute-start(bf16[512,1280]{1,0:T(8,128)(2,1)} %param.16), channel_id=1, source_target_pairs={{0,4},{1,5},{2,6},{3,7},{4,0},{5,1},{6,2},{7,3},{8,12},{9,13},{10,... | collective-permute-start | bytes 3932168 | tf_op jit(solution)/shard_map/ppermute | solution.py:139
  5.2 15.9 %collective-permute-start = (bf16[128,1024]{1,0:T(8,128)(2,1)}, bf16[128,1024]{1,0:T(8,128)(2,1)S(1)}, u32[]{:S(2)}, u32[]{:S(2)}) collective-permute-start(bf16[128,1024]{1,0:T(8,128)(2,1)} %get-tuple-element.128), channel_id=1, source_target_pairs={{0,8},{1,9},{2,10},{3,11},{4,12},{5,13},{6,14},{7,15},{8,0},{9,1},... | collective-permute-start | bytes 786440 | tf_op jit(solution)/shard_map/ppermute | solution.py:139
  6.5 14.6 %collective-permute-start.1 = (bf16[128,1024]{1,0:T(8,128)(2,1)}, bf16[128,1024]{1,0:T(8,128)(2,1)S(1)}, u32[]{:S(2)}, u32[]{:S(2)}) collective-permute-start(bf16[128,1024]{1,0:T(8,128)(2,1)} %get-tuple-element.127), channel_id=1, source_target_pairs={{0,16},{1,17},{2,18},{3,19},{4,20},{5,21},{6,22},{7,23},{8,24},{9,... | collective-permute-start | bytes 786440 | tf_op jit(solution)/shard_map/ppermute | solution.py:139
  8.8 16.8 %collective-permute-start.2 = (bf16[128,1024]{1,0:T(8,128)(2,1)}, bf16[128,1024]{1,0:T(8,128)(2,1)S(1)}, u32[]{:S(2)}, u32[]{:S(2)}) collective-permute-start(bf16[128,1024]{1,0:T(8,128)(2,1)} %get-tuple-element.126), channel_id=1, source_target_pairs={{0,24},{1,25},{2,26},{3,27},{4,28},{5,29},{6,30},{7,31},{8,16},{9,... | collective-permute-start | bytes 786440 | tf_op jit(solution)/shard_map/ppermute | solution.py:139
  31.5 29.4 %collective-permute-start.6 = (bf16[512,1280]{1,0:T(8,128)(2,1)}, bf16[512,1280]{1,0:T(8,128)(2,1)}, u32[]{:S(2)}, u32[]{:S(2)}) collective-permute-start(bf16[512,1280]{1,0:T(8,128)(2,1)} %shard_map.137), channel_id=1, source_target_pairs={{0,8},{1,9},{2,10},{3,11},{4,12},{5,13},{6,14},{7,15},{8,0},{9,1},... | collective-permute-start | bytes 3932168 | tf_op jit(solution)/shard_map/ppermute | solution.py:139
  32.7 28.1 %collective-permute-start.7 = (bf16[512,1280]{1,0:T(8,128)(2,1)}, bf16[512,1280]{1,0:T(8,128)(2,1)}, u32[]{:S(2)}, u32[]{:S(2)}) collective-permute-start(bf16[512,1280]{1,0:T(8,128)(2,1)} %shard_map.137), channel_id=1, source_target_pairs={{8,16},{9,17},{10,18},{11,19},{12,20},{13,21},{14,22},{15,23},{16,... | collective-permute-start | bytes 3932168 | tf_op jit(solution)/shard_map/ppermute | solution.py:139
  34.4 28.5 %collective-permute-start.8 = (bf16[512,1280]{1,0:T(8,128)(2,1)S(1)}, bf16[512,1280]{1,0:T(8,128)(2,1)}, u32[]{:S(2)}, u32[]{:S(2)}) collective-permute-start(bf16[512,1280]{1,0:T(8,128)(2,1)S(1)} %copy-done.3), channel_id=1, source_target_pairs={{0,4},{1,5},{2,6},{3,7},{4,0},{5,1},{6,2},{7,3},{8,12},{9,13},{10,... | collective-permute-start | bytes 3932168 | tf_op jit(solution)/shard_map/ppermute | solution.py:139
  35.6 53.3 %collective-permute-start.4 = (bf16[512,1280]{1,0:T(8,128)(2,1)}, bf16[512,1280]{1,0:T(8,128)(2,1)}, u32[]{:S(2)}, u32[]{:S(2)}) collective-permute-start(bf16[512,1280]{1,0:T(8,128)(2,1)} %shard_map.138), channel_id=1, source_target_pairs={{0,8},{1,9},{2,10},{3,11},{4,12},{5,13},{6,14},{7,15},{8,0},{9,1},... | collective-permute-start | bytes 3932168 | tf_op jit(solution)/shard_map/ppermute | solution.py:139
  38.5 50.4 %collective-permute-start.5 = (bf16[512,1280]{1,0:T(8,128)(2,1)}, bf16[512,1280]{1,0:T(8,128)(2,1)}, u32[]{:S(2)}, u32[]{:S(2)}) collective-permute-start(bf16[512,1280]{1,0:T(8,128)(2,1)} %shard_map.138), channel_id=1, source_target_pairs={{8,16},{9,17},{10,18},{11,19},{12,20},{13,21},{14,22},{15,23},{16,... | collective-permute-start | bytes 3932168 | tf_op jit(solution)/shard_map/ppermute | solution.py:139
  63.0 25.9 %collective-permute-start.9 = (bf16[3,128,1024]{2,1,0:T(8,128)(2,1)S(1)}, bf16[3,128,1024]{2,1,0:T(8,128)(2,1)}, u32[]{:S(2)}, u32[]{:S(2)}) collective-permute-start(bf16[3,128,1024]{2,1,0:T(8,128)(2,1)S(1)} %pad_maximum_fusion.8), channel_id=1, source_target_pairs={{0,2},{1,3},{2,0},{3,1},{4,6},{5,7},{6,4},{7,5},{8,10},{9,11},{10,... | collective-permute-start | bytes 2359304 | tf_op jit(solution)/shard_map/ppermute | solution.py:139
  67.7 49.2 %collective-permute-start.12 = (bf16[512,1280]{1,0:T(8,128)(2,1)}, bf16[512,1280]{1,0:T(8,128)(2,1)S(1)}, u32[]{:S(2)}, u32[]{:S(2)}) collective-permute-start(bf16[512,1280]{1,0:T(8,128)(2,1)} %collective-permute-done.7), channel_id=1, source_target_pairs={{8,0},{9,1},{10,2},{11,3},{12,4},{13,5},{14,6},{15,7},{16,24},{17,... | collective-permute-start | bytes 3932168 | tf_op jit(solution)/shard_map/ppermute | solution.py:139
  69.1 47.8 %collective-permute-start.13 = (bf16[512,1280]{1,0:T(8,128)(2,1)}, bf16[512,1280]{1,0:T(8,128)(2,1)S(1)}, u32[]{:S(2)}, u32[]{:S(2)}) collective-permute-start(bf16[512,1280]{1,0:T(8,128)(2,1)} %collective-permute-done.6), channel_id=1, source_target_pairs={{8,16},{9,17},{10,18},{11,19},{12,20},{13,21},{14,22},{15,23},{16,... | collective-permute-start | bytes 3932168 | tf_op jit(solution)/shard_map/ppermute | solution.py:139
  88.9 56.1 %collective-permute-start.10 = (bf16[512,1280]{1,0:T(8,128)(2,1)}, bf16[512,1280]{1,0:T(8,128)(2,1)S(1)}, u32[]{:S(2)}, u32[]{:S(2)}) collective-permute-start(bf16[512,1280]{1,0:T(8,128)(2,1)} %collective-permute-done.5), channel_id=1, source_target_pairs={{8,0},{9,1},{10,2},{11,3},{12,4},{13,5},{14,6},{15,7},{16,24},{17,... | collective-permute-start | bytes 3932168 | tf_op jit(solution)/shard_map/ppermute | solution.py:139
  90.2 54.8 %collective-permute-start.11 = (bf16[512,1280]{1,0:T(8,128)(2,1)}, bf16[512,1280]{1,0:T(8,128)(2,1)S(1)}, u32[]{:S(2)}, u32[]{:S(2)}) collective-permute-start(bf16[512,1280]{1,0:T(8,128)(2,1)} %collective-permute-done.4), channel_id=1, source_target_pairs={{8,16},{9,17},{10,18},{11,19},{12,20},{13,21},{14,22},{15,23},{16,... | collective-permute-start | bytes 3932168 | tf_op jit(solution)/shard_map/ppermute | solution.py:139
  92.2 24.6 %collective-permute-start.14 = (bf16[2,3,128,1024]{3,2,1,0:T(8,128)(2,1)S(1)}, bf16[2,3,128,1024]{3,2,1,0:T(8,128)(2,1)S(1)}, u32[]{:S(2)}, u32[]{:S(2)}) collective-permute-start(bf16[2,3,128,1024]{3,2,1,0:T(8,128)(2,1)S(1)} %pad_maximum_fusion.6), channel_id=1, source_target_pairs={{0,1},{1,0},{2,3},{3,2},{4,5},{5,4},{6,7},{7,6},{8,9},{9,8},{10,11... | collective-permute-start | bytes 4718600 | tf_op jit(solution)/shard_map/ppermute | solution.py:139
  116.9 56.2 %collective-permute-start.17 = (bf16[512,1280]{1,0:T(8,128)(2,1)S(1)}, bf16[512,1280]{1,0:T(8,128)(2,1)S(1)}, u32[]{:S(2)}, u32[]{:S(2)}) collective-permute-start(bf16[512,1280]{1,0:T(8,128)(2,1)S(1)} %collective-permute-done.13), channel_id=1, source_target_pairs={{8,0},{9,1},{10,2},{11,3},{12,4},{13,5},{14,6},{15,7},{16,24},{17,... | collective-permute-start | bytes 3932168 | tf_op jit(solution)/shard_map/ppermute | solution.py:139
  118.7 12.5 %collective-permute-start.15 = (bf16[512,1024]{1,0:T(8,128)(2,1)S(1)}, bf16[512,1024]{1,0:T(8,128)(2,1)S(1)}, u32[]{:S(2)}, u32[]{:S(2)}) collective-permute-start(bf16[512,1024]{1,0:T(8,128)(2,1)S(1)} %select_convert_fusion.1), channel_id=1, source_target_pairs={{0,1},{1,0},{2,3},{3,2},{4,5},{5,4},{6,7},{7,6},{8,9},{9,8},{10,11... | collective-permute-start | bytes 3145736 | tf_op jit(solution)/shard_map/ppermute | solution.py:139
  145.0 56.2 %collective-permute-start.18 = (bf16[512,1280]{1,0:T(8,128)(2,1)S(1)}, bf16[512,1280]{1,0:T(8,128)(2,1)S(1)}, u32[]{:S(2)}, u32[]{:S(2)}) collective-permute-start(bf16[512,1280]{1,0:T(8,128)(2,1)S(1)} %collective-permute-done.11), channel_id=1, source_target_pairs={{8,0},{9,1},{10,2},{11,3},{12,4},{13,5},{14,6},{15,7},{16,24},{17,... | collective-permute-start | bytes 3932168 | tf_op jit(solution)/shard_map/ppermute | solution.py:139
  146.8 26.3 %collective-permute-start.16 = (bf16[256,1024]{1,0:T(8,128)(2,1)S(1)}, bf16[256,1024]{1,0:T(8,128)(2,1)S(1)}, u32[]{:S(2)}, u32[]{:S(2)}) collective-permute-start(bf16[256,1024]{1,0:T(8,128)(2,1)S(1)} %dynamic-slice_convert_fusion.1), channel_id=1, source_target_pairs={{0,2},{1,3},{2,0},{3,1},{4,6},{5,7},{6,4},{7,5},{8,10},{9,11},{10,... | collective-permute-start | bytes 1572872 | tf_op jit(solution)/shard_map/ppermute | solution.py:139
  176.0 26.4 %collective-permute-start.19 = (bf16[512,1280]{1,0:T(8,128)(2,1)S(1)}, bf16[512,1280]{1,0:T(8,128)(2,1)S(1)}, u32[]{:S(2)}, u32[]{:S(2)}) collective-permute-start(bf16[512,1280]{1,0:T(8,128)(2,1)S(1)} %add_convert_fusion.1), channel_id=1, source_target_pairs={{0,4},{1,5},{2,6},{3,7},{4,0},{5,1},{6,2},{7,3},{8,12},{9,13},{10,... | collective-permute-start | bytes 3932168 | tf_op jit(solution)/shard_map/ppermute | solution.py:139
  177.0 31.2 %collective-permute-start.20 = (bf16[256,1024]{1,0:T(8,128)(2,1)S(1)}, bf16[256,1024]{1,0:T(8,128)(2,1)S(1)}, u32[]{:S(2)}, u32[]{:S(2)}) collective-permute-start(bf16[256,1024]{1,0:T(8,128)(2,1)S(1)} %add_convert_fusion.3), channel_id=1, source_target_pairs={{0,0},{1,8},{4,4},{5,12},{8,9},{9,1},{12,13},{13,5},{16,18},{17,26... | collective-permute-start | bytes 1572872 | tf_op jit(solution)/shard_map/ppermute | solution.py:139
  182.9 26.2 %collective-permute-start.21 = (bf16[256,1024]{1,0:T(8,128)(2,1)S(1)}, bf16[256,1024]{1,0:T(8,128)(2,1)S(1)}, u32[]{:S(2)}, u32[]{:S(2)}) collective-permute-start(bf16[256,1024]{1,0:T(8,128)(2,1)S(1)} %add_convert_fusion.3), channel_id=1, source_target_pairs={{2,0},{3,8},{6,4},{7,12},{10,9},{11,1},{14,13},{15,5},{18,18},{19,... | collective-permute-start | bytes 1572872 | tf_op jit(solution)/shard_map/ppermute | solution.py:139
  212.3 3.4 %collective-permute-start.22 = (bf16[512,1024]{1,0:T(8,128)(2,1)S(1)}, bf16[512,1024]{1,0:T(8,128)(2,1)S(1)}, u32[]{:S(2)}, u32[]{:S(2)}) collective-permute-start(bf16[512,1024]{1,0:T(8,128)(2,1)S(1)} %get-tuple-element.135), channel_id=1, source_target_pairs={{0,1},{1,0},{2,3},{3,2},{4,5},{5,4},{6,7},{7,6},{8,9},{9,8},{10,11... | collective-permute-start | bytes 3145736 | tf_op jit(solution)/shard_map/ppermute | solution.py:139
  216.5 13.2 %collective-permute-start.23 = (bf16[256,1024]{1,0:T(8,128)(2,1)S(1)}, bf16[256,1024]{1,0:T(8,128)(2,1)S(1)}, u32[]{:S(2)}, u32[]{:S(2)}) collective-permute-start(bf16[256,1024]{1,0:T(8,128)(2,1)S(1)} %dynamic-slice_convert_fusion), channel_id=1, source_target_pairs={{0,2},{1,3},{2,0},{3,1},{4,6},{5,7},{6,4},{7,5},{8,10},{9,11},{10,... | collective-permute-start | bytes 1572872 | tf_op jit(solution)/shard_map/ppermute | solution.py:139
  217.4 29.7 %collective-permute-start.26 = (bf16[512,1280]{1,0:T(8,128)(2,1)S(1)}, bf16[512,1280]{1,0:T(8,128)(2,1)S(1)}, u32[]{:S(2)}, u32[]{:S(2)}) collective-permute-start(bf16[512,1280]{1,0:T(8,128)(2,1)S(1)} %add_convert_fusion), channel_id=1, source_target_pairs={{0,4},{1,5},{2,6},{3,7},{4,0},{5,1},{6,2},{7,3},{8,12},{9,13},{10,... | collective-permute-start | bytes 3932168 | tf_op jit(solution)/shard_map/ppermute | solution.py:139
  229.9 17.2 %collective-permute-start.24 = (bf16[256,1024]{1,0:T(8,128)(2,1)S(1)}, bf16[256,1024]{1,0:T(8,128)(2,1)S(1)}, u32[]{:S(2)}, u32[]{:S(2)}) collective-permute-start(bf16[256,1024]{1,0:T(8,128)(2,1)S(1)} %add_convert_fusion.2), channel_id=1, source_target_pairs={{0,16},{1,24},{4,20},{5,28},{8,25},{9,17},{12,29},{13,21},{16,2},{... | collective-permute-start | bytes 1572872 | tf_op jit(solution)/shard_map/ppermute | solution.py:139
  235.9 11.3 %collective-permute-start.25 = (bf16[256,1024]{1,0:T(8,128)(2,1)S(1)}, bf16[256,1024]{1,0:T(8,128)(2,1)S(1)}, u32[]{:S(2)}, u32[]{:S(2)}) collective-permute-start(bf16[256,1024]{1,0:T(8,128)(2,1)S(1)} %add_convert_fusion.2), channel_id=1, source_target_pairs={{2,16},{3,24},{6,20},{7,28},{10,25},{11,17},{14,29},{15,21},{18,2}... | collective-permute-start | bytes 1572872 | tf_op jit(solution)/shard_map/ppermute | solution.py:139
  250.1 12.0 %collective-permute-start.28 = (f32[2,512]{1,0:T(2,128)S(1)}, f32[2,512]{1,0:T(2,128)S(1)}, u32[]{:S(2)}, u32[]{:S(2)}) collective-permute-start(f32[2,512]{1,0:T(2,128)S(1)} %fusion.38), channel_id=1, source_target_pairs={{0,2},{1,3},{2,0},{3,1},{4,6},{5,7},{6,4},{7,5},{8,10},{9,11},{10,... | collective-permute-start | bytes 12296 | tf_op jit(solution)/shard_map/ppermute | solution.py:139
  263.2 2.7 collective-permute-start.29
  268.6 4.7 %collective-permute-start.31 = (f32[5120]{0:T(1024)S(1)}, f32[5120]{0:T(1024)S(1)}, u32[]{:S(2)}, u32[]{:S(2)}) collective-permute-start(f32[5120]{0:T(1024)S(1)} %add.185), channel_id=1, source_target_pairs={{0,16},{1,17},{2,18},{3,19},{4,20},{5,21},{6,22},{7,23},{8,24},{9,... | collective-permute-start | bytes 61448 | tf_op jit(solution)/shard_map/ppermute | solution.py:139
  273.5 6.6 %collective-permute-start.32 = (f32[2,128]{0,1:T(8,128)S(1)}, f32[2,128]{0,1:T(8,128)S(1)}, u32[]{:S(2)}, u32[]{:S(2)}) collective-permute-start(f32[2,128]{0,1:T(8,128)S(1)} %broadcast_in_dim.20), channel_id=1, source_target_pairs={{0,1},{1,0},{2,3},{3,2},{4,5},{5,4},{6,7},{7,6},{8,9},{9,8},{10,11... | collective-permute-start | bytes 3080 | tf_op jit(solution)/shard_map/ppermute | solution.py:139
  280.1 3.8 %collective-permute-start.33 = (f32[2,128]{0,1:T(8,128)S(1)}, f32[2,128]{0,1:T(8,128)S(1)}, u32[]{:S(2)}, u32[]{:S(2)}) collective-permute-start(f32[2,128]{0,1:T(8,128)S(1)} %broadcast_add_fusion), channel_id=1, source_target_pairs={{0,2},{1,3},{2,0},{3,1},{4,6},{5,7},{6,4},{7,5},{8,10},{9,11},{10,... | collective-permute-start | bytes 3080 | tf_op jit(solution)/shard_map/ppermute | solution.py:139
  (17 other events, 280.8 us)
where the time goes:
time: 291 us; the launch traced here: 290 us
  waiting for transfers between devices  138 us (47%)
  starting transfers between devices  73.8 us (25%)
  matrix products  34 us (12%)
  other arithmetic  21.5 us (7%)
  Pallas kernels  10.8 us (4%)
  local copies, waits for them, and re-layouts  10.1 us (3%)
    ppermute x34, waiting for transfers between devices, send(): return lax.ppermute(value, AXES, permutation)  138 us
    ppermute x34, starting transfers between devices, send(): return lax.ppermute(value, AXES, permutation)  73.8 us
    dot_general x8, matrix products, dot_first(): lax.dot_general(a, b, (((0,), (0,)), ((), ())), preferred_element_type=f32)  18.8 us
    dot_general x6, matrix products, dot_last(): lax.dot_general(a, b, (((1,), (1,)), ((), ())), preferred_element_type=f32)  15.2 us
    pallas_call x2, Pallas kernels, front(): pl.pallas_call(kernel, grid=(tokens // rows,), in_specs=[pl.BlockSpec((ro...  10.8 us
  transfers between devices with their start and end apart: 34, of which 20 were waited for; matrix products, arithmetic and copies ran while one was open for 19% of the time, Pallas kernels for 4%

commit v1 on v0

--- a/solution.py
+++ b/solution.py
@@ -135,6 +135,20 @@
     return pairs(lambda z, x, y, c: (z ^ (first + c), x, z >> 1, z & 1) if y == half else None)
 
 
+def home_from(core, k, half):
+    return pairs(
+        lambda z, x, y, c: (z ^ k, x, z >> 1, z & 1) if (y, c) == (half, core) else None
+    )
+
+
+def to_core(core):
+    return pairs(lambda z, x, y, c: (z, x, y, core) if c != core else None)
+
+
+def flip_y_of(core):
+    return pairs(lambda z, x, y, c: (z, x, 1 - y, c) if c == core else None)
+
+
 def send(value, permutation):
     return lax.ppermute(value, AXES, permutation)
 
@@ -220,6 +234,8 @@
     y, c = m // 2, m % 2
     piece_rows = tokens // model_size
     plane = 2 * rows
+    edge = cols * 4 // 10 // 128 * 128
+    up_spans = [slice(0, edge), slice(edge, cols)]
     grad_scale = 1.0 / math.sqrt(tokens * data_size)
 
     def plane_rows(own, other):
@@ -268,19 +284,19 @@
         u_near, u_over, gate_rows, up_rows, piece, piece_y
     )
 
-    u_far = send(u_over, OUTWARD)
     u_near_over = send(u_near, MIDDLE)
     pieces = jnp.stack([piece, piece_y])
     pieces_c = send(pieces, FLIP_C)
     early = dot_last(jnp.concatenate([g, g_near], axis=0), gate_rows)
     early = early + dot_last(jnp.concatenate([u, u_near], axis=0), up_rows)
     early_keep, early_away = over_core(early[:tokens], early[tokens:])
-    g_far, g_near_over, pieces, pieces_c, early_keep, early_away = tie(
-        g_far, g_near_over, pieces, pieces_c, early_keep, early_away
+    g_far, g_near_over, pieces, pieces_c, early_keep, early_away, u_over = tie(
+        g_far, g_near_over, pieces, pieces_c, early_keep, early_away, u_over
     )
 
     early_recv = send(early_away, FLIP_C)
     g_farthest = send(g_near_over, OUTWARD)
+    u_far = send(u_over, OUTWARD)
     far = jnp.zeros((3, model_size, piece_rows, plane), bf16)
     for part, place in ((pieces[0], m), (pieces_c[0], m ^ 1), (pieces[1], m ^ 2), (pieces_c[1], m ^ 3)):
         far = lax.dynamic_update_slice(far, part[:, None], (0, place, 0, 0))
@@ -301,45 +317,60 @@
     g_third = g_near_over + g_far
     g_products = near_products(jnp.concatenate([g, g_near, g_third], axis=0))
     early_keep, early_away = over_y(early_keep + early_recv.astype(f32))
-    u_far, u_near_over, g_products, inputs_keep, inputs_away, early_keep, early_away = tie(
-        u_far, u_near_over, g_products, inputs_keep, inputs_away, early_keep, early_away
-    )
-
-    u_farthest = send(u_near_over, OUTWARD)
-    u_third = u_near_over + u_far
-    u_products = near_products(jnp.concatenate([u, u_near, u_third], axis=0))
-    early_recv = send(early_away, FLIP_Y)
-    third = dot_last(g_third, gate_rows) + dot_last(u_third, up_rows)
-    u_products, third, early_recv, g_farthest = tie(u_products, third, early_recv, g_farthest)
-
+    u_near_over, g_farthest, g_products, inputs_keep, inputs_away, early_keep, early_away = tie(
+        u_near_over, g_farthest, g_products, inputs_keep, inputs_away, early_keep, early_away
+    )
+
+    u_farthest = [send(u_near_over[:, span], OUTWARD) for span in up_spans]
     g_last = g_over + g_farthest
     away, g_keep = last_products(g_last, g_products, slice(None))
     g_recv = send(away, FLIP_X)
+    early_recv = send(early_away, FLIP_Y)
+    u_far, early_recv, g_keep, g_last = tie(u_far, early_recv, g_keep, g_last)
+
+    u_third = u_near_over + u_far
+    u_products = near_products(jnp.concatenate([u, u_near, u_third], axis=0))
+    third = dot_last(g_third, gate_rows) + dot_last(u_third, up_rows)
     early_sum = (early_keep + early_recv.astype(f32)).astype(bf16)
+    third_recv = send(third.astype(bf16), to_core(0))
+    u_products, third, third_recv, early_sum, u_farthest[0], g_recv = tie(
+        u_products, third, third_recv, early_sum, u_farthest[0], g_recv
+    )
+
+    block = u_over[:, up_spans[0]] + u_farthest[0]
+    away, first_keep = last_products(block, u_products, up_spans[0])
+    first_recv = send(away, FLIP_X)
+    last = dot_last(g_last, gate_rows) + dot_last(block, up_rows[:, up_spans[0]])
     early_home = [send(early_sum, home(0, h)) for h in range(2)]
-    g_keep, g_last, u_farthest, g_recv = tie(g_keep, g_last, u_farthest, g_recv)
-
-    block = u_over + u_farthest
-    away, up_keep = last_products(block, u_products, slice(None))
-    away, block, g_last, early_home = tie(away, block, g_last, early_home)
-    up_recv = send(away, FLIP_X)
-    last = dot_last(g_last, gate_rows) + dot_last(block, up_rows)
-    late_keep, late_away = over_core(third, last)
-    late_recv = send(late_away, FLIP_C)
-    late_keep, late_away = over_y(late_keep + late_recv.astype(f32))
+    third_keep, third_away = over_y(third + third_recv.astype(f32))
+    third_recv = send(third_away, flip_y_of(0))
+    last, first_keep, first_recv, u_farthest[1], early_home, third_keep, third_recv = tie(
+        last, first_keep, first_recv, u_farthest[1], early_home, third_keep, third_recv
+    )
+
+    block = u_over[:, up_spans[1]] + u_farthest[1]
+    away, second_keep = last_products(block, u_products, up_spans[1])
+    second_recv = send(away, FLIP_X)
+    last = last + dot_last(block, up_rows[:, up_spans[1]])
+    late_recv = send(last.astype(bf16), to_core(1))
+    third_sum = (third_keep + third_recv.astype(f32)).astype(bf16)
+    third_home = [send(third_sum, home_from(0, 2, h)) for h in range(2)]
+    late_keep, late_away = over_y(last + late_recv.astype(f32))
     gate_gradient = gradient(g_keep, g_recv)
     gate_row = jnp.sum(gate_gradient * gate_gradient, axis=1)
     gate_col = jnp.sum(gate_gradient * gate_gradient, axis=0)
-    late_away, late_keep, gate_row, gate_col, gate_gradient, up_keep = tie(
-        late_away, late_keep, gate_row, gate_col, gate_gradient, up_keep
-    )
-    late_recv = send(late_away, FLIP_Y)
+    late_away, late_keep, gate_row, gate_col, gate_gradient, second_keep = tie(
+        late_away, late_keep, gate_row, gate_col, gate_gradient, second_keep
+    )
+    late_recv = send(late_away, flip_y_of(1))
+    late_recv, second_recv, third_home = tie(late_recv, second_recv, third_home)
     late_sum = (late_keep + late_recv.astype(f32)).astype(bf16)
-    late_home = [send(late_sum, home(2, h)) for h in range(2)]
-    late_home, up_recv = tie(late_home, up_recv)
+    late_home = [send(late_sum, home_from(1, 3, h)) for h in range(2)]
 
     entry_count = rows * data_size * cols * model_size
-    up_gradient = gradient(up_keep, up_recv)
+    up_gradient = jnp.concatenate(
+        [gradient(first_keep, first_recv), gradient(second_keep, second_recv)], axis=1
+    )
     gradients = (gate_gradient, up_gradient)
     squares = up_gradient * up_gradient
     row_total = sum_over(jnp.stack([gate_row, jnp.sum(squares, axis=1)]), OVER_MP)
@@ -360,7 +391,9 @@
     updates = [
         v * row_factor[k][:, None] * col_factor[k][None, :] for k, v in enumerate(gradients)
     ]
-    input_grad = jnp.concatenate([early_home[h] + late_home[h] for h in range(2)], axis=0)
+    input_grad = jnp.concatenate(
+        [early_home[h] + third_home[h] + late_home[h] for h in range(2)], axis=0
+    )
     return input_grad, updates[0], updates[1], new_rows, new_cols
 
 

time: 291 us -> 286 us (0.983)
  starting transfers between devices: 73.8 us -> 67.3 us
  local copies, waits for them, and re-layouts: 10.1 us -> 15.7 us
  waiting for transfers between devices: 138 us -> 133 us
  matrix products: 34 us -> 37.6 us
    ppermute x34 -> x40, starting transfers between devices: 73.8 us -> 67.3 us  [send(): return lax.ppermute(value, AXES, permutation)]
    ppermute x34 -> x40, waiting for transfers between devices: 138 us -> 133 us  [send(): return lax.ppermute(value, AXES, permutation)]
    dot_general x6 -> x7, matrix products: 15.2 us -> 19.2 us  [dot_last(): lax.dot_general(a, b, (((1,), (1,)), ((), ())), preferred_element_type=f32)]
    dot_general x8 -> x10, matrix products: 18.8 us -> 18.4 us  [dot_first(): lax.dot_general(a, b, (((0,), (0,)), ((), ())), preferred_element_type=f32)]
  transfers between devices with their start and end apart: 34 -> 40, of which waited for: 20 -> 21; matrix products, arithmetic and copies ran while one was open for 19% -> 24% of each run, Pallas kernels for 4% -> 4%
where the time goes in v1:
time: 286 us; the launch traced here: 285 us
  waiting for transfers between devices  133 us (47%)
  starting transfers between devices  67.3 us (24%)
  matrix products  37.6 us (13%)
  other arithmetic  18.7 us (7%)
  local copies, waits for them, and re-layouts  15.7 us (5%)
  Pallas kernels  10.8 us (4%)
    ppermute x40, waiting for transfers between devices, send(): return lax.ppermute(value, AXES, permutation)  133 us
    ppermute x40, starting transfers between devices, send(): return lax.ppermute(value, AXES, permutation)  67.3 us
    dot_general x7, matrix products, dot_last(): lax.dot_general(a, b, (((1,), (1,)), ((), ())), preferred_element_type=f32)  19.2 us
    dot_general x10, matrix products, dot_first(): lax.dot_general(a, b, (((0,), (0,)), ((), ())), preferred_element_type=f32)  18.4 us
    pallas_call x2, Pallas kernels, front(): pl.pallas_call(kernel, grid=(tokens // rows,), in_specs=[pl.BlockSpec((ro...  10.8 us
  transfers between devices with their start and end apart: 40, of which 21 were waited for; matrix products, arithmetic and copies ran while one was open for 24% of the time, Pallas kernels for 4%

profile of v1, /device:TPU:1, one launch (start us, length us, event | category | flops | bytes accessed | tf_op | source)
XLA Modules:
  0.0 284.9 jit_solution(14404376874513250690)
XLA Ops:
  2.7 2.5 fusion.54
  10.4 4.4 %shard_map.138 = bf16[512,1280]{1,0:T(8,128)(2,1)} custom-call(s32[512,1]{1,0:T(8,128)} %copy.15.ids_ref, f32[1,64]{1,0:T(1,128)} %bitcast.56, bf16[512,1280]{1,0:T(8,128)(2,1)} %cot_ref.3, bf16[512,1280]{1,0:T(8,128)(2,1)} %gate_ref.3), custom_call_target="tpu_custom_call" | custom-call | flops 655360 | bytes 655360 | tf_op jit(solution)/shard_map/pallas_call | solution.py:181
  14.8 6.4 %shard_map.137 = bf16[512,1280]{1,0:T(8,128)(2,1)} custom-call(s32[512,1]{1,0:T(8,128)} %copy.15.ids_ref, f32[1,64]{1,0:T(1,128)} %bitcast.57, bf16[512,1280]{1,0:T(8,128)(2,1)} %cot_ref.3, bf16[512,1280]{1,0:T(8,128)(2,1)} %gate_ref.3, bf16[512,1280]{1,0:T(8,128)(2,1)} %up_ref.1), custom_call_target="tpu_custom_call" | custom-call | flops 655360 | bytes 655360 | tf_op jit(solution)/shard_map/pallas_call | solution.py:181
  21.2 4.4 %collective-permute-done.2 = bf16[128,1024]{1,0:T(8,128)(2,1)S(1)} collective-permute-done((bf16[128,1024]{1,0:T(8,128)(2,1)}, bf16[128,1024]{1,0:T(8,128)(2,1)S(1)}, u32[]{:S(2)}, u32[]{:S(2)}) %collective-permute-start.2) | collective-permute-done | bytes 262176 | tf_op jit(solution)/shard_map/ppermute | solution.py:153
  25.6 5.9 %collective-permute-done.3 = bf16[512,1280]{1,0:T(8,128)(2,1)S(1)} collective-permute-done((bf16[512,1280]{1,0:T(8,128)(2,1)}, bf16[512,1280]{1,0:T(8,128)(2,1)S(1)}, u32[]{:S(2)}, u32[]{:S(2)}) %collective-permute-start.3) | collective-permute-done | bytes 1310752 | tf_op jit(solution)/shard_map/ppermute | solution.py:153
  36.4 4.1 %collective-permute-start.9 = (bf16[512,1280]{1,0:T(8,128)(2,1)S(1)}, bf16[512,1280]{1,0:T(8,128)(2,1)}, u32[]{:S(2)}, u32[]{:S(2)}) collective-permute-start(bf16[512,1280]{1,0:T(8,128)(2,1)S(1)} %copy-done.1), channel_id=1, source_target_pairs={{0,8},{1,9},{2,10},{3,11},{4,12},{5,13},{6,14},{7,15},{8,0},{9,1},... | collective-permute-start | bytes 3932168 | tf_op jit(solution)/shard_map/ppermute | solution.py:153
  41.8 19.0 %collective-permute-done.4 = bf16[512,1280]{1,0:T(8,128)(2,1)} collective-permute-done((bf16[512,1280]{1,0:T(8,128)(2,1)}, bf16[512,1280]{1,0:T(8,128)(2,1)}, u32[]{:S(2)}, u32[]{:S(2)}) %collective-permute-start.4) | collective-permute-done | bytes 1310752 | tf_op jit(solution)/shard_map/ppermute | solution.py:153
  60.8 2.4 collective-permute-done.6
  72.3 2.6 constant_dynamic-update-slice_fusion
  74.9 14.0 %collective-permute-done.9 = bf16[512,1280]{1,0:T(8,128)(2,1)} collective-permute-done((bf16[512,1280]{1,0:T(8,128)(2,1)S(1)}, bf16[512,1280]{1,0:T(8,128)(2,1)}, u32[]{:S(2)}, u32[]{:S(2)}) %collective-permute-start.9) | collective-permute-done | bytes 1310752 | tf_op jit(solution)/shard_map/ppermute | solution.py:153
  90.2 4.0 %collective-permute-start.12 = (bf16[2,3,128,1024]{3,2,1,0:T(8,128)(2,1)S(1)}, bf16[2,3,128,1024]{3,2,1,0:T(8,128)(2,1)S(1)}, u32[]{:S(2)}, u32[]{:S(2)}) collective-permute-start(bf16[2,3,128,1024]{3,2,1,0:T(8,128)(2,1)S(1)} %pad_maximum_fusion.7), channel_id=1, source_target_pairs={{0,1},{1,0},{2,3},{3,2},{4,5},{5,4},{6,7},{7,6},{8,9},{9,8},{10,11... | collective-permute-start | bytes 4718600 | tf_op jit(solution)/shard_map/ppermute | solution.py:153
  94.9 4.2 %fusion.4 = f32[1024,1024]{1,0:T(8,128)S(1)} fusion(bf16[1024,1280]{1,0:T(8,128)(2,1)S(1)} %get-tuple-element.81, bf16[512,1280]{1,0:T(8,128)(2,1)} %collective-permute-done.9, bf16[512,1280]{1,0:T(8,128)(2,1)S(1)} %copy-done.1), kind=kOutput, calls=%fused_computation.10 | convolution fusion | flops 2689597440 | bytes 9437184 | tf_op jit(solution)/shard_map/dot_general | solution.py:202
  99.1 5.1 %fusion.10 = f32[1024,1024]{1,0:T(8,128)S(1)} fusion(f32[1024,1024]{1,0:T(8,128)S(1)} %fusion.4, bf16[1024,1280]{1,0:T(8,128)(2,1)} %get-tuple-element.79, bf16[512,1280]{1,0:T(8,128)(2,1)} %collective-permute-done.4, bf16[512,1280]{1,0:T(8,128)(2,1)S(1)} %copy-done.5), kind=kOutput, calls=%fused_computation.32 | convolution fusion | flops 2690646016 | bytes 13631488 | tf_op jit(solution)/shard_map/dot_general | solution.py:202
  105.0 11.9 %collective-permute-done.7 = bf16[512,1280]{1,0:T(8,128)(2,1)S(1)} collective-permute-done((bf16[512,1280]{1,0:T(8,128)(2,1)}, bf16[512,1280]{1,0:T(8,128)(2,1)S(1)}, u32[]{:S(2)}, u32[]{:S(2)}) %collective-permute-start.7) | collective-permute-done | bytes 1310752 | tf_op jit(solution)/shard_map/ppermute | solution.py:153
  123.4 3.6 %fusion.15 = f32[512,1280]{1,0:T(8,128)S(1)} fusion(bf16[512,1280]{1,0:T(8,128)(2,1)S(1)} %add.190, bf16[512,1280]{1,0:T(8,128)(2,1)} %collective-permute-done.4, bf16[512,1280]{1,0:T(8,128)(2,1)S(1)} %copy-done.5, bf16[2048,512]{1,0:T(8,128)(2,1)S(1)} %get-tuple-element.92), kind=kOutput, calls=%fused_computation.35 | convolution fusion | flops 2025062400 | bytes 8126464 | tf_op jit(solution)/shard_map/dot_general | solution.py:198
  127.0 3.6 %fusion.16 = f32[512,1280]{1,0:T(8,128)S(1)} fusion(bf16[512,1280]{1,0:T(8,128)(2,1)S(1)} %add.190, bf16[512,1280]{1,0:T(8,128)(2,1)} %collective-permute-done.4, bf16[512,1280]{1,0:T(8,128)(2,1)S(1)} %copy-done.5, bf16[2048,512]{1,0:T(8,128)(2,1)S(1)} %get-tuple-element.95), kind=kOutput, calls=%fused_computation.36 | convolution fusion | flops 2025062400 | bytes 8126464 | tf_op jit(solution)/shard_map/dot_general | solution.py:198
  131.1 24.6 %collective-permute-done.15 = bf16[512,1280]{1,0:T(8,128)(2,1)S(1)} collective-permute-done((bf16[512,1280]{1,0:T(8,128)(2,1)S(1)}, bf16[512,1280]{1,0:T(8,128)(2,1)S(1)}, u32[]{:S(2)}, u32[]{:S(2)}) %collective-permute-start.15) | collective-permute-done | bytes 1310752 | tf_op jit(solution)/shard_map/ppermute | solution.py:153
  165.2 18.7 %collective-permute-done.13 = bf16[512,1280]{1,0:T(8,128)(2,1)S(1)} collective-permute-done((bf16[512,1280]{1,0:T(8,128)(2,1)S(1)}, bf16[512,1280]{1,0:T(8,128)(2,1)S(1)}, u32[]{:S(2)}, u32[]{:S(2)}) %collective-permute-start.13) | collective-permute-done | bytes 1310752 | tf_op jit(solution)/shard_map/ppermute | solution.py:153
  185.7 3.3 %fusion.57 = (bf16[512,1024]{1,0:T(8,128)(2,1)S(1)}, f32[512,1024]{1,0:T(8,128)S(1)}) fusion(f32[512,1024]{1,0:T(8,128)S(1)} %fusion.58, bf16[512,1280]{1,0:T(8,128)(2,1)S(1)} %add.190, bf16[1024,1280]{1,0:T(8,128)(2,1)} %get-tuple-element.79), kind=kOutput, calls=%fused_computation.115 | convolution fusion | flops 1343225856 | bytes 9175040 | tf_op jit(solution)/shard_map/dot_general | solution.py:202
  189.0 3.0 %collective-permute-start.18 = (bf16[512,1024]{1,0:T(8,128)(2,1)S(1)}, bf16[512,1024]{1,0:T(8,128)(2,1)S(1)}, u32[]{:S(2)}, u32[]{:S(2)}) collective-permute-start(bf16[512,1024]{1,0:T(8,128)(2,1)S(1)} %get-tuple-element.151), channel_id=1, source_target_pairs={{1,0},{3,2},{5,4},{7,6},{9,8},{11,10},{13,12},{15,14},{17,16},{19,... | collective-permute-start | bytes 3145736 | tf_op jit(solution)/shard_map/ppermute | solution.py:153
  192.0 3.6 %fusion.13 = f32[512,1280]{1,0:T(8,128)S(1)} fusion(bf16[512,1280]{1,0:T(8,128)(2,1)S(1)} %add.196, bf16[512,1280]{1,0:T(8,128)(2,1)} %collective-permute-done.9, bf16[512,1280]{1,0:T(8,128)(2,1)S(1)} %copy-done.1, bf16[2048,512]{1,0:T(8,128)(2,1)S(1)} %get-tuple-element.92), kind=kOutput, calls=%fused_computation.33 | convolution fusion | flops 2025062400 | bytes 8126464 | tf_op jit(solution)/shard_map/dot_general | solution.py:198
  195.8 3.6 %fusion.14 = f32[512,1280]{1,0:T(8,128)S(1)} fusion(bf16[512,1280]{1,0:T(8,128)(2,1)S(1)} %add.196, bf16[512,1280]{1,0:T(8,128)(2,1)} %collective-permute-done.9, bf16[512,1280]{1,0:T(8,128)(2,1)S(1)} %copy-done.1, bf16[2048,512]{1,0:T(8,128)(2,1)S(1)} %get-tuple-element.95), kind=kOutput, calls=%fused_computation.34 | convolution fusion | flops 2025062400 | bytes 8126464 | tf_op jit(solution)/shard_map/dot_general | solution.py:198
  206.8 3.3 %convolution_add_fusion.1 = f32[512,1024]{1,0:T(8,128)S(1)} fusion(f32[512,1024]{1,0:T(8,128)S(1)} %fusion.23, bf16[512,1280]{1,0:T(8,128)(2,1)S(1)} %add.194, bf16[1024,1280]{1,0:T(8,128)(2,1)} %get-tuple-element.79), kind=kOutput, calls=%fused_computation.48 | convolution fusion | flops 1342701568 | bytes 8126464 | tf_op jit(solution)/shard_map/dot_general | solution.py:202
  211.9 4.5 %collective-permute-done.21 = bf16[512,512]{1,0:T(8,128)(2,1)S(1)} collective-permute-done((bf16[512,512]{1,0:T(8,128)(2,1)S(1)}, bf16[512,512]{1,0:T(8,128)(2,1)S(1)}, u32[]{:S(2)}, u32[]{:S(2)}) %collective-permute-start.21) | collective-permute-done | bytes 524320 | tf_op jit(solution)/shard_map/ppermute | solution.py:153
  228.3 2.7 collective-permute-start.27
  231.3 6.5 %collective-permute-done.28 = bf16[512,768]{1,0:T(8,128)(2,1)S(1)} collective-permute-done((bf16[512,768]{1,0:T(8,128)(2,1)S(1)}, bf16[512,768]{1,0:T(8,128)(2,1)S(1)}, u32[]{:S(2)}, u32[]{:S(2)}) %collective-permute-start.28) | collective-permute-done | bytes 786464 | tf_op jit(solution)/shard_map/ppermute | solution.py:153
  237.7 4.7 %collective-permute-done.27 = bf16[256,1024]{1,0:T(8,128)(2,1)} collective-permute-done((bf16[256,1024]{1,0:T(8,128)(2,1)S(1)}, bf16[256,1024]{1,0:T(8,128)(2,1)}, u32[]{:S(2)}, u32[]{:S(2)}) %collective-permute-start.27) | collective-permute-done | bytes 524320 | tf_op jit(solution)/shard_map/ppermute | solution.py:153
  254.2 2.8 collective-permute-start.37
  258.4 4.7 %collective-permute-start.38 = (f32[2,128]{0,1:T(8,128)S(1)}, f32[2,128]{0,1:T(8,128)S(1)}, u32[]{:S(2)}, u32[]{:S(2)}) collective-permute-start(f32[2,128]{0,1:T(8,128)S(1)} %broadcast_in_dim.20), channel_id=1, source_target_pairs={{0,1},{1,0},{2,3},{3,2},{4,5},{5,4},{6,7},{7,6},{8,9},{9,8},{10,11... | collective-permute-start | bytes 3080 | tf_op jit(solution)/shard_map/ppermute | solution.py:153
  264.7 3.9 %collective-permute-start.31 = (bf16[256,1024]{1,0:T(8,128)(2,1)S(1)}, bf16[256,1024]{1,0:T(8,128)(2,1)S(1)}, u32[]{:S(2)}, u32[]{:S(2)}) collective-permute-start(bf16[256,1024]{1,0:T(8,128)(2,1)S(1)} %add_convert_fusion.2), channel_id=1, source_target_pairs={{1,24},{5,28},{9,17},{13,21},{17,10},{21,14},{25,3},{29,7}} | collective-permute-start | bytes 1572872 | tf_op jit(solution)/shard_map/ppermute | solution.py:153
  271.2 6.1 %collective-permute-done.39 = f32[2,128]{0,1:T(8,128)S(1)} collective-permute-done((f32[2,128]{0,1:T(8,128)S(1)}, f32[2,128]{0,1:T(8,128)S(1)}, u32[]{:S(2)}, u32[]{:S(2)}) %collective-permute-start.39) | collective-permute-done | bytes 1056 | tf_op jit(solution)/shard_map/ppermute | solution.py:153
  277.4 3.5 %multiply_multiply_fusion.1 = f32[512,1280]{1,0:T(8,128)} fusion(f32[512,1280]{1,0:T(8,128)} %copy-done, f32[1280]{0:T(1024)S(1)} %get-tuple-element.132, f32[512]{0:T(512)S(1)} %bitcast.52), kind=kLoop, calls=%fused_computation.16 | loop fusion | flops 1310720 | bytes 5250048 | tf_op jit(solution)/shard_map/mul | solution.py:392
  (173 shorter events, 85.8 us)
Async XLA Ops:
  0.6 30.8 %collective-permute-start.3 = (bf16[512,1280]{1,0:T(8,128)(2,1)}, bf16[512,1280]{1,0:T(8,128)(2,1)S(1)}, u32[]{:S(2)}, u32[]{:S(2)}) collective-permute-start(bf16[512,1280]{1,0:T(8,128)(2,1)} %param.16), channel_id=1, source_target_pairs={{0,4},{1,5},{2,6},{3,7},{4,0},{5,1},{6,2},{7,3},{8,12},{9,13},{10,... | collective-permute-start | bytes 3932168 | tf_op jit(solution)/shard_map/ppermute | solution.py:153
  5.2 16.0 %collective-permute-start = (bf16[128,1024]{1,0:T(8,128)(2,1)}, bf16[128,1024]{1,0:T(8,128)(2,1)S(1)}, u32[]{:S(2)}, u32[]{:S(2)}) collective-permute-start(bf16[128,1024]{1,0:T(8,128)(2,1)} %get-tuple-element.144), channel_id=1, source_target_pairs={{0,8},{1,9},{2,10},{3,11},{4,12},{5,13},{6,14},{7,15},{8,0},{9,1},... | collective-permute-start | bytes 786440 | tf_op jit(solution)/shard_map/ppermute | solution.py:153
  6.5 14.7 %collective-permute-start.1 = (bf16[128,1024]{1,0:T(8,128)(2,1)}, bf16[128,1024]{1,0:T(8,128)(2,1)S(1)}, u32[]{:S(2)}, u32[]{:S(2)}) collective-permute-start(bf16[128,1024]{1,0:T(8,128)(2,1)} %get-tuple-element.143), channel_id=1, source_target_pairs={{0,16},{1,17},{2,18},{3,19},{4,20},{5,21},{6,22},{7,23},{8,24},{9,... | collective-permute-start | bytes 786440 | tf_op jit(solution)/shard_map/ppermute | solution.py:153
  8.8 16.8 %collective-permute-start.2 = (bf16[128,1024]{1,0:T(8,128)(2,1)}, bf16[128,1024]{1,0:T(8,128)(2,1)S(1)}, u32[]{:S(2)}, u32[]{:S(2)}) collective-permute-start(bf16[128,1024]{1,0:T(8,128)(2,1)} %get-tuple-element.142), channel_id=1, source_target_pairs={{0,24},{1,25},{2,26},{3,27},{4,28},{5,29},{6,30},{7,31},{8,16},{9,... | collective-permute-start | bytes 786440 | tf_op jit(solution)/shard_map/ppermute | solution.py:153
  31.5 29.4 %collective-permute-start.4 = (bf16[512,1280]{1,0:T(8,128)(2,1)}, bf16[512,1280]{1,0:T(8,128)(2,1)}, u32[]{:S(2)}, u32[]{:S(2)}) collective-permute-start(bf16[512,1280]{1,0:T(8,128)(2,1)} %shard_map.137), channel_id=1, source_target_pairs={{0,8},{1,9},{2,10},{3,11},{4,12},{5,13},{6,14},{7,15},{8,0},{9,1},... | collective-permute-start | bytes 3932168 | tf_op jit(solution)/shard_map/ppermute | solution.py:153
  32.7 28.1 %collective-permute-start.5 = (bf16[512,1280]{1,0:T(8,128)(2,1)}, bf16[512,1280]{1,0:T(8,128)(2,1)}, u32[]{:S(2)}, u32[]{:S(2)}) collective-permute-start(bf16[512,1280]{1,0:T(8,128)(2,1)} %shard_map.137), channel_id=1, source_target_pairs={{8,16},{9,17},{10,18},{11,19},{12,20},{13,21},{14,22},{15,23},{16,... | collective-permute-start | bytes 3932168 | tf_op jit(solution)/shard_map/ppermute | solution.py:153
  34.4 28.8 %collective-permute-start.6 = (bf16[512,1280]{1,0:T(8,128)(2,1)}, bf16[512,1280]{1,0:T(8,128)(2,1)}, u32[]{:S(2)}, u32[]{:S(2)}) collective-permute-start(bf16[512,1280]{1,0:T(8,128)(2,1)} %param.17), channel_id=1, source_target_pairs={{0,4},{1,5},{2,6},{3,7},{4,0},{5,1},{6,2},{7,3},{8,12},{9,13},{10,... | collective-permute-start | bytes 3932168 | tf_op jit(solution)/shard_map/ppermute | solution.py:153
  35.6 39.3 %collective-permute-start.10 = (bf16[512,1280]{1,0:T(8,128)(2,1)S(1)}, bf16[512,1280]{1,0:T(8,128)(2,1)S(1)}, u32[]{:S(2)}, u32[]{:S(2)}) collective-permute-start(bf16[512,1280]{1,0:T(8,128)(2,1)S(1)} %copy-done.1), channel_id=1, source_target_pairs={{8,16},{9,17},{10,18},{11,19},{12,20},{13,21},{14,22},{15,23},{16,... | collective-permute-start | bytes 3932168 | tf_op jit(solution)/shard_map/ppermute | solution.py:153
  36.4 52.5 %collective-permute-start.9 = (bf16[512,1280]{1,0:T(8,128)(2,1)S(1)}, bf16[512,1280]{1,0:T(8,128)(2,1)}, u32[]{:S(2)}, u32[]{:S(2)}) collective-permute-start(bf16[512,1280]{1,0:T(8,128)(2,1)S(1)} %copy-done.1), channel_id=1, source_target_pairs={{0,8},{1,9},{2,10},{3,11},{4,12},{5,13},{6,14},{7,15},{8,0},{9,1},... | collective-permute-start | bytes 3932168 | tf_op jit(solution)/shard_map/ppermute | solution.py:153
  63.2 25.7 %collective-permute-start.11 = (bf16[3,128,1024]{2,1,0:T(8,128)(2,1)S(1)}, bf16[3,128,1024]{2,1,0:T(8,128)(2,1)}, u32[]{:S(2)}, u32[]{:S(2)}) collective-permute-start(bf16[3,128,1024]{2,1,0:T(8,128)(2,1)S(1)} %pad_maximum_fusion.9), channel_id=1, source_target_pairs={{0,2},{1,3},{2,0},{3,1},{4,6},{5,7},{6,4},{7,5},{8,10},{9,11},{10,... | collective-permute-start | bytes 2359304 | tf_op jit(solution)/shard_map/ppermute | solution.py:153
  70.3 46.6 %collective-permute-start.7 = (bf16[512,1280]{1,0:T(8,128)(2,1)}, bf16[512,1280]{1,0:T(8,128)(2,1)S(1)}, u32[]{:S(2)}, u32[]{:S(2)}) collective-permute-start(bf16[512,1280]{1,0:T(8,128)(2,1)} %collective-permute-done.5), channel_id=1, source_target_pairs={{8,0},{9,1},{10,2},{11,3},{12,4},{13,5},{14,6},{15,7},{16,24},{17,... | collective-permute-start | bytes 3932168 | tf_op jit(solution)/shard_map/ppermute | solution.py:153
  71.6 45.3 %collective-permute-start.8 = (bf16[512,1280]{1,0:T(8,128)(2,1)}, bf16[512,1280]{1,0:T(8,128)(2,1)S(1)}, u32[]{:S(2)}, u32[]{:S(2)}) collective-permute-start(bf16[512,1280]{1,0:T(8,128)(2,1)} %collective-permute-done.4), channel_id=1, source_target_pairs={{8,16},{9,17},{10,18},{11,19},{12,20},{13,21},{14,22},{15,23},{16,... | collective-permute-start | bytes 3932168 | tf_op jit(solution)/shard_map/ppermute | solution.py:153
  90.2 26.7 %collective-permute-start.12 = (bf16[2,3,128,1024]{3,2,1,0:T(8,128)(2,1)S(1)}, bf16[2,3,128,1024]{3,2,1,0:T(8,128)(2,1)S(1)}, u32[]{:S(2)}, u32[]{:S(2)}) collective-permute-start(bf16[2,3,128,1024]{3,2,1,0:T(8,128)(2,1)S(1)} %pad_maximum_fusion.7), channel_id=1, source_target_pairs={{0,1},{1,0},{2,3},{3,2},{4,5},{5,4},{6,7},{7,6},{8,9},{9,8},{10,11... | collective-permute-start | bytes 4718600 | tf_op jit(solution)/shard_map/ppermute | solution.py:153
  94.2 37.0 %collective-permute-start.14 = (bf16[512,1280]{1,0:T(8,128)(2,1)}, bf16[512,1280]{1,0:T(8,128)(2,1)S(1)}, u32[]{:S(2)}, u32[]{:S(2)}) collective-permute-start(bf16[512,1280]{1,0:T(8,128)(2,1)} %collective-permute-done.9), channel_id=1, source_target_pairs={{8,16},{9,17},{10,18},{11,19},{12,20},{13,21},{14,22},{15,23},{16,... | collective-permute-start | bytes 3932168 | tf_op jit(solution)/shard_map/ppermute | solution.py:153
  116.9 13.7 %collective-permute-start.16 = (bf16[512,1024]{1,0:T(8,128)(2,1)S(1)}, bf16[512,1024]{1,0:T(8,128)(2,1)S(1)}, u32[]{:S(2)}, u32[]{:S(2)}) collective-permute-start(bf16[512,1024]{1,0:T(8,128)(2,1)S(1)} %select_convert_fusion), channel_id=1, source_target_pairs={{0,1},{1,0},{2,3},{3,2},{4,5},{5,4},{6,7},{7,6},{8,9},{9,8},{10,11... | collective-permute-start | bytes 3145736 | tf_op jit(solution)/shard_map/ppermute | solution.py:153
  119.0 36.7 %collective-permute-start.15 = (bf16[512,1280]{1,0:T(8,128)(2,1)S(1)}, bf16[512,1280]{1,0:T(8,128)(2,1)S(1)}, u32[]{:S(2)}, u32[]{:S(2)}) collective-permute-start(bf16[512,1280]{1,0:T(8,128)(2,1)S(1)} %collective-permute-done.8), channel_id=1, source_target_pairs={{8,0},{9,1},{10,2},{11,3},{12,4},{13,5},{14,6},{15,7},{16,24},{17,... | collective-permute-start | bytes 3932168 | tf_op jit(solution)/shard_map/ppermute | solution.py:153
  120.7 63.2 %collective-permute-start.13 = (bf16[512,1280]{1,0:T(8,128)(2,1)S(1)}, bf16[512,1280]{1,0:T(8,128)(2,1)S(1)}, u32[]{:S(2)}, u32[]{:S(2)}) collective-permute-start(bf16[512,1280]{1,0:T(8,128)(2,1)S(1)} %collective-permute-done.10), channel_id=1, source_target_pairs={{8,0},{9,1},{10,2},{11,3},{12,4},{13,5},{14,6},{15,7},{16,24},{17,... | collective-permute-start | bytes 3932168 | tf_op jit(solution)/shard_map/ppermute | solution.py:153
  157.4 26.4 %collective-permute-start.17 = (bf16[256,1024]{1,0:T(8,128)(2,1)S(1)}, bf16[256,1024]{1,0:T(8,128)(2,1)S(1)}, u32[]{:S(2)}, u32[]{:S(2)}) collective-permute-start(bf16[256,1024]{1,0:T(8,128)(2,1)S(1)} %dynamic-slice_convert_fusion.2), channel_id=1, source_target_pairs={{0,2},{1,3},{2,0},{3,1},{4,6},{5,7},{6,4},{7,5},{8,10},{9,11},{10,... | collective-permute-start | bytes 1572872 | tf_op jit(solution)/shard_map/ppermute | solution.py:153
  160.1 39.3 %collective-permute-start.20 = (bf16[512,1280]{1,0:T(8,128)(2,1)S(1)}, bf16[512,1280]{1,0:T(8,128)(2,1)S(1)}, u32[]{:S(2)}, u32[]{:S(2)}) collective-permute-start(bf16[512,1280]{1,0:T(8,128)(2,1)S(1)} %add_convert_fusion), channel_id=1, source_target_pairs={{0,4},{1,5},{2,6},{3,7},{4,0},{5,1},{6,2},{7,3},{8,12},{9,13},{10,... | collective-permute-start | bytes 3932168 | tf_op jit(solution)/shard_map/ppermute | solution.py:153
  161.4 38.0 %collective-permute-start.19 = (bf16[512,512]{1,0:T(8,128)(2,1)S(1)}, bf16[512,512]{1,0:T(8,128)(2,1)S(1)}, u32[]{:S(2)}, u32[]{:S(2)}) collective-permute-start(bf16[512,512]{1,0:T(8,128)(2,1)S(1)} %slice.129), channel_id=1, source_target_pairs={{8,0},{9,1},{10,2},{11,3},{12,4},{13,5},{14,6},{15,7},{16,24},{17,... | collective-permute-start | bytes 1572872 | tf_op jit(solution)/shard_map/ppermute | solution.py:153
  162.7 49.3 %collective-permute-start.22 = (bf16[512,768]{1,0:T(8,128)(2,1)S(1)}, bf16[512,768]{1,0:T(8,128)(2,1)S(1)}, u32[]{:S(2)}, u32[]{:S(2)}) collective-permute-start(bf16[512,768]{1,0:T(8,128)(2,1)S(1)} %slice.134), channel_id=1, source_target_pairs={{8,0},{9,1},{10,2},{11,3},{12,4},{13,5},{14,6},{15,7},{16,24},{17,... | collective-permute-start | bytes 2359304 | tf_op jit(solution)/shard_map/ppermute | solution.py:153
  189.0 10.4 %collective-permute-start.18 = (bf16[512,1024]{1,0:T(8,128)(2,1)S(1)}, bf16[512,1024]{1,0:T(8,128)(2,1)S(1)}, u32[]{:S(2)}, u32[]{:S(2)}) collective-permute-start(bf16[512,1024]{1,0:T(8,128)(2,1)S(1)} %get-tuple-element.151), channel_id=1, source_target_pairs={{1,0},{3,2},{5,4},{7,6},{9,8},{11,10},{13,12},{15,14},{17,16},{19,... | collective-permute-start | bytes 3145736 | tf_op jit(solution)/shard_map/ppermute | solution.py:153
  199.4 18.3 %collective-permute-start.23 = (bf16[256,1024]{1,0:T(8,128)(2,1)S(1)}, bf16[256,1024]{1,0:T(8,128)(2,1)S(1)}, u32[]{:S(2)}, u32[]{:S(2)}) collective-permute-start(bf16[256,1024]{1,0:T(8,128)(2,1)S(1)} %add_convert_fusion.5), channel_id=1, source_target_pairs={{0,0},{1,8},{4,4},{5,12},{8,9},{9,1},{12,13},{13,5},{16,18},{17,26... | collective-permute-start | bytes 1572872 | tf_op jit(solution)/shard_map/ppermute | solution.py:153
  201.4 17.2 %collective-permute-start.24 = (bf16[256,1024]{1,0:T(8,128)(2,1)S(1)}, bf16[256,1024]{1,0:T(8,128)(2,1)S(1)}, u32[]{:S(2)}, u32[]{:S(2)}) collective-permute-start(bf16[256,1024]{1,0:T(8,128)(2,1)S(1)} %add_convert_fusion.5), channel_id=1, source_target_pairs={{2,0},{3,8},{6,4},{7,12},{10,9},{11,1},{14,13},{15,5},{18,18},{19,... | collective-permute-start | bytes 1572872 | tf_op jit(solution)/shard_map/ppermute | solution.py:153
  203.0 8.9 %collective-permute-start.25 = (bf16[256,1024]{1,0:T(8,128)(2,1)S(1)}, bf16[256,1024]{1,0:T(8,128)(2,1)S(1)}, u32[]{:S(2)}, u32[]{:S(2)}) collective-permute-start(bf16[256,1024]{1,0:T(8,128)(2,1)S(1)} %dynamic-slice_convert_fusion.1), channel_id=1, source_target_pairs={{0,2},{2,0},{4,6},{6,4},{8,10},{10,8},{12,14},{14,12},{16,18},{18,... | collective-permute-start | bytes 1572872 | tf_op jit(solution)/shard_map/ppermute | solution.py:153
  205.0 11.5 %collective-permute-start.21 = (bf16[512,512]{1,0:T(8,128)(2,1)S(1)}, bf16[512,512]{1,0:T(8,128)(2,1)S(1)}, u32[]{:S(2)}, u32[]{:S(2)}) collective-permute-start(bf16[512,512]{1,0:T(8,128)(2,1)S(1)} %add_convert_fusion.4), channel_id=1, source_target_pairs={{0,4},{1,5},{2,6},{3,7},{4,0},{5,1},{6,2},{7,3},{8,12},{9,13},{10,... | collective-permute-start | bytes 1572872 | tf_op jit(solution)/shard_map/ppermute | solution.py:153
  222.1 9.1 %collective-permute-start.29 = (bf16[256,1024]{1,0:T(8,128)(2,1)S(1)}, bf16[256,1024]{1,0:T(8,128)(2,1)S(1)}, u32[]{:S(2)}, u32[]{:S(2)}) collective-permute-start(bf16[256,1024]{1,0:T(8,128)(2,1)S(1)} %add_convert_fusion.3), channel_id=1, source_target_pairs={{0,16},{4,20},{8,25},{12,29},{16,2},{20,6},{24,11},{28,15}} | collective-permute-start | bytes 1572872 | tf_op jit(solution)/shard_map/ppermute | solution.py:153
  224.2 13.6 %collective-permute-start.28 = (bf16[512,768]{1,0:T(8,128)(2,1)S(1)}, bf16[512,768]{1,0:T(8,128)(2,1)S(1)}, u32[]{:S(2)}, u32[]{:S(2)}) collective-permute-start(bf16[512,768]{1,0:T(8,128)(2,1)S(1)} %add_convert_fusion.1), channel_id=1, source_target_pairs={{0,4},{1,5},{2,6},{3,7},{4,0},{5,1},{6,2},{7,3},{8,12},{9,13},{10,... | collective-permute-start | bytes 2359304 | tf_op jit(solution)/shard_map/ppermute | solution.py:153
  228.3 14.1 %collective-permute-start.27 = (bf16[256,1024]{1,0:T(8,128)(2,1)S(1)}, bf16[256,1024]{1,0:T(8,128)(2,1)}, u32[]{:S(2)}, u32[]{:S(2)}) collective-permute-start(bf16[256,1024]{1,0:T(8,128)(2,1)S(1)} %dynamic-slice_convert_fusion), channel_id=1, source_target_pairs={{1,3},{3,1},{5,7},{7,5},{9,11},{11,9},{13,15},{15,13},{17,19},{19,... | collective-permute-start | bytes 1572872 | tf_op jit(solution)/shard_map/ppermute | solution.py:153
  258.4 10.9 %collective-permute-start.38 = (f32[2,128]{0,1:T(8,128)S(1)}, f32[2,128]{0,1:T(8,128)S(1)}, u32[]{:S(2)}, u32[]{:S(2)}) collective-permute-start(f32[2,128]{0,1:T(8,128)S(1)} %broadcast_in_dim.20), channel_id=1, source_target_pairs={{0,1},{1,0},{2,3},{3,2},{4,5},{5,4},{6,7},{7,6},{8,9},{9,8},{10,11... | collective-permute-start | bytes 3080 | tf_op jit(solution)/shard_map/ppermute | solution.py:153
  264.7 18.0 %collective-permute-start.31 = (bf16[256,1024]{1,0:T(8,128)(2,1)S(1)}, bf16[256,1024]{1,0:T(8,128)(2,1)S(1)}, u32[]{:S(2)}, u32[]{:S(2)}) collective-permute-start(bf16[256,1024]{1,0:T(8,128)(2,1)S(1)} %add_convert_fusion.2), channel_id=1, source_target_pairs={{1,24},{5,28},{9,17},{13,21},{17,10},{21,14},{25,3},{29,7}} | collective-permute-start | bytes 1572872 | tf_op jit(solution)/shard_map/ppermute | solution.py:153
  268.6 14.2 %collective-permute-start.32 = (bf16[256,1024]{1,0:T(8,128)(2,1)S(1)}, bf16[256,1024]{1,0:T(8,128)(2,1)S(1)}, u32[]{:S(2)}, u32[]{:S(2)}) collective-permute-start(bf16[256,1024]{1,0:T(8,128)(2,1)S(1)} %add_convert_fusion.2), channel_id=1, source_target_pairs={{3,24},{7,28},{11,17},{15,21},{19,10},{23,14},{27,3},{31,7}} | collective-permute-start | bytes 1572872 | tf_op jit(solution)/shard_map/ppermute | solution.py:153
  (27 other events, 271.4 us)

commit v2 on v1

--- a/solution.py
+++ b/solution.py
@@ -290,11 +290,13 @@
     early = dot_last(jnp.concatenate([g, g_near], axis=0), gate_rows)
     early = early + dot_last(jnp.concatenate([u, u_near], axis=0), up_rows)
     early_keep, early_away = over_core(early[:tokens], early[tokens:])
-    g_far, g_near_over, pieces, pieces_c, early_keep, early_away, u_over = tie(
-        g_far, g_near_over, pieces, pieces_c, early_keep, early_away, u_over
-    )
-
     early_recv = send(early_away, FLIP_C)
+    g_far, g_near_over, pieces, pieces_c, early_keep, early_recv, u_over = tie(
+        g_far, g_near_over, pieces, pieces_c, early_keep, early_recv, u_over
+    )
+
+    early_keep, early_away = over_y(early_keep + early_recv.astype(f32))
+    early_recv = send(early_away, FLIP_Y)
     g_farthest = send(g_near_over, OUTWARD)
     u_far = send(u_over, OUTWARD)
     far = jnp.zeros((3, model_size, piece_rows, plane), bf16)
@@ -316,36 +318,35 @@
 
     g_third = g_near_over + g_far
     g_products = near_products(jnp.concatenate([g, g_near, g_third], axis=0))
-    early_keep, early_away = over_y(early_keep + early_recv.astype(f32))
-    u_near_over, g_farthest, g_products, inputs_keep, inputs_away, early_keep, early_away = tie(
-        u_near_over, g_farthest, g_products, inputs_keep, inputs_away, early_keep, early_away
-    )
-
-    u_farthest = [send(u_near_over[:, span], OUTWARD) for span in up_spans]
+    early_sum = (early_keep + early_recv.astype(f32)).astype(bf16)
+    u_near_over, g_farthest, g_products, inputs_keep, inputs_away, early_sum = tie(
+        u_near_over, g_farthest, g_products, inputs_keep, inputs_away, early_sum
+    )
+
+    u_farthest = [send(u_near_over[:, up_spans[0]], OUTWARD)]
     g_last = g_over + g_farthest
     away, g_keep = last_products(g_last, g_products, slice(None))
     g_recv = send(away, FLIP_X)
-    early_recv = send(early_away, FLIP_Y)
-    u_far, early_recv, g_keep, g_last = tie(u_far, early_recv, g_keep, g_last)
-
+    early_home = [send(early_sum, home(0, h)) for h in range(2)]
+    u_far, early_home, g_keep, g_last, u_near_over = tie(u_far, early_home, g_keep, g_last, u_near_over)
+
+    u_farthest.append(send(u_near_over[:, up_spans[1]], OUTWARD))
     u_third = u_near_over + u_far
     u_products = near_products(jnp.concatenate([u, u_near, u_third], axis=0))
     third = dot_last(g_third, gate_rows) + dot_last(u_third, up_rows)
-    early_sum = (early_keep + early_recv.astype(f32)).astype(bf16)
     third_recv = send(third.astype(bf16), to_core(0))
-    u_products, third, third_recv, early_sum, u_farthest[0], g_recv = tie(
-        u_products, third, third_recv, early_sum, u_farthest[0], g_recv
+    u_products, third, third_recv, u_farthest[0], g_recv = tie(
+        u_products, third, third_recv, u_farthest[0], g_recv
     )
 
     block = u_over[:, up_spans[0]] + u_farthest[0]
     away, first_keep = last_products(block, u_products, up_spans[0])
     first_recv = send(away, FLIP_X)
     last = dot_last(g_last, gate_rows) + dot_last(block, up_rows[:, up_spans[0]])
-    early_home = [send(early_sum, home(0, h)) for h in range(2)]
     third_keep, third_away = over_y(third + third_recv.astype(f32))
     third_recv = send(third_away, flip_y_of(0))
-    last, first_keep, first_recv, u_farthest[1], early_home, third_keep, third_recv = tie(
-        last, first_keep, first_recv, u_farthest[1], early_home, third_keep, third_recv
+    last, first_keep, first_recv, u_farthest[1], third_keep, third_recv = tie(
+        last, first_keep, first_recv, u_farthest[1], third_keep, third_recv
     )
 
     block = u_over[:, up_spans[1]] + u_farthest[1]

time: 286 us -> 286 us (level)
  waiting for transfers between devices: 133 us -> 123 us
  starting transfers between devices: 67.3 us -> 75.6 us
  matrix products: 37.6 us -> 33.3 us
  other arithmetic: 18.7 us -> 22.5 us
    ppermute x40, waiting for transfers between devices: 133 us -> 123 us  [send(): return lax.ppermute(value, AXES, permutation)]
    ppermute x40, starting transfers between devices: 67.3 us -> 75.6 us  [send(): return lax.ppermute(value, AXES, permutation)]
    dot_general x7, matrix products: 19.2 us -> 14.9 us  [dot_last(): lax.dot_general(a, b, (((1,), (1,)), ((), ())), preferred_element_type=f32)]
    unnamed x38 -> x48, local copies, waits for them, and re-layouts: 1.01 us -> 3.93 us
  transfers between devices with their start and end apart: 40 -> 40, of which waited for: 21 -> 19; matrix products, arithmetic and copies ran while one was open for 24% -> 23% of each run, Pallas kernels for 4% -> 4%
where the time goes in v2:
time: 286 us; the launch traced here: 284 us
  waiting for transfers between devices  123 us (43%)
  starting transfers between devices  75.6 us (26%)
  matrix products  33.3 us (12%)
  other arithmetic  22.5 us (8%)
  local copies, waits for them, and re-layouts  17.3 us (6%)
  Pallas kernels  10.8 us (4%)
    ppermute x40, waiting for transfers between devices, send(): return lax.ppermute(value, AXES, permutation)  123 us
    ppermute x40, starting transfers between devices, send(): return lax.ppermute(value, AXES, permutation)  75.6 us
    dot_general x10, matrix products, dot_first(): lax.dot_general(a, b, (((0,), (0,)), ((), ())), preferred_element_type=f32)  18.4 us
    dot_general x7, matrix products, dot_last(): lax.dot_general(a, b, (((1,), (1,)), ((), ())), preferred_element_type=f32)  14.9 us
    pallas_call x2, Pallas kernels, front(): pl.pallas_call(kernel, grid=(tokens // rows,), in_specs=[pl.BlockSpec((ro...  10.8 us
  transfers between devices with their start and end apart: 40, of which 19 were waited for; matrix products, arithmetic and copies ran while one was open for 23% of the time, Pallas kernels for 4%

profile of v2, /device:TPU:1, one launch (start us, length us, event | category | flops | bytes accessed | tf_op | source)
XLA Modules:
  0.0 284.5 jit_solution(5668699384826759283)
XLA Ops:
  2.7 2.5 fusion.54
  6.5 2.3 collective-permute-start.1
  10.4 4.4 %shard_map.138 = bf16[512,1280]{1,0:T(8,128)(2,1)} custom-call(s32[512,1]{1,0:T(8,128)} %copy.15.ids_ref, f32[1,64]{1,0:T(1,128)} %bitcast.57, bf16[512,1280]{1,0:T(8,128)(2,1)} %cot_ref.3, bf16[512,1280]{1,0:T(8,128)(2,1)} %gate_ref.3), custom_call_target="tpu_custom_call" | custom-call | flops 655360 | bytes 655360 | tf_op jit(solution)/shard_map/pallas_call | solution.py:181
  14.8 6.4 %shard_map.137 = bf16[512,1280]{1,0:T(8,128)(2,1)} custom-call(s32[512,1]{1,0:T(8,128)} %copy.15.ids_ref, f32[1,64]{1,0:T(1,128)} %bitcast.58, bf16[512,1280]{1,0:T(8,128)(2,1)} %cot_ref.3, bf16[512,1280]{1,0:T(8,128)(2,1)} %gate_ref.3, bf16[512,1280]{1,0:T(8,128)(2,1)} %up_ref.1), custom_call_target="tpu_custom_call" | custom-call | flops 655360 | bytes 655360 | tf_op jit(solution)/shard_map/pallas_call | solution.py:181
  21.2 4.4 %collective-permute-done.2 = bf16[128,1024]{1,0:T(8,128)(2,1)S(1)} collective-permute-done((bf16[128,1024]{1,0:T(8,128)(2,1)}, bf16[128,1024]{1,0:T(8,128)(2,1)S(1)}, u32[]{:S(2)}, u32[]{:S(2)}) %collective-permute-start.2) | collective-permute-done | bytes 262176 | tf_op jit(solution)/shard_map/ppermute | solution.py:153
  25.6 5.9 %collective-permute-done.3 = bf16[512,1280]{1,0:T(8,128)(2,1)S(1)} collective-permute-done((bf16[512,1280]{1,0:T(8,128)(2,1)}, bf16[512,1280]{1,0:T(8,128)(2,1)S(1)}, u32[]{:S(2)}, u32[]{:S(2)}) %collective-permute-start.3) | collective-permute-done | bytes 1310752 | tf_op jit(solution)/shard_map/ppermute | solution.py:153
  36.4 4.1 %collective-permute-start.9 = (bf16[512,1280]{1,0:T(8,128)(2,1)S(1)}, bf16[512,1280]{1,0:T(8,128)(2,1)}, u32[]{:S(2)}, u32[]{:S(2)}) collective-permute-start(bf16[512,1280]{1,0:T(8,128)(2,1)S(1)} %copy-done.6), channel_id=1, source_target_pairs={{0,8},{1,9},{2,10},{3,11},{4,12},{5,13},{6,14},{7,15},{8,0},{9,1},... | collective-permute-start | bytes 3932168 | tf_op jit(solution)/shard_map/ppermute | solution.py:153
  40.5 20.3 %collective-permute-done.4 = bf16[512,1280]{1,0:T(8,128)(2,1)} collective-permute-done((bf16[512,1280]{1,0:T(8,128)(2,1)}, bf16[512,1280]{1,0:T(8,128)(2,1)}, u32[]{:S(2)}, u32[]{:S(2)}) %collective-permute-start.4) | collective-permute-done | bytes 1310752 | tf_op jit(solution)/shard_map/ppermute | solution.py:153
  60.8 2.4 collective-permute-done.6
  71.2 17.7 %collective-permute-done.9 = bf16[512,1280]{1,0:T(8,128)(2,1)} collective-permute-done((bf16[512,1280]{1,0:T(8,128)(2,1)S(1)}, bf16[512,1280]{1,0:T(8,128)(2,1)}, u32[]{:S(2)}, u32[]{:S(2)}) %collective-permute-start.9) | collective-permute-done | bytes 1310752 | tf_op jit(solution)/shard_map/ppermute | solution.py:153
  89.1 4.0 %collective-permute-start.12 = (bf16[2,3,128,1024]{3,2,1,0:T(8,128)(2,1)S(1)}, bf16[2,3,128,1024]{3,2,1,0:T(8,128)(2,1)}, u32[]{:S(2)}, u32[]{:S(2)}) collective-permute-start(bf16[2,3,128,1024]{3,2,1,0:T(8,128)(2,1)S(1)} %pad_maximum_fusion.7), channel_id=1, source_target_pairs={{0,1},{1,0},{2,3},{3,2},{4,5},{5,4},{6,7},{7,6},{8,9},{9,8},{10,11... | collective-permute-start | bytes 4718600 | tf_op jit(solution)/shard_map/ppermute | solution.py:153
  93.0 4.2 %fusion.4 = f32[1024,1024]{1,0:T(8,128)S(1)} fusion(bf16[1024,1280]{1,0:T(8,128)(2,1)S(1)} %get-tuple-element.79, bf16[512,1280]{1,0:T(8,128)(2,1)} %collective-permute-done.9, bf16[512,1280]{1,0:T(8,128)(2,1)S(1)} %copy-done.7), kind=kOutput, calls=%fused_computation.10 | convolution fusion | flops 2689597440 | bytes 9437184 | tf_op jit(solution)/shard_map/dot_general | solution.py:202
  97.3 4.3 %fusion.10 = f32[1024,1024]{1,0:T(8,128)S(1)} fusion(f32[1024,1024]{1,0:T(8,128)S(1)} %fusion.4, bf16[1024,1280]{1,0:T(8,128)(2,1)S(1)} %get-tuple-element.77, bf16[512,1280]{1,0:T(8,128)(2,1)} %collective-permute-done.4, bf16[512,1280]{1,0:T(8,128)(2,1)S(1)} %copy-done.10), kind=kOutput, calls=%fused_computation.32 | convolution fusion | flops 2690646016 | bytes 13631488 | tf_op jit(solution)/shard_map/dot_general | solution.py:202
  106.8 2.6 slice_select_fusion
  109.4 7.6 %collective-permute-done.7 = bf16[512,1280]{1,0:T(8,128)(2,1)} collective-permute-done((bf16[512,1280]{1,0:T(8,128)(2,1)}, bf16[512,1280]{1,0:T(8,128)(2,1)}, u32[]{:S(2)}, u32[]{:S(2)}) %collective-permute-start.7) | collective-permute-done | bytes 1310752 | tf_op jit(solution)/shard_map/ppermute | solution.py:153
  128.7 3.6 %fusion.15 = f32[512,1280]{1,0:T(8,128)S(1)} fusion(bf16[512,1280]{1,0:T(8,128)(2,1)S(1)} %add.190, bf16[512,1280]{1,0:T(8,128)(2,1)} %collective-permute-done.4, bf16[512,1280]{1,0:T(8,128)(2,1)S(1)} %copy-done.11, bf16[2048,512]{1,0:T(8,128)(2,1)S(1)} %get-tuple-element.90), kind=kOutput, calls=%fused_computation.35 | convolution fusion | flops 2025062400 | bytes 8126464 | tf_op jit(solution)/shard_map/dot_general | solution.py:198
  132.3 3.6 %fusion.16 = f32[512,1280]{1,0:T(8,128)S(1)} fusion(bf16[512,1280]{1,0:T(8,128)(2,1)S(1)} %add.190, bf16[512,1280]{1,0:T(8,128)(2,1)} %collective-permute-done.4, bf16[512,1280]{1,0:T(8,128)(2,1)S(1)} %copy-done.11, bf16[2048,512]{1,0:T(8,128)(2,1)S(1)} %get-tuple-element.95), kind=kOutput, calls=%fused_computation.36 | convolution fusion | flops 2025062400 | bytes 8126464 | tf_op jit(solution)/shard_map/dot_general | solution.py:198
  136.1 13.6 %collective-permute-done.16 = bf16[512,1280]{1,0:T(8,128)(2,1)S(1)} collective-permute-done((bf16[512,1280]{1,0:T(8,128)(2,1)}, bf16[512,1280]{1,0:T(8,128)(2,1)S(1)}, u32[]{:S(2)}, u32[]{:S(2)}) %collective-permute-start.16) | collective-permute-done | bytes 1310752 | tf_op jit(solution)/shard_map/ppermute | solution.py:153
  149.7 11.7 %collective-permute-start.18 = (bf16[256,1024]{1,0:T(8,128)(2,1)S(1)}, bf16[256,1024]{1,0:T(8,128)(2,1)S(1)}, u32[]{:S(2)}, u32[]{:S(2)}) collective-permute-start(bf16[256,1024]{1,0:T(8,128)(2,1)S(1)} %add_convert_fusion.5), channel_id=1, source_target_pairs={{0,0},{1,8},{4,4},{5,12},{8,9},{9,1},{12,13},{13,5},{16,18},{17,26... | collective-permute-start | bytes 1572872 | tf_op jit(solution)/shard_map/ppermute | solution.py:153
  169.5 8.3 %collective-permute-done.14 = bf16[512,1280]{1,0:T(8,128)(2,1)S(1)} collective-permute-done((bf16[512,1280]{1,0:T(8,128)(2,1)S(1)}, bf16[512,1280]{1,0:T(8,128)(2,1)S(1)}, u32[]{:S(2)}, u32[]{:S(2)}) %collective-permute-start.14) | collective-permute-done | bytes 1310752 | tf_op jit(solution)/shard_map/ppermute | solution.py:153
  177.8 11.2 %collective-permute-done.18 = bf16[256,1024]{1,0:T(8,128)(2,1)S(1)} collective-permute-done((bf16[256,1024]{1,0:T(8,128)(2,1)S(1)}, bf16[256,1024]{1,0:T(8,128)(2,1)S(1)}, u32[]{:S(2)}, u32[]{:S(2)}) %collective-permute-start.18) | collective-permute-done | bytes 524320 | tf_op jit(solution)/shard_map/ppermute | solution.py:153
  195.7 3.6 %fusion.13 = f32[512,1280]{1,0:T(8,128)S(1)} fusion(bf16[512,1280]{1,0:T(8,128)(2,1)S(1)} %add.197, bf16[512,1280]{1,0:T(8,128)(2,1)} %collective-permute-done.9, bf16[512,1280]{1,0:T(8,128)(2,1)S(1)} %copy-done.8, bf16[2048,512]{1,0:T(8,128)(2,1)S(1)} %get-tuple-element.90), kind=kOutput, calls=%fused_computation.33 | convolution fusion | flops 2025062400 | bytes 8126464 | tf_op jit(solution)/shard_map/dot_general | solution.py:198
  199.3 3.6 %fusion.14 = f32[512,1280]{1,0:T(8,128)S(1)} fusion(bf16[512,1280]{1,0:T(8,128)(2,1)S(1)} %add.197, bf16[512,1280]{1,0:T(8,128)(2,1)} %collective-permute-done.9, bf16[512,1280]{1,0:T(8,128)(2,1)S(1)} %copy-done.8, bf16[2048,512]{1,0:T(8,128)(2,1)S(1)} %get-tuple-element.95), kind=kOutput, calls=%fused_computation.34 | convolution fusion | flops 2025062400 | bytes 8126464 | tf_op jit(solution)/shard_map/dot_general | solution.py:198
  208.7 7.9 %collective-permute-done.24 = bf16[512,768]{1,0:T(8,128)(2,1)S(1)} collective-permute-done((bf16[512,768]{1,0:T(8,128)(2,1)S(1)}, bf16[512,768]{1,0:T(8,128)(2,1)S(1)}, u32[]{:S(2)}, u32[]{:S(2)}) %collective-permute-start.24) | collective-permute-done | bytes 786464 | tf_op jit(solution)/shard_map/ppermute | solution.py:153
  229.3 6.4 %collective-permute-done.28 = bf16[512,768]{1,0:T(8,128)(2,1)S(1)} collective-permute-done((bf16[512,768]{1,0:T(8,128)(2,1)S(1)}, bf16[512,768]{1,0:T(8,128)(2,1)S(1)}, u32[]{:S(2)}, u32[]{:S(2)}) %collective-permute-start.28) | collective-permute-done | bytes 786464 | tf_op jit(solution)/shard_map/ppermute | solution.py:153
  235.7 4.8 %collective-permute-done.27 = bf16[256,1024]{1,0:T(8,128)(2,1)} collective-permute-done((bf16[256,1024]{1,0:T(8,128)(2,1)S(1)}, bf16[256,1024]{1,0:T(8,128)(2,1)}, u32[]{:S(2)}, u32[]{:S(2)}) %collective-permute-start.27) | collective-permute-done | bytes 524320 | tf_op jit(solution)/shard_map/ppermute | solution.py:153
  241.0 3.1 %collective-permute-start.33 = (f32[2,512]{1,0:T(2,128)S(1)}, f32[2,512]{1,0:T(2,128)S(1)}, u32[]{:S(2)}, u32[]{:S(2)}) collective-permute-start(f32[2,512]{1,0:T(2,128)S(1)} %pad_maximum_fusion.11), channel_id=1, source_target_pairs={{0,1},{1,0},{2,3},{3,2},{4,5},{5,4},{6,7},{7,6},{8,9},{9,8},{10,11... | collective-permute-start | bytes 12296 | tf_op jit(solution)/shard_map/ppermute | solution.py:153
  253.9 2.4 collective-permute-start.37
  257.7 4.7 %collective-permute-start.38 = (f32[2,128]{0,1:T(8,128)S(1)}, f32[2,128]{0,1:T(8,128)S(1)}, u32[]{:S(2)}, u32[]{:S(2)}) collective-permute-start(f32[2,128]{0,1:T(8,128)S(1)} %broadcast_in_dim.20), channel_id=1, source_target_pairs={{0,1},{1,0},{2,3},{3,2},{4,5},{5,4},{6,7},{7,6},{8,9},{9,8},{10,11... | collective-permute-start | bytes 3080 | tf_op jit(solution)/shard_map/ppermute | solution.py:153
  263.9 4.4 %collective-permute-start.31 = (bf16[256,1024]{1,0:T(8,128)(2,1)S(1)}, bf16[256,1024]{1,0:T(8,128)(2,1)S(1)}, u32[]{:S(2)}, u32[]{:S(2)}) collective-permute-start(bf16[256,1024]{1,0:T(8,128)(2,1)S(1)} %add_convert_fusion.2), channel_id=1, source_target_pairs={{1,24},{5,28},{9,17},{13,21},{17,10},{21,14},{25,3},{29,7}} | collective-permute-start | bytes 1572872 | tf_op jit(solution)/shard_map/ppermute | solution.py:153
  270.9 5.9 %collective-permute-done.39 = f32[2,128]{0,1:T(8,128)S(1)} collective-permute-done((f32[2,128]{0,1:T(8,128)S(1)}, f32[2,128]{0,1:T(8,128)S(1)}, u32[]{:S(2)}, u32[]{:S(2)}) %collective-permute-start.39) | collective-permute-done | bytes 1056 | tf_op jit(solution)/shard_map/ppermute | solution.py:153
  277.0 3.5 %multiply_multiply_fusion.1 = f32[512,1280]{1,0:T(8,128)} fusion(f32[512,1280]{1,0:T(8,128)} %copy-done, f32[1280]{0:T(1024)S(1)} %get-tuple-element.128, f32[512]{0:T(512)S(1)} %bitcast.53), kind=kLoop, calls=%fused_computation.16 | loop fusion | flops 1310720 | bytes 5250048 | tf_op jit(solution)/shard_map/mul | solution.py:393
  (182 shorter events, 87.6 us)
Async XLA Ops:
  0.6 30.8 %collective-permute-start.3 = (bf16[512,1280]{1,0:T(8,128)(2,1)}, bf16[512,1280]{1,0:T(8,128)(2,1)S(1)}, u32[]{:S(2)}, u32[]{:S(2)}) collective-permute-start(bf16[512,1280]{1,0:T(8,128)(2,1)} %param.16), channel_id=1, source_target_pairs={{0,4},{1,5},{2,6},{3,7},{4,0},{5,1},{6,2},{7,3},{8,12},{9,13},{10,... | collective-permute-start | bytes 3932168 | tf_op jit(solution)/shard_map/ppermute | solution.py:153
  5.2 16.0 %collective-permute-start = (bf16[128,1024]{1,0:T(8,128)(2,1)}, bf16[128,1024]{1,0:T(8,128)(2,1)S(1)}, u32[]{:S(2)}, u32[]{:S(2)}) collective-permute-start(bf16[128,1024]{1,0:T(8,128)(2,1)} %get-tuple-element.140), channel_id=1, source_target_pairs={{0,8},{1,9},{2,10},{3,11},{4,12},{5,13},{6,14},{7,15},{8,0},{9,1},... | collective-permute-start | bytes 786440 | tf_op jit(solution)/shard_map/ppermute | solution.py:153
  6.5 14.7 %collective-permute-start.1 = (bf16[128,1024]{1,0:T(8,128)(2,1)}, bf16[128,1024]{1,0:T(8,128)(2,1)S(1)}, u32[]{:S(2)}, u32[]{:S(2)}) collective-permute-start(bf16[128,1024]{1,0:T(8,128)(2,1)} %get-tuple-element.139), channel_id=1, source_target_pairs={{0,16},{1,17},{2,18},{3,19},{4,20},{5,21},{6,22},{7,23},{8,24},{9,... | collective-permute-start | bytes 786440 | tf_op jit(solution)/shard_map/ppermute | solution.py:153
  8.8 16.8 %collective-permute-start.2 = (bf16[128,1024]{1,0:T(8,128)(2,1)}, bf16[128,1024]{1,0:T(8,128)(2,1)S(1)}, u32[]{:S(2)}, u32[]{:S(2)}) collective-permute-start(bf16[128,1024]{1,0:T(8,128)(2,1)} %get-tuple-element.138), channel_id=1, source_target_pairs={{0,24},{1,25},{2,26},{3,27},{4,28},{5,29},{6,30},{7,31},{8,16},{9,... | collective-permute-start | bytes 786440 | tf_op jit(solution)/shard_map/ppermute | solution.py:153
  31.5 29.4 %collective-permute-start.4 = (bf16[512,1280]{1,0:T(8,128)(2,1)}, bf16[512,1280]{1,0:T(8,128)(2,1)}, u32[]{:S(2)}, u32[]{:S(2)}) collective-permute-start(bf16[512,1280]{1,0:T(8,128)(2,1)} %shard_map.137), channel_id=1, source_target_pairs={{0,8},{1,9},{2,10},{3,11},{4,12},{5,13},{6,14},{7,15},{8,0},{9,1},... | collective-permute-start | bytes 3932168 | tf_op jit(solution)/shard_map/ppermute | solution.py:153
  32.7 28.1 %collective-permute-start.5 = (bf16[512,1280]{1,0:T(8,128)(2,1)}, bf16[512,1280]{1,0:T(8,128)(2,1)}, u32[]{:S(2)}, u32[]{:S(2)}) collective-permute-start(bf16[512,1280]{1,0:T(8,128)(2,1)} %shard_map.137), channel_id=1, source_target_pairs={{8,16},{9,17},{10,18},{11,19},{12,20},{13,21},{14,22},{15,23},{16,... | collective-permute-start | bytes 3932168 | tf_op jit(solution)/shard_map/ppermute | solution.py:153
  34.4 28.8 %collective-permute-start.6 = (bf16[512,1280]{1,0:T(8,128)(2,1)}, bf16[512,1280]{1,0:T(8,128)(2,1)}, u32[]{:S(2)}, u32[]{:S(2)}) collective-permute-start(bf16[512,1280]{1,0:T(8,128)(2,1)} %param.17), channel_id=1, source_target_pairs={{0,4},{1,5},{2,6},{3,7},{4,0},{5,1},{6,2},{7,3},{8,12},{9,13},{10,... | collective-permute-start | bytes 3932168 | tf_op jit(solution)/shard_map/ppermute | solution.py:153
  35.6 35.5 %collective-permute-start.10 = (bf16[512,1280]{1,0:T(8,128)(2,1)S(1)}, bf16[512,1280]{1,0:T(8,128)(2,1)S(1)}, u32[]{:S(2)}, u32[]{:S(2)}) collective-permute-start(bf16[512,1280]{1,0:T(8,128)(2,1)S(1)} %copy-done.6), channel_id=1, source_target_pairs={{8,16},{9,17},{10,18},{11,19},{12,20},{13,21},{14,22},{15,23},{16,... | collective-permute-start | bytes 3932168 | tf_op jit(solution)/shard_map/ppermute | solution.py:153
  36.4 52.5 %collective-permute-start.9 = (bf16[512,1280]{1,0:T(8,128)(2,1)S(1)}, bf16[512,1280]{1,0:T(8,128)(2,1)}, u32[]{:S(2)}, u32[]{:S(2)}) collective-permute-start(bf16[512,1280]{1,0:T(8,128)(2,1)S(1)} %copy-done.6), channel_id=1, source_target_pairs={{0,8},{1,9},{2,10},{3,11},{4,12},{5,13},{6,14},{7,15},{8,0},{9,1},... | collective-permute-start | bytes 3932168 | tf_op jit(solution)/shard_map/ppermute | solution.py:153
  63.2 25.7 %collective-permute-start.11 = (bf16[3,128,1024]{2,1,0:T(8,128)(2,1)S(1)}, bf16[3,128,1024]{2,1,0:T(8,128)(2,1)S(1)}, u32[]{:S(2)}, u32[]{:S(2)}) collective-permute-start(bf16[3,128,1024]{2,1,0:T(8,128)(2,1)S(1)} %pad_maximum_fusion.9), channel_id=1, source_target_pairs={{0,2},{1,3},{2,0},{3,1},{4,6},{5,7},{6,4},{7,5},{8,10},{9,11},{10,... | collective-permute-start | bytes 2359304 | tf_op jit(solution)/shard_map/ppermute | solution.py:153
  66.5 50.5 %collective-permute-start.7 = (bf16[512,1280]{1,0:T(8,128)(2,1)}, bf16[512,1280]{1,0:T(8,128)(2,1)}, u32[]{:S(2)}, u32[]{:S(2)}) collective-permute-start(bf16[512,1280]{1,0:T(8,128)(2,1)} %collective-permute-done.5), channel_id=1, source_target_pairs={{8,0},{9,1},{10,2},{11,3},{12,4},{13,5},{14,6},{15,7},{16,24},{17,... | collective-permute-start | bytes 3932168 | tf_op jit(solution)/shard_map/ppermute | solution.py:153
  67.8 49.2 %collective-permute-start.8 = (bf16[512,1280]{1,0:T(8,128)(2,1)}, bf16[512,1280]{1,0:T(8,128)(2,1)}, u32[]{:S(2)}, u32[]{:S(2)}) collective-permute-start(bf16[512,1280]{1,0:T(8,128)(2,1)} %collective-permute-done.4), channel_id=1, source_target_pairs={{8,16},{9,17},{10,18},{11,19},{12,20},{13,21},{14,22},{15,23},{16,... | collective-permute-start | bytes 3932168 | tf_op jit(solution)/shard_map/ppermute | solution.py:153
  89.1 27.9 %collective-permute-start.12 = (bf16[2,3,128,1024]{3,2,1,0:T(8,128)(2,1)S(1)}, bf16[2,3,128,1024]{3,2,1,0:T(8,128)(2,1)}, u32[]{:S(2)}, u32[]{:S(2)}) collective-permute-start(bf16[2,3,128,1024]{3,2,1,0:T(8,128)(2,1)S(1)} %pad_maximum_fusion.7), channel_id=1, source_target_pairs={{0,1},{1,0},{2,3},{3,2},{4,5},{5,4},{6,7},{7,6},{8,9},{9,8},{10,11... | collective-permute-start | bytes 4718600 | tf_op jit(solution)/shard_map/ppermute | solution.py:153
  104.6 12.3 %collective-permute-start.13 = (bf16[512,1024]{1,0:T(8,128)(2,1)}, bf16[512,1024]{1,0:T(8,128)(2,1)}, u32[]{:S(2)}, u32[]{:S(2)}) collective-permute-start(bf16[512,1024]{1,0:T(8,128)(2,1)} %select_convert_fusion), channel_id=1, source_target_pairs={{0,1},{1,0},{2,3},{3,2},{4,5},{5,4},{6,7},{7,6},{8,9},{9,8},{10,11... | collective-permute-start | bytes 3145736 | tf_op jit(solution)/shard_map/ppermute | solution.py:153
  106.1 30.1 %collective-permute-start.15 = (bf16[512,1280]{1,0:T(8,128)(2,1)}, bf16[512,1280]{1,0:T(8,128)(2,1)S(1)}, u32[]{:S(2)}, u32[]{:S(2)}) collective-permute-start(bf16[512,1280]{1,0:T(8,128)(2,1)} %collective-permute-done.9), channel_id=1, source_target_pairs={{8,16},{9,17},{10,18},{11,19},{12,20},{13,21},{14,22},{15,23},{16,... | collective-permute-start | bytes 3932168 | tf_op jit(solution)/shard_map/ppermute | solution.py:153
  118.8 17.2 %collective-permute-start.17 = (bf16[256,1024]{1,0:T(8,128)(2,1)S(1)}, bf16[256,1024]{1,0:T(8,128)(2,1)S(1)}, u32[]{:S(2)}, u32[]{:S(2)}) collective-permute-start(bf16[256,1024]{1,0:T(8,128)(2,1)S(1)} %dynamic-slice_convert_fusion.2), channel_id=1, source_target_pairs={{0,2},{1,3},{2,0},{3,1},{4,6},{5,7},{6,4},{7,5},{8,10},{9,11},{10,... | collective-permute-start | bytes 1572872 | tf_op jit(solution)/shard_map/ppermute | solution.py:153
  119.7 30.1 %collective-permute-start.16 = (bf16[512,1280]{1,0:T(8,128)(2,1)}, bf16[512,1280]{1,0:T(8,128)(2,1)S(1)}, u32[]{:S(2)}, u32[]{:S(2)}) collective-permute-start(bf16[512,1280]{1,0:T(8,128)(2,1)} %collective-permute-done.8), channel_id=1, source_target_pairs={{8,0},{9,1},{10,2},{11,3},{12,4},{13,5},{14,6},{15,7},{16,24},{17,... | collective-permute-start | bytes 3932168 | tf_op jit(solution)/shard_map/ppermute | solution.py:153
  123.0 54.8 %collective-permute-start.14 = (bf16[512,1280]{1,0:T(8,128)(2,1)S(1)}, bf16[512,1280]{1,0:T(8,128)(2,1)S(1)}, u32[]{:S(2)}, u32[]{:S(2)}) collective-permute-start(bf16[512,1280]{1,0:T(8,128)(2,1)S(1)} %collective-permute-done.10), channel_id=1, source_target_pairs={{8,0},{9,1},{10,2},{11,3},{12,4},{13,5},{14,6},{15,7},{16,24},{17,... | collective-permute-start | bytes 3932168 | tf_op jit(solution)/shard_map/ppermute | solution.py:153
  149.7 39.3 %collective-permute-start.18 = (bf16[256,1024]{1,0:T(8,128)(2,1)S(1)}, bf16[256,1024]{1,0:T(8,128)(2,1)S(1)}, u32[]{:S(2)}, u32[]{:S(2)}) collective-permute-start(bf16[256,1024]{1,0:T(8,128)(2,1)S(1)} %add_convert_fusion.5), channel_id=1, source_target_pairs={{0,0},{1,8},{4,4},{5,12},{8,9},{9,1},{12,13},{13,5},{16,18},{17,26... | collective-permute-start | bytes 1572872 | tf_op jit(solution)/shard_map/ppermute | solution.py:153
  161.4 27.7 %collective-permute-start.19 = (bf16[256,1024]{1,0:T(8,128)(2,1)S(1)}, bf16[256,1024]{1,0:T(8,128)(2,1)S(1)}, u32[]{:S(2)}, u32[]{:S(2)}) collective-permute-start(bf16[256,1024]{1,0:T(8,128)(2,1)S(1)} %add_convert_fusion.5), channel_id=1, source_target_pairs={{2,0},{3,8},{6,4},{7,12},{10,9},{11,1},{14,13},{15,5},{18,18},{19,... | collective-permute-start | bytes 1572872 | tf_op jit(solution)/shard_map/ppermute | solution.py:153
  165.6 37.3 %collective-permute-start.22 = (bf16[512,1280]{1,0:T(8,128)(2,1)S(1)}, bf16[512,1280]{1,0:T(8,128)(2,1)S(1)}, u32[]{:S(2)}, u32[]{:S(2)}) collective-permute-start(bf16[512,1280]{1,0:T(8,128)(2,1)S(1)} %add_convert_fusion), channel_id=1, source_target_pairs={{0,4},{1,5},{2,6},{3,7},{4,0},{5,1},{6,2},{7,3},{8,12},{9,13},{10,... | collective-permute-start | bytes 3932168 | tf_op jit(solution)/shard_map/ppermute | solution.py:153
  167.0 36.0 %collective-permute-start.21 = (bf16[512,512]{1,0:T(8,128)(2,1)S(1)}, bf16[512,512]{1,0:T(8,128)(2,1)S(1)}, u32[]{:S(2)}, u32[]{:S(2)}) collective-permute-start(bf16[512,512]{1,0:T(8,128)(2,1)S(1)} %slice.129), channel_id=1, source_target_pairs={{8,0},{9,1},{10,2},{11,3},{12,4},{13,5},{14,6},{15,7},{16,24},{17,... | collective-permute-start | bytes 1572872 | tf_op jit(solution)/shard_map/ppermute | solution.py:153
  192.8 10.2 %collective-permute-start.20 = (bf16[512,1024]{1,0:T(8,128)(2,1)S(1)}, bf16[512,1024]{1,0:T(8,128)(2,1)S(1)}, u32[]{:S(2)}, u32[]{:S(2)}) collective-permute-start(bf16[512,1024]{1,0:T(8,128)(2,1)S(1)} %get-tuple-element.147), channel_id=1, source_target_pairs={{1,0},{3,2},{5,4},{7,6},{9,8},{11,10},{13,12},{15,14},{17,16},{19,... | collective-permute-start | bytes 3145736 | tf_op jit(solution)/shard_map/ppermute | solution.py:153
  194.1 22.5 %collective-permute-start.24 = (bf16[512,768]{1,0:T(8,128)(2,1)S(1)}, bf16[512,768]{1,0:T(8,128)(2,1)S(1)}, u32[]{:S(2)}, u32[]{:S(2)}) collective-permute-start(bf16[512,768]{1,0:T(8,128)(2,1)S(1)} %slice.134), channel_id=1, source_target_pairs={{8,0},{9,1},{10,2},{11,3},{12,4},{13,5},{14,6},{15,7},{16,24},{17,... | collective-permute-start | bytes 2359304 | tf_op jit(solution)/shard_map/ppermute | solution.py:153
  203.3 13.3 %collective-permute-start.25 = (bf16[256,1024]{1,0:T(8,128)(2,1)S(1)}, bf16[256,1024]{1,0:T(8,128)(2,1)S(1)}, u32[]{:S(2)}, u32[]{:S(2)}) collective-permute-start(bf16[256,1024]{1,0:T(8,128)(2,1)S(1)} %dynamic-slice_convert_fusion.1), channel_id=1, source_target_pairs={{0,2},{2,0},{4,6},{6,4},{8,10},{10,8},{12,14},{14,12},{16,18},{18,... | collective-permute-start | bytes 1572872 | tf_op jit(solution)/shard_map/ppermute | solution.py:153
  205.3 12.5 %collective-permute-start.23 = (bf16[512,512]{1,0:T(8,128)(2,1)S(1)}, bf16[512,512]{1,0:T(8,128)(2,1)S(1)}, u32[]{:S(2)}, u32[]{:S(2)}) collective-permute-start(bf16[512,512]{1,0:T(8,128)(2,1)S(1)} %add_convert_fusion.4), channel_id=1, source_target_pairs={{0,4},{1,5},{2,6},{3,7},{4,0},{5,1},{6,2},{7,3},{8,12},{9,13},{10,... | collective-permute-start | bytes 1572872 | tf_op jit(solution)/shard_map/ppermute | solution.py:153
  223.5 12.2 %collective-permute-start.28 = (bf16[512,768]{1,0:T(8,128)(2,1)S(1)}, bf16[512,768]{1,0:T(8,128)(2,1)S(1)}, u32[]{:S(2)}, u32[]{:S(2)}) collective-permute-start(bf16[512,768]{1,0:T(8,128)(2,1)S(1)} %add_convert_fusion.1), channel_id=1, source_target_pairs={{0,4},{1,5},{2,6},{3,7},{4,0},{5,1},{6,2},{7,3},{8,12},{9,13},{10,... | collective-permute-start | bytes 2359304 | tf_op jit(solution)/shard_map/ppermute | solution.py:153
  226.9 13.6 %collective-permute-start.27 = (bf16[256,1024]{1,0:T(8,128)(2,1)S(1)}, bf16[256,1024]{1,0:T(8,128)(2,1)}, u32[]{:S(2)}, u32[]{:S(2)}) collective-permute-start(bf16[256,1024]{1,0:T(8,128)(2,1)S(1)} %dynamic-slice_convert_fusion), channel_id=1, source_target_pairs={{1,3},{3,1},{5,7},{7,5},{9,11},{11,9},{13,15},{15,13},{17,19},{19,... | collective-permute-start | bytes 1572872 | tf_op jit(solution)/shard_map/ppermute | solution.py:153
  257.7 11.4 %collective-permute-start.38 = (f32[2,128]{0,1:T(8,128)S(1)}, f32[2,128]{0,1:T(8,128)S(1)}, u32[]{:S(2)}, u32[]{:S(2)}) collective-permute-start(f32[2,128]{0,1:T(8,128)S(1)} %broadcast_in_dim.20), channel_id=1, source_target_pairs={{0,1},{1,0},{2,3},{3,2},{4,5},{5,4},{6,7},{7,6},{8,9},{9,8},{10,11... | collective-permute-start | bytes 3080 | tf_op jit(solution)/shard_map/ppermute | solution.py:153
  263.9 18.4 %collective-permute-start.31 = (bf16[256,1024]{1,0:T(8,128)(2,1)S(1)}, bf16[256,1024]{1,0:T(8,128)(2,1)S(1)}, u32[]{:S(2)}, u32[]{:S(2)}) collective-permute-start(bf16[256,1024]{1,0:T(8,128)(2,1)S(1)} %add_convert_fusion.2), channel_id=1, source_target_pairs={{1,24},{5,28},{9,17},{13,21},{17,10},{21,14},{25,3},{29,7}} | collective-permute-start | bytes 1572872 | tf_op jit(solution)/shard_map/ppermute | solution.py:153
  268.3 14.0 %collective-permute-start.32 = (bf16[256,1024]{1,0:T(8,128)(2,1)S(1)}, bf16[256,1024]{1,0:T(8,128)(2,1)S(1)}, u32[]{:S(2)}, u32[]{:S(2)}) collective-permute-start(bf16[256,1024]{1,0:T(8,128)(2,1)S(1)} %add_convert_fusion.2), channel_id=1, source_target_pairs={{3,24},{7,28},{11,17},{15,21},{19,10},{23,14},{27,3},{31,7}} | collective-permute-start | bytes 1572872 | tf_op jit(solution)/shard_map/ppermute | solution.py:153
  269.1 7.8 %collective-permute-start.39 = (f32[2,128]{0,1:T(8,128)S(1)}, f32[2,128]{0,1:T(8,128)S(1)}, u32[]{:S(2)}, u32[]{:S(2)}) collective-permute-start(f32[2,128]{0,1:T(8,128)S(1)} %broadcast_add_fusion), channel_id=1, source_target_pairs={{0,2},{1,3},{2,0},{3,1},{4,6},{5,7},{6,4},{7,5},{8,10},{9,11},{10,... | collective-permute-start | bytes 3080 | tf_op jit(solution)/shard_map/ppermute | solution.py:153
  (32 other events, 316.7 us)

commit v3 on v2

--- a/solution.py
+++ b/solution.py
@@ -262,27 +262,27 @@
         send(lax.dynamic_slice(mine, (0, (z ^ k) * plane), (piece_rows, plane)), flip_z(k))
         for k in (1, 2, 3)
     ]
-    gate_other = send(gate_weight, FLIP_X)
     g = front(gate_kernel, teacher_ids, adv_table, (hidden_cot, gate_pre, up_pre))
     u = front(up_kernel, teacher_ids, adv_table, (hidden_cot, gate_pre))
-    piece, g, u, gate_other, up_weight = tie(piece, g, u, gate_other, up_weight)
+    piece, g, u, gate_weight, up_weight = tie(piece, g, u, gate_weight, up_weight)
+    gate_other = send(gate_weight, FLIP_X)
 
     g_near = send(g, flip_z(1))
     g_over = send(g, MIDDLE)
     u_near = send(u, flip_z(1))
     u_over = send(u, MIDDLE)
+    piece = jnp.stack(piece)
+    g_near, g_over, gate_other, piece, up_weight = tie(g_near, g_over, gate_other, piece, up_weight)
     up_other = send(up_weight, FLIP_X)
-    piece = jnp.stack(piece)
-    g_near, g_over, up_other, piece = tie(g_near, g_over, up_other, piece)
 
     g_far = send(g_over, OUTWARD)
     g_near_over = send(g_near, MIDDLE)
     piece_y = send(piece, FLIP_Y)
     gate_rows = plane_rows(gate_weight, gate_other)
+    u_near, u_over, gate_rows, up_other, piece, piece_y = tie(
+        u_near, u_over, gate_rows, up_other, piece, piece_y
+    )
     up_rows = plane_rows(up_weight, up_other)
-    u_near, u_over, gate_rows, up_rows, piece, piece_y = tie(
-        u_near, u_over, gate_rows, up_rows, piece, piece_y
-    )
 
     u_near_over = send(u_near, MIDDLE)
     pieces = jnp.stack([piece, piece_y])
@@ -295,9 +295,10 @@
         g_far, g_near_over, pieces, pieces_c, early_keep, early_recv, u_over
     )
 
-    early_keep, early_away = over_y(early_keep + early_recv.astype(f32))
+    early_sum = early_keep + early_recv.astype(f32)
+    g_farthest = send(g_near_over, OUTWARD)
+    early_keep, early_away = over_y(early_sum)
     early_recv = send(early_away, FLIP_Y)
-    g_farthest = send(g_near_over, OUTWARD)
     u_far = send(u_over, OUTWARD)
     far = jnp.zeros((3, model_size, piece_rows, plane), bf16)
     for part, place in ((pieces[0], m), (pieces_c[0], m ^ 1), (pieces[1], m ^ 2), (pieces_c[1], m ^ 3)):

time: 286 us -> 282 us (0.986)
  waiting for transfers between devices: 123 us -> 104 us
  starting transfers between devices: 75.6 us -> 88.3 us
    ppermute x40, waiting for transfers between devices: 123 us -> 104 us  [send(): return lax.ppermute(value, AXES, permutation)]
    ppermute x40, starting transfers between devices: 75.6 us -> 88.3 us  [send(): return lax.ppermute(value, AXES, permutation)]
where the time goes in v3:
time: 282 us; the launch traced here: 281 us
  waiting for transfers between devices  104 us (37%)
  starting transfers between devices  88.3 us (31%)
  matrix products  33.4 us (12%)
  other arithmetic  23.1 us (8%)
  local copies, waits for them, and re-layouts  19.3 us (7%)
  Pallas kernels  10.8 us (4%)
    ppermute x40, waiting for transfers between devices, send(): return lax.ppermute(value, AXES, permutation)  104 us
    ppermute x40, starting transfers between devices, send(): return lax.ppermute(value, AXES, permutation)  88.3 us
    dot_general x10, matrix products, dot_first(): lax.dot_general(a, b, (((0,), (0,)), ((), ())), preferred_element_type=f32)  18.4 us
    dot_general x7, matrix products, dot_last(): lax.dot_general(a, b, (((1,), (1,)), ((), ())), preferred_element_type=f32)  15 us
    pallas_call x2, Pallas kernels, front(): pl.pallas_call(kernel, grid=(tokens // rows,), in_specs=[pl.BlockSpec((ro...  10.8 us
  transfers between devices with their start and end apart: 40, of which 19 were waited for; matrix products, arithmetic and copies ran while one was open for 23% of the time, Pallas kernels for 4%

profile of v3, /device:TPU:1, one launch (start us, length us, event | category | flops | bytes accessed | tf_op | source)
XLA Modules:
  0.0 280.7 jit_solution(3902920396701317639)
XLA Ops:
  2.3 2.2 collective-permute-start
  4.5 2.3 collective-permute-start.1
  8.4 4.4 %shard_map.138 = bf16[512,1280]{1,0:T(8,128)(2,1)} custom-call(s32[512,1]{1,0:T(8,128)} %copy.15.ids_ref, f32[1,64]{1,0:T(1,128)} %bitcast.57, bf16[512,1280]{1,0:T(8,128)(2,1)} %cot_ref.3, bf16[512,1280]{1,0:T(8,128)(2,1)} %gate_ref.3), custom_call_target="tpu_custom_call" | custom-call | flops 655360 | bytes 655360 | tf_op jit(solution)/shard_map/pallas_call | solution.py:181
  12.8 6.4 %shard_map.137 = bf16[512,1280]{1,0:T(8,128)(2,1)} custom-call(s32[512,1]{1,0:T(8,128)} %copy.15.ids_ref, f32[1,64]{1,0:T(1,128)} %bitcast.58, bf16[512,1280]{1,0:T(8,128)(2,1)} %cot_ref.3, bf16[512,1280]{1,0:T(8,128)(2,1)} %gate_ref.3, bf16[512,1280]{1,0:T(8,128)(2,1)} %up_ref.1), custom_call_target="tpu_custom_call" | custom-call | flops 655360 | bytes 655360 | tf_op jit(solution)/shard_map/pallas_call | solution.py:181
  19.2 4.5 %collective-permute-done.2 = bf16[128,1024]{1,0:T(8,128)(2,1)S(1)} collective-permute-done((bf16[128,1024]{1,0:T(8,128)(2,1)S(1)}, bf16[128,1024]{1,0:T(8,128)(2,1)S(1)}, u32[]{:S(2)}, u32[]{:S(2)}) %collective-permute-start.2) | collective-permute-done | bytes 262176 | tf_op jit(solution)/shard_map/ppermute | solution.py:153
  23.7 5.8 %collective-permute-start.3 = (bf16[512,1280]{1,0:T(8,128)(2,1)}, bf16[512,1280]{1,0:T(8,128)(2,1)}, u32[]{:S(2)}, u32[]{:S(2)}) collective-permute-start(bf16[512,1280]{1,0:T(8,128)(2,1)} %shard_map.137), channel_id=1, source_target_pairs={{0,8},{1,9},{2,10},{3,11},{4,12},{5,13},{6,14},{7,15},{8,0},{9,1},... | collective-permute-start | bytes 3932168 | tf_op jit(solution)/shard_map/ppermute | solution.py:153
  35.9 21.1 %collective-permute-done.3 = bf16[512,1280]{1,0:T(8,128)(2,1)} collective-permute-done((bf16[512,1280]{1,0:T(8,128)(2,1)}, bf16[512,1280]{1,0:T(8,128)(2,1)}, u32[]{:S(2)}, u32[]{:S(2)}) %collective-permute-start.3) | collective-permute-done | bytes 1310752 | tf_op jit(solution)/shard_map/ppermute | solution.py:153
  57.1 2.6 collective-permute-done.5
  67.0 18.2 %collective-permute-done.8 = bf16[512,1280]{1,0:T(8,128)(2,1)} collective-permute-done((bf16[512,1280]{1,0:T(8,128)(2,1)S(1)}, bf16[512,1280]{1,0:T(8,128)(2,1)}, u32[]{:S(2)}, u32[]{:S(2)}) %collective-permute-start.8) | collective-permute-done | bytes 1310752 | tf_op jit(solution)/shard_map/ppermute | solution.py:153
  87.4 4.2 %collective-permute-start.12 = (bf16[2,3,128,1024]{3,2,1,0:T(8,128)(2,1)S(1)}, bf16[2,3,128,1024]{3,2,1,0:T(8,128)(2,1)}, u32[]{:S(2)}, u32[]{:S(2)}) collective-permute-start(bf16[2,3,128,1024]{3,2,1,0:T(8,128)(2,1)S(1)} %pad_maximum_fusion.7), channel_id=1, source_target_pairs={{0,1},{1,0},{2,3},{3,2},{4,5},{5,4},{6,7},{7,6},{8,9},{9,8},{10,11... | collective-permute-start | bytes 4718600 | tf_op jit(solution)/shard_map/ppermute | solution.py:153
  94.6 4.3 %fusion.4 = f32[1024,1024]{1,0:T(8,128)S(1)} fusion(bf16[1024,1280]{1,0:T(8,128)(2,1)S(1)} %constant_dynamic-update-slice_fusion, bf16[512,1280]{1,0:T(8,128)(2,1)} %collective-permute-done.8, bf16[512,1280]{1,0:T(8,128)(2,1)S(1)} %copy-done.9), kind=kOutput, calls=%fused_computation.10 | convolution fusion | flops 2689597440 | bytes 9437184 | tf_op jit(solution)/shard_map/dot_general | solution.py:202
  98.9 4.3 %fusion.10 = f32[1024,1024]{1,0:T(8,128)S(1)} fusion(f32[1024,1024]{1,0:T(8,128)S(1)} %fusion.4, bf16[1024,1280]{1,0:T(8,128)(2,1)S(1)} %constant_dynamic-update-slice_fusion.2, bf16[512,1280]{1,0:T(8,128)(2,1)} %collective-permute-done.3, bf16[512,1280]{1,0:T(8,128)(2,1)S(1)} %copy-done.12), kind=kOutput, calls=%fused_computation.32 | convolution fusion | flops 2690646016 | bytes 13631488 | tf_op jit(solution)/shard_map/dot_general | solution.py:202
  108.5 2.6 slice_select_fusion
  125.3 3.6 %fusion.15 = f32[512,1280]{1,0:T(8,128)S(1)} fusion(bf16[512,1280]{1,0:T(8,128)(2,1)S(1)} %add.190, bf16[512,1280]{1,0:T(8,128)(2,1)} %collective-permute-done.3, bf16[512,1280]{1,0:T(8,128)(2,1)S(1)} %copy-done.13, bf16[2048,512]{1,0:T(8,128)(2,1)S(1)} %get-tuple-element.92), kind=kOutput, calls=%fused_computation.35 | convolution fusion | flops 2025062400 | bytes 8126464 | tf_op jit(solution)/shard_map/dot_general | solution.py:198
  128.9 3.6 %fusion.16 = f32[512,1280]{1,0:T(8,128)S(1)} fusion(bf16[512,1280]{1,0:T(8,128)(2,1)S(1)} %add.190, bf16[512,1280]{1,0:T(8,128)(2,1)} %collective-permute-done.3, bf16[512,1280]{1,0:T(8,128)(2,1)S(1)} %copy-done.13, bf16[2048,512]{1,0:T(8,128)(2,1)S(1)} %get-tuple-element.97), kind=kOutput, calls=%fused_computation.36 | convolution fusion | flops 2025062400 | bytes 8126464 | tf_op jit(solution)/shard_map/dot_general | solution.py:198
  132.7 9.7 %collective-permute-done.16 = bf16[512,1280]{1,0:T(8,128)(2,1)S(1)} collective-permute-done((bf16[512,1280]{1,0:T(8,128)(2,1)}, bf16[512,1280]{1,0:T(8,128)(2,1)S(1)}, u32[]{:S(2)}, u32[]{:S(2)}) %collective-permute-start.16) | collective-permute-done | bytes 1310752 | tf_op jit(solution)/shard_map/ppermute | solution.py:153
  142.4 16.5 %collective-permute-start.18 = (bf16[256,1024]{1,0:T(8,128)(2,1)S(1)}, bf16[256,1024]{1,0:T(8,128)(2,1)S(1)}, u32[]{:S(2)}, u32[]{:S(2)}) collective-permute-start(bf16[256,1024]{1,0:T(8,128)(2,1)S(1)} %add_convert_fusion.5), channel_id=1, source_target_pairs={{0,0},{1,8},{4,4},{5,12},{8,9},{9,1},{12,13},{13,5},{16,18},{17,26... | collective-permute-start | bytes 1572872 | tf_op jit(solution)/shard_map/ppermute | solution.py:153
  167.0 3.5 %collective-permute-done.14 = bf16[512,1280]{1,0:T(8,128)(2,1)S(1)} collective-permute-done((bf16[512,1280]{1,0:T(8,128)(2,1)S(1)}, bf16[512,1280]{1,0:T(8,128)(2,1)S(1)}, u32[]{:S(2)}, u32[]{:S(2)}) %collective-permute-start.14) | collective-permute-done | bytes 1310752 | tf_op jit(solution)/shard_map/ppermute | solution.py:153
  170.5 11.2 %collective-permute-done.18 = bf16[256,1024]{1,0:T(8,128)(2,1)S(1)} collective-permute-done((bf16[256,1024]{1,0:T(8,128)(2,1)S(1)}, bf16[256,1024]{1,0:T(8,128)(2,1)S(1)}, u32[]{:S(2)}, u32[]{:S(2)}) %collective-permute-start.18) | collective-permute-done | bytes 524320 | tf_op jit(solution)/shard_map/ppermute | solution.py:153
  185.4 6.1 %collective-permute-start.20 = (bf16[512,1024]{1,0:T(8,128)(2,1)S(1)}, bf16[512,1024]{1,0:T(8,128)(2,1)S(1)}, u32[]{:S(2)}, u32[]{:S(2)}) collective-permute-start(bf16[512,1024]{1,0:T(8,128)(2,1)S(1)} %get-tuple-element.149), channel_id=1, source_target_pairs={{1,0},{3,2},{5,4},{7,6},{9,8},{11,10},{13,12},{15,14},{17,16},{19,... | collective-permute-start | bytes 3145736 | tf_op jit(solution)/shard_map/ppermute | solution.py:153
  193.1 3.6 %fusion.13 = f32[512,1280]{1,0:T(8,128)S(1)} fusion(bf16[512,1280]{1,0:T(8,128)(2,1)S(1)} %add.197, bf16[512,1280]{1,0:T(8,128)(2,1)} %collective-permute-done.8, bf16[512,1280]{1,0:T(8,128)(2,1)S(1)} %copy-done.10, bf16[2048,512]{1,0:T(8,128)(2,1)S(1)} %get-tuple-element.92), kind=kOutput, calls=%fused_computation.33 | convolution fusion | flops 2025062400 | bytes 8126464 | tf_op jit(solution)/shard_map/dot_general | solution.py:198
  196.7 3.6 %fusion.14 = f32[512,1280]{1,0:T(8,128)S(1)} fusion(bf16[512,1280]{1,0:T(8,128)(2,1)S(1)} %add.197, bf16[512,1280]{1,0:T(8,128)(2,1)} %collective-permute-done.8, bf16[512,1280]{1,0:T(8,128)(2,1)S(1)} %copy-done.10, bf16[2048,512]{1,0:T(8,128)(2,1)S(1)} %get-tuple-element.97), kind=kOutput, calls=%fused_computation.34 | convolution fusion | flops 2025062400 | bytes 8126464 | tf_op jit(solution)/shard_map/dot_general | solution.py:198
  206.1 6.7 %collective-permute-done.24 = bf16[512,768]{1,0:T(8,128)(2,1)S(1)} collective-permute-done((bf16[512,768]{1,0:T(8,128)(2,1)S(1)}, bf16[512,768]{1,0:T(8,128)(2,1)S(1)}, u32[]{:S(2)}, u32[]{:S(2)}) %collective-permute-start.24) | collective-permute-done | bytes 786464 | tf_op jit(solution)/shard_map/ppermute | solution.py:153
  212.8 2.3 collective-permute-done.23
  226.6 6.6 %collective-permute-done.28 = bf16[512,768]{1,0:T(8,128)(2,1)S(1)} collective-permute-done((bf16[512,768]{1,0:T(8,128)(2,1)S(1)}, bf16[512,768]{1,0:T(8,128)(2,1)S(1)}, u32[]{:S(2)}, u32[]{:S(2)}) %collective-permute-start.28) | collective-permute-done | bytes 786464 | tf_op jit(solution)/shard_map/ppermute | solution.py:153
  233.2 4.6 %collective-permute-done.27 = bf16[256,1024]{1,0:T(8,128)(2,1)} collective-permute-done((bf16[256,1024]{1,0:T(8,128)(2,1)S(1)}, bf16[256,1024]{1,0:T(8,128)(2,1)}, u32[]{:S(2)}, u32[]{:S(2)}) %collective-permute-start.27) | collective-permute-done | bytes 524320 | tf_op jit(solution)/shard_map/ppermute | solution.py:153
  238.2 3.1 %collective-permute-start.33 = (f32[2,512]{1,0:T(2,128)S(1)}, f32[2,512]{1,0:T(2,128)S(1)}, u32[]{:S(2)}, u32[]{:S(2)}) collective-permute-start(f32[2,512]{1,0:T(2,128)S(1)} %pad_maximum_fusion.11), channel_id=1, source_target_pairs={{0,1},{1,0},{2,3},{3,2},{4,5},{5,4},{6,7},{7,6},{8,9},{9,8},{10,11... | collective-permute-start | bytes 12296 | tf_op jit(solution)/shard_map/ppermute | solution.py:153
  251.2 2.5 collective-permute-start.37
  255.1 4.7 %collective-permute-start.38 = (f32[2,128]{0,1:T(8,128)S(1)}, f32[2,128]{0,1:T(8,128)S(1)}, u32[]{:S(2)}, u32[]{:S(2)}) collective-permute-start(f32[2,128]{0,1:T(8,128)S(1)} %broadcast_in_dim.20), channel_id=1, source_target_pairs={{0,1},{1,0},{2,3},{3,2},{4,5},{5,4},{6,7},{7,6},{8,9},{9,8},{10,11... | collective-permute-start | bytes 3080 | tf_op jit(solution)/shard_map/ppermute | solution.py:153
  261.3 5.0 %collective-permute-start.31 = (bf16[256,1024]{1,0:T(8,128)(2,1)S(1)}, bf16[256,1024]{1,0:T(8,128)(2,1)S(1)}, u32[]{:S(2)}, u32[]{:S(2)}) collective-permute-start(bf16[256,1024]{1,0:T(8,128)(2,1)S(1)} %add_convert_fusion.2), channel_id=1, source_target_pairs={{1,24},{5,28},{9,17},{13,21},{17,10},{21,14},{25,3},{29,7}} | collective-permute-start | bytes 1572872 | tf_op jit(solution)/shard_map/ppermute | solution.py:153
  268.9 4.8 %collective-permute-done.39 = f32[2,128]{0,1:T(8,128)S(1)} collective-permute-done((f32[2,128]{0,1:T(8,128)S(1)}, f32[2,128]{0,1:T(8,128)S(1)}, u32[]{:S(2)}, u32[]{:S(2)}) %collective-permute-start.39) | collective-permute-done | bytes 1056 | tf_op jit(solution)/shard_map/ppermute | solution.py:153
  273.9 4.7 %multiply_multiply_fusion = (f32[512,1280]{1,0:T(8,128)}, f32[512,1280]{1,0:T(8,128)}) fusion(f32[1280]{0:T(1024)S(1)} %get-tuple-element.129, f32[512]{0:T(512)S(1)} %bitcast.52, f32[512,768]{1,0:T(8,128)S(1)} %add_multiply_fusion.1, f32[512,512]{1,0:T(8,128)S(1)} %add_multiply_fusion.2, f32[1280]{0:T(1024)S(1)} %get-tuple-element.130, ...), kind=kLoop, calls=%fused_computation.15 | loop fusion | flops 3276800 | bytes 10500096 | tf_op jit(solution)/shard_map/mul | solution.py:394
  (188 shorter events, 89.7 us)
Async XLA Ops:
  2.3 16.8 %collective-permute-start = (bf16[128,1024]{1,0:T(8,128)(2,1)S(1)}, bf16[128,1024]{1,0:T(8,128)(2,1)S(1)}, u32[]{:S(2)}, u32[]{:S(2)}) collective-permute-start(bf16[128,1024]{1,0:T(8,128)(2,1)S(1)} %get-tuple-element.142), channel_id=1, source_target_pairs={{0,8},{1,9},{2,10},{3,11},{4,12},{5,13},{6,14},{7,15},{8,0},{9,1},... | collective-permute-start | bytes 786440 | tf_op jit(solution)/shard_map/ppermute | solution.py:153
  4.5 14.7 %collective-permute-start.1 = (bf16[128,1024]{1,0:T(8,128)(2,1)S(1)}, bf16[128,1024]{1,0:T(8,128)(2,1)S(1)}, u32[]{:S(2)}, u32[]{:S(2)}) collective-permute-start(bf16[128,1024]{1,0:T(8,128)(2,1)S(1)} %get-tuple-element.141), channel_id=1, source_target_pairs={{0,16},{1,17},{2,18},{3,19},{4,20},{5,21},{6,22},{7,23},{8,24},{9,... | collective-permute-start | bytes 786440 | tf_op jit(solution)/shard_map/ppermute | solution.py:153
  6.8 16.9 %collective-permute-start.2 = (bf16[128,1024]{1,0:T(8,128)(2,1)S(1)}, bf16[128,1024]{1,0:T(8,128)(2,1)S(1)}, u32[]{:S(2)}, u32[]{:S(2)}) collective-permute-start(bf16[128,1024]{1,0:T(8,128)(2,1)S(1)} %get-tuple-element.140), channel_id=1, source_target_pairs={{0,24},{1,25},{2,26},{3,27},{4,28},{5,29},{6,30},{7,31},{8,16},{9,... | collective-permute-start | bytes 786440 | tf_op jit(solution)/shard_map/ppermute | solution.py:153
  23.7 33.4 %collective-permute-start.3 = (bf16[512,1280]{1,0:T(8,128)(2,1)}, bf16[512,1280]{1,0:T(8,128)(2,1)}, u32[]{:S(2)}, u32[]{:S(2)}) collective-permute-start(bf16[512,1280]{1,0:T(8,128)(2,1)} %shard_map.137), channel_id=1, source_target_pairs={{0,8},{1,9},{2,10},{3,11},{4,12},{5,13},{6,14},{7,15},{8,0},{9,1},... | collective-permute-start | bytes 3932168 | tf_op jit(solution)/shard_map/ppermute | solution.py:153
  29.5 27.6 %collective-permute-start.4 = (bf16[512,1280]{1,0:T(8,128)(2,1)}, bf16[512,1280]{1,0:T(8,128)(2,1)}, u32[]{:S(2)}, u32[]{:S(2)}) collective-permute-start(bf16[512,1280]{1,0:T(8,128)(2,1)} %shard_map.137), channel_id=1, source_target_pairs={{8,16},{9,17},{10,18},{11,19},{12,20},{13,21},{14,22},{15,23},{16,... | collective-permute-start | bytes 3932168 | tf_op jit(solution)/shard_map/ppermute | solution.py:153
  31.2 28.5 %collective-permute-start.5 = (bf16[512,1280]{1,0:T(8,128)(2,1)}, bf16[512,1280]{1,0:T(8,128)(2,1)}, u32[]{:S(2)}, u32[]{:S(2)}) collective-permute-start(bf16[512,1280]{1,0:T(8,128)(2,1)} %param.16), channel_id=1, source_target_pairs={{0,4},{1,5},{2,6},{3,7},{4,0},{5,1},{6,2},{7,3},{8,12},{9,13},{10,... | collective-permute-start | bytes 3932168 | tf_op jit(solution)/shard_map/ppermute | solution.py:153
  32.4 52.8 %collective-permute-start.8 = (bf16[512,1280]{1,0:T(8,128)(2,1)S(1)}, bf16[512,1280]{1,0:T(8,128)(2,1)}, u32[]{:S(2)}, u32[]{:S(2)}) collective-permute-start(bf16[512,1280]{1,0:T(8,128)(2,1)S(1)} %copy-done.8), channel_id=1, source_target_pairs={{0,8},{1,9},{2,10},{3,11},{4,12},{5,13},{6,14},{7,15},{8,0},{9,1},... | collective-permute-start | bytes 3932168 | tf_op jit(solution)/shard_map/ppermute | solution.py:153
  34.0 52.9 %collective-permute-start.9 = (bf16[512,1280]{1,0:T(8,128)(2,1)S(1)}, bf16[512,1280]{1,0:T(8,128)(2,1)S(1)}, u32[]{:S(2)}, u32[]{:S(2)}) collective-permute-start(bf16[512,1280]{1,0:T(8,128)(2,1)S(1)} %copy-done.8), channel_id=1, source_target_pairs={{8,16},{9,17},{10,18},{11,19},{12,20},{13,21},{14,22},{15,23},{16,... | collective-permute-start | bytes 3932168 | tf_op jit(solution)/shard_map/ppermute | solution.py:153
  59.7 27.6 %collective-permute-start.10 = (bf16[512,1280]{1,0:T(8,128)(2,1)}, bf16[512,1280]{1,0:T(8,128)(2,1)}, u32[]{:S(2)}, u32[]{:S(2)}) collective-permute-start(bf16[512,1280]{1,0:T(8,128)(2,1)} %param.17), channel_id=1, source_target_pairs={{0,4},{1,5},{2,6},{3,7},{4,0},{5,1},{6,2},{7,3},{8,12},{9,13},{10,... | collective-permute-start | bytes 3932168 | tf_op jit(solution)/shard_map/ppermute | solution.py:153
  60.9 26.0 %collective-permute-start.11 = (bf16[3,128,1024]{2,1,0:T(8,128)(2,1)S(1)}, bf16[3,128,1024]{2,1,0:T(8,128)(2,1)S(1)}, u32[]{:S(2)}, u32[]{:S(2)}) collective-permute-start(bf16[3,128,1024]{2,1,0:T(8,128)(2,1)S(1)} %pad_maximum_fusion.9), channel_id=1, source_target_pairs={{0,2},{1,3},{2,0},{3,1},{4,6},{5,7},{6,4},{7,5},{8,10},{9,11},{10,... | collective-permute-start | bytes 2359304 | tf_op jit(solution)/shard_map/ppermute | solution.py:153
  63.8 49.4 %collective-permute-start.6 = (bf16[512,1280]{1,0:T(8,128)(2,1)}, bf16[512,1280]{1,0:T(8,128)(2,1)}, u32[]{:S(2)}, u32[]{:S(2)}) collective-permute-start(bf16[512,1280]{1,0:T(8,128)(2,1)} %collective-permute-done.4), channel_id=1, source_target_pairs={{8,0},{9,1},{10,2},{11,3},{12,4},{13,5},{14,6},{15,7},{16,24},{17,... | collective-permute-start | bytes 3932168 | tf_op jit(solution)/shard_map/ppermute | solution.py:153
  85.2 28.1 %collective-permute-start.7 = (bf16[512,1280]{1,0:T(8,128)(2,1)}, bf16[512,1280]{1,0:T(8,128)(2,1)}, u32[]{:S(2)}, u32[]{:S(2)}) collective-permute-start(bf16[512,1280]{1,0:T(8,128)(2,1)} %collective-permute-done.3), channel_id=1, source_target_pairs={{8,16},{9,17},{10,18},{11,19},{12,20},{13,21},{14,22},{15,23},{16,... | collective-permute-start | bytes 3932168 | tf_op jit(solution)/shard_map/ppermute | solution.py:153
  87.4 25.9 %collective-permute-start.12 = (bf16[2,3,128,1024]{3,2,1,0:T(8,128)(2,1)S(1)}, bf16[2,3,128,1024]{3,2,1,0:T(8,128)(2,1)}, u32[]{:S(2)}, u32[]{:S(2)}) collective-permute-start(bf16[2,3,128,1024]{3,2,1,0:T(8,128)(2,1)S(1)} %pad_maximum_fusion.7), channel_id=1, source_target_pairs={{0,1},{1,0},{2,3},{3,2},{4,5},{5,4},{6,7},{7,6},{8,9},{9,8},{10,11... | collective-permute-start | bytes 4718600 | tf_op jit(solution)/shard_map/ppermute | solution.py:153
  107.7 25.0 %collective-permute-start.15 = (bf16[512,1280]{1,0:T(8,128)(2,1)}, bf16[512,1280]{1,0:T(8,128)(2,1)S(1)}, u32[]{:S(2)}, u32[]{:S(2)}) collective-permute-start(bf16[512,1280]{1,0:T(8,128)(2,1)} %collective-permute-done.8), channel_id=1, source_target_pairs={{8,16},{9,17},{10,18},{11,19},{12,20},{13,21},{14,22},{15,23},{16,... | collective-permute-start | bytes 3932168 | tf_op jit(solution)/shard_map/ppermute | solution.py:153
  115.0 17.5 %collective-permute-start.17 = (bf16[256,1024]{1,0:T(8,128)(2,1)S(1)}, bf16[256,1024]{1,0:T(8,128)(2,1)S(1)}, u32[]{:S(2)}, u32[]{:S(2)}) collective-permute-start(bf16[256,1024]{1,0:T(8,128)(2,1)S(1)} %dynamic-slice_convert_fusion.2), channel_id=1, source_target_pairs={{0,2},{1,3},{2,0},{3,1},{4,6},{5,7},{6,4},{7,5},{8,10},{9,11},{10,... | collective-permute-start | bytes 1572872 | tf_op jit(solution)/shard_map/ppermute | solution.py:153
  116.3 26.1 %collective-permute-start.16 = (bf16[512,1280]{1,0:T(8,128)(2,1)}, bf16[512,1280]{1,0:T(8,128)(2,1)S(1)}, u32[]{:S(2)}, u32[]{:S(2)}) collective-permute-start(bf16[512,1280]{1,0:T(8,128)(2,1)} %collective-permute-done.7), channel_id=1, source_target_pairs={{8,0},{9,1},{10,2},{11,3},{12,4},{13,5},{14,6},{15,7},{16,24},{17,... | collective-permute-start | bytes 3932168 | tf_op jit(solution)/shard_map/ppermute | solution.py:153
  119.6 50.9 %collective-permute-start.14 = (bf16[512,1280]{1,0:T(8,128)(2,1)S(1)}, bf16[512,1280]{1,0:T(8,128)(2,1)S(1)}, u32[]{:S(2)}, u32[]{:S(2)}) collective-permute-start(bf16[512,1280]{1,0:T(8,128)(2,1)S(1)} %collective-permute-done.9), channel_id=1, source_target_pairs={{8,0},{9,1},{10,2},{11,3},{12,4},{13,5},{14,6},{15,7},{16,24},{17,... | collective-permute-start | bytes 3932168 | tf_op jit(solution)/shard_map/ppermute | solution.py:153
  142.4 39.3 %collective-permute-start.18 = (bf16[256,1024]{1,0:T(8,128)(2,1)S(1)}, bf16[256,1024]{1,0:T(8,128)(2,1)S(1)}, u32[]{:S(2)}, u32[]{:S(2)}) collective-permute-start(bf16[256,1024]{1,0:T(8,128)(2,1)S(1)} %add_convert_fusion.5), channel_id=1, source_target_pairs={{0,0},{1,8},{4,4},{5,12},{8,9},{9,1},{12,13},{13,5},{16,18},{17,26... | collective-permute-start | bytes 1572872 | tf_op jit(solution)/shard_map/ppermute | solution.py:153
  158.9 22.8 %collective-permute-start.19 = (bf16[256,1024]{1,0:T(8,128)(2,1)S(1)}, bf16[256,1024]{1,0:T(8,128)(2,1)S(1)}, u32[]{:S(2)}, u32[]{:S(2)}) collective-permute-start(bf16[256,1024]{1,0:T(8,128)(2,1)S(1)} %add_convert_fusion.5), channel_id=1, source_target_pairs={{2,0},{3,8},{6,4},{7,12},{10,9},{11,1},{14,13},{15,5},{18,18},{19,... | collective-permute-start | bytes 1572872 | tf_op jit(solution)/shard_map/ppermute | solution.py:153
  163.1 37.2 %collective-permute-start.22 = (bf16[512,1280]{1,0:T(8,128)(2,1)S(1)}, bf16[512,1280]{1,0:T(8,128)(2,1)S(1)}, u32[]{:S(2)}, u32[]{:S(2)}) collective-permute-start(bf16[512,1280]{1,0:T(8,128)(2,1)S(1)} %add_convert_fusion), channel_id=1, source_target_pairs={{0,4},{1,5},{2,6},{3,7},{4,0},{5,1},{6,2},{7,3},{8,12},{9,13},{10,... | collective-permute-start | bytes 3932168 | tf_op jit(solution)/shard_map/ppermute | solution.py:153
  164.4 35.9 %collective-permute-start.21 = (bf16[512,512]{1,0:T(8,128)(2,1)S(1)}, bf16[512,512]{1,0:T(8,128)(2,1)S(1)}, u32[]{:S(2)}, u32[]{:S(2)}) collective-permute-start(bf16[512,512]{1,0:T(8,128)(2,1)S(1)} %slice.129), channel_id=1, source_target_pairs={{8,0},{9,1},{10,2},{11,3},{12,4},{13,5},{14,6},{15,7},{16,24},{17,... | collective-permute-start | bytes 1572872 | tf_op jit(solution)/shard_map/ppermute | solution.py:153
  185.4 15.0 %collective-permute-start.20 = (bf16[512,1024]{1,0:T(8,128)(2,1)S(1)}, bf16[512,1024]{1,0:T(8,128)(2,1)S(1)}, u32[]{:S(2)}, u32[]{:S(2)}) collective-permute-start(bf16[512,1024]{1,0:T(8,128)(2,1)S(1)} %get-tuple-element.149), channel_id=1, source_target_pairs={{1,0},{3,2},{5,4},{7,6},{9,8},{11,10},{13,12},{15,14},{17,16},{19,... | collective-permute-start | bytes 3145736 | tf_op jit(solution)/shard_map/ppermute | solution.py:153
  191.5 21.2 %collective-permute-start.24 = (bf16[512,768]{1,0:T(8,128)(2,1)S(1)}, bf16[512,768]{1,0:T(8,128)(2,1)S(1)}, u32[]{:S(2)}, u32[]{:S(2)}) collective-permute-start(bf16[512,768]{1,0:T(8,128)(2,1)S(1)} %slice.134), channel_id=1, source_target_pairs={{8,0},{9,1},{10,2},{11,3},{12,4},{13,5},{14,6},{15,7},{16,24},{17,... | collective-permute-start | bytes 2359304 | tf_op jit(solution)/shard_map/ppermute | solution.py:153
  200.7 12.0 %collective-permute-start.25 = (bf16[256,1024]{1,0:T(8,128)(2,1)S(1)}, bf16[256,1024]{1,0:T(8,128)(2,1)S(1)}, u32[]{:S(2)}, u32[]{:S(2)}) collective-permute-start(bf16[256,1024]{1,0:T(8,128)(2,1)S(1)} %dynamic-slice_convert_fusion.1), channel_id=1, source_target_pairs={{0,2},{2,0},{4,6},{6,4},{8,10},{10,8},{12,14},{14,12},{16,18},{18,... | collective-permute-start | bytes 1572872 | tf_op jit(solution)/shard_map/ppermute | solution.py:153
  202.7 12.4 %collective-permute-start.23 = (bf16[512,512]{1,0:T(8,128)(2,1)S(1)}, bf16[512,512]{1,0:T(8,128)(2,1)S(1)}, u32[]{:S(2)}, u32[]{:S(2)}) collective-permute-start(bf16[512,512]{1,0:T(8,128)(2,1)S(1)} %add_convert_fusion.4), channel_id=1, source_target_pairs={{0,4},{1,5},{2,6},{3,7},{4,0},{5,1},{6,2},{7,3},{8,12},{9,13},{10,... | collective-permute-start | bytes 1572872 | tf_op jit(solution)/shard_map/ppermute | solution.py:153
  218.7 7.8 %collective-permute-start.29 = (bf16[256,1024]{1,0:T(8,128)(2,1)S(1)}, bf16[256,1024]{1,0:T(8,128)(2,1)S(1)}, u32[]{:S(2)}, u32[]{:S(2)}) collective-permute-start(bf16[256,1024]{1,0:T(8,128)(2,1)S(1)} %add_convert_fusion.3), channel_id=1, source_target_pairs={{0,16},{4,20},{8,25},{12,29},{16,2},{20,6},{24,11},{28,15}} | collective-permute-start | bytes 1572872 | tf_op jit(solution)/shard_map/ppermute | solution.py:153
  219.4 7.1 %collective-permute-start.30 = (bf16[256,1024]{1,0:T(8,128)(2,1)S(1)}, bf16[256,1024]{1,0:T(8,128)(2,1)S(1)}, u32[]{:S(2)}, u32[]{:S(2)}) collective-permute-start(bf16[256,1024]{1,0:T(8,128)(2,1)S(1)} %add_convert_fusion.3), channel_id=1, source_target_pairs={{2,16},{6,20},{10,25},{14,29},{18,2},{22,6},{26,11},{30,15}} | collective-permute-start | bytes 1572872 | tf_op jit(solution)/shard_map/ppermute | solution.py:153
  220.8 12.4 %collective-permute-start.28 = (bf16[512,768]{1,0:T(8,128)(2,1)S(1)}, bf16[512,768]{1,0:T(8,128)(2,1)S(1)}, u32[]{:S(2)}, u32[]{:S(2)}) collective-permute-start(bf16[512,768]{1,0:T(8,128)(2,1)S(1)} %add_convert_fusion.1), channel_id=1, source_target_pairs={{0,4},{1,5},{2,6},{3,7},{4,0},{5,1},{6,2},{7,3},{8,12},{9,13},{10,... | collective-permute-start | bytes 2359304 | tf_op jit(solution)/shard_map/ppermute | solution.py:153
  224.2 13.6 %collective-permute-start.27 = (bf16[256,1024]{1,0:T(8,128)(2,1)S(1)}, bf16[256,1024]{1,0:T(8,128)(2,1)}, u32[]{:S(2)}, u32[]{:S(2)}) collective-permute-start(bf16[256,1024]{1,0:T(8,128)(2,1)S(1)} %dynamic-slice_convert_fusion), channel_id=1, source_target_pairs={{1,3},{3,1},{5,7},{7,5},{9,11},{11,9},{13,15},{15,13},{17,19},{19,... | collective-permute-start | bytes 1572872 | tf_op jit(solution)/shard_map/ppermute | solution.py:153
  255.1 12.0 %collective-permute-start.38 = (f32[2,128]{0,1:T(8,128)S(1)}, f32[2,128]{0,1:T(8,128)S(1)}, u32[]{:S(2)}, u32[]{:S(2)}) collective-permute-start(f32[2,128]{0,1:T(8,128)S(1)} %broadcast_in_dim.20), channel_id=1, source_target_pairs={{0,1},{1,0},{2,3},{3,2},{4,5},{5,4},{6,7},{7,6},{8,9},{9,8},{10,11... | collective-permute-start | bytes 3080 | tf_op jit(solution)/shard_map/ppermute | solution.py:153
  261.3 17.2 %collective-permute-start.31 = (bf16[256,1024]{1,0:T(8,128)(2,1)S(1)}, bf16[256,1024]{1,0:T(8,128)(2,1)S(1)}, u32[]{:S(2)}, u32[]{:S(2)}) collective-permute-start(bf16[256,1024]{1,0:T(8,128)(2,1)S(1)} %add_convert_fusion.2), channel_id=1, source_target_pairs={{1,24},{5,28},{9,17},{13,21},{17,10},{21,14},{25,3},{29,7}} | collective-permute-start | bytes 1572872 | tf_op jit(solution)/shard_map/ppermute | solution.py:153
  266.3 12.3 %collective-permute-start.32 = (bf16[256,1024]{1,0:T(8,128)(2,1)S(1)}, bf16[256,1024]{1,0:T(8,128)(2,1)S(1)}, u32[]{:S(2)}, u32[]{:S(2)}) collective-permute-start(bf16[256,1024]{1,0:T(8,128)(2,1)S(1)} %add_convert_fusion.2), channel_id=1, source_target_pairs={{3,24},{7,28},{11,17},{15,21},{19,10},{23,14},{27,3},{31,7}} | collective-permute-start | bytes 1572872 | tf_op jit(solution)/shard_map/ppermute | solution.py:153
  (35 other events, 355.8 us)

commit v4 on v3

--- a/solution.py
+++ b/solution.py
@@ -295,10 +295,7 @@
         g_far, g_near_over, pieces, pieces_c, early_keep, early_recv, u_over
     )
 
-    early_sum = early_keep + early_recv.astype(f32)
     g_farthest = send(g_near_over, OUTWARD)
-    early_keep, early_away = over_y(early_sum)
-    early_recv = send(early_away, FLIP_Y)
     u_far = send(u_over, OUTWARD)
     far = jnp.zeros((3, model_size, piece_rows, plane), bf16)
     for part, place in ((pieces[0], m), (pieces_c[0], m ^ 1), (pieces[1], m ^ 2), (pieces_c[1], m ^ 3)):
@@ -308,6 +305,10 @@
     near_tokens = 3 * tokens
     inputs_keep = lax.dynamic_slice(inputs, (0, x * rows), (4 * tokens, rows))
     inputs_away = lax.dynamic_slice(inputs, (0, (1 - x) * rows), (4 * tokens, rows))
+
+    inputs, early_keep, early_recv = tie(inputs, early_keep, early_recv)
+    early_keep, early_away = over_y(early_keep + early_recv.astype(f32))
+    early_recv = send(early_away, FLIP_Y)
 
     def near_products(block):
         return dot_first(inputs_away[:near_tokens], block), dot_first(inputs_keep[:near_tokens], block)

time: 282 us -> 282 us (level)
  no operation moved by 1% of the time
where the time goes in v4:
time: 282 us; the launch traced here: 281 us
  waiting for transfers between devices  104 us (37%)
  starting transfers between devices  88.3 us (31%)
  matrix products  33.4 us (12%)
  other arithmetic  23.1 us (8%)
  local copies, waits for them, and re-layouts  19.3 us (7%)
  Pallas kernels  10.8 us (4%)
    ppermute x40, waiting for transfers between devices, send(): return lax.ppermute(value, AXES, permutation)  104 us
    ppermute x40, starting transfers between devices, send(): return lax.ppermute(value, AXES, permutation)  88.3 us
    dot_general x10, matrix products, dot_first(): lax.dot_general(a, b, (((0,), (0,)), ((), ())), preferred_element_type=f32)  18.4 us
    dot_general x7, matrix products, dot_last(): lax.dot_general(a, b, (((1,), (1,)), ((), ())), preferred_element_type=f32)  15 us
    pallas_call x2, Pallas kernels, front(): pl.pallas_call(kernel, grid=(tokens // rows,), in_specs=[pl.BlockSpec((ro...  10.8 us
  transfers between devices with their start and end apart: 40, of which 19 were waited for; matrix products, arithmetic and copies ran while one was open for 23% of the time, Pallas kernels for 4%

profile of v4, /device:TPU:1, one launch (start us, length us, event | category | flops | bytes accessed | tf_op | source)
XLA Modules:
  0.0 280.7 jit_solution(3902920396701317639)
XLA Ops:
  2.3 2.2 collective-permute-start
  4.5 2.3 collective-permute-start.1
  8.4 4.4 %shard_map.138 = bf16[512,1280]{1,0:T(8,128)(2,1)} custom-call(s32[512,1]{1,0:T(8,128)} %copy.15.ids_ref, f32[1,64]{1,0:T(1,128)} %bitcast.57, bf16[512,1280]{1,0:T(8,128)(2,1)} %cot_ref.3, bf16[512,1280]{1,0:T(8,128)(2,1)} %gate_ref.3), custom_call_target="tpu_custom_call" | custom-call | flops 655360 | bytes 655360 | tf_op jit(solution)/shard_map/pallas_call | solution.py:181
  12.8 6.4 %shard_map.137 = bf16[512,1280]{1,0:T(8,128)(2,1)} custom-call(s32[512,1]{1,0:T(8,128)} %copy.15.ids_ref, f32[1,64]{1,0:T(1,128)} %bitcast.58, bf16[512,1280]{1,0:T(8,128)(2,1)} %cot_ref.3, bf16[512,1280]{1,0:T(8,128)(2,1)} %gate_ref.3, bf16[512,1280]{1,0:T(8,128)(2,1)} %up_ref.1), custom_call_target="tpu_custom_call" | custom-call | flops 655360 | bytes 655360 | tf_op jit(solution)/shard_map/pallas_call | solution.py:181
  19.2 4.5 %collective-permute-done.2 = bf16[128,1024]{1,0:T(8,128)(2,1)S(1)} collective-permute-done((bf16[128,1024]{1,0:T(8,128)(2,1)S(1)}, bf16[128,1024]{1,0:T(8,128)(2,1)S(1)}, u32[]{:S(2)}, u32[]{:S(2)}) %collective-permute-start.2) | collective-permute-done | bytes 262176 | tf_op jit(solution)/shard_map/ppermute | solution.py:153
  23.7 5.8 %collective-permute-start.3 = (bf16[512,1280]{1,0:T(8,128)(2,1)}, bf16[512,1280]{1,0:T(8,128)(2,1)}, u32[]{:S(2)}, u32[]{:S(2)}) collective-permute-start(bf16[512,1280]{1,0:T(8,128)(2,1)} %shard_map.137), channel_id=1, source_target_pairs={{0,8},{1,9},{2,10},{3,11},{4,12},{5,13},{6,14},{7,15},{8,0},{9,1},... | collective-permute-start | bytes 3932168 | tf_op jit(solution)/shard_map/ppermute | solution.py:153
  35.9 21.1 %collective-permute-done.3 = bf16[512,1280]{1,0:T(8,128)(2,1)} collective-permute-done((bf16[512,1280]{1,0:T(8,128)(2,1)}, bf16[512,1280]{1,0:T(8,128)(2,1)}, u32[]{:S(2)}, u32[]{:S(2)}) %collective-permute-start.3) | collective-permute-done | bytes 1310752 | tf_op jit(solution)/shard_map/ppermute | solution.py:153
  57.1 2.6 collective-permute-done.5
  67.0 18.2 %collective-permute-done.8 = bf16[512,1280]{1,0:T(8,128)(2,1)} collective-permute-done((bf16[512,1280]{1,0:T(8,128)(2,1)S(1)}, bf16[512,1280]{1,0:T(8,128)(2,1)}, u32[]{:S(2)}, u32[]{:S(2)}) %collective-permute-start.8) | collective-permute-done | bytes 1310752 | tf_op jit(solution)/shard_map/ppermute | solution.py:153
  87.4 4.2 %collective-permute-start.12 = (bf16[2,3,128,1024]{3,2,1,0:T(8,128)(2,1)S(1)}, bf16[2,3,128,1024]{3,2,1,0:T(8,128)(2,1)}, u32[]{:S(2)}, u32[]{:S(2)}) collective-permute-start(bf16[2,3,128,1024]{3,2,1,0:T(8,128)(2,1)S(1)} %pad_maximum_fusion.8), channel_id=1, source_target_pairs={{0,1},{1,0},{2,3},{3,2},{4,5},{5,4},{6,7},{7,6},{8,9},{9,8},{10,11... | collective-permute-start | bytes 4718600 | tf_op jit(solution)/shard_map/ppermute | solution.py:153
  94.6 4.3 %fusion.4 = f32[1024,1024]{1,0:T(8,128)S(1)} fusion(bf16[1024,1280]{1,0:T(8,128)(2,1)S(1)} %constant_dynamic-update-slice_fusion, bf16[512,1280]{1,0:T(8,128)(2,1)} %collective-permute-done.8, bf16[512,1280]{1,0:T(8,128)(2,1)S(1)} %copy-done.9), kind=kOutput, calls=%fused_computation.11 | convolution fusion | flops 2689597440 | bytes 9437184 | tf_op jit(solution)/shard_map/dot_general | solution.py:202
  98.9 4.3 %fusion.10 = f32[1024,1024]{1,0:T(8,128)S(1)} fusion(f32[1024,1024]{1,0:T(8,128)S(1)} %fusion.4, bf16[1024,1280]{1,0:T(8,128)(2,1)S(1)} %constant_dynamic-update-slice_fusion.2, bf16[512,1280]{1,0:T(8,128)(2,1)} %collective-permute-done.3, bf16[512,1280]{1,0:T(8,128)(2,1)S(1)} %copy-done.12), kind=kOutput, calls=%fused_computation.33 | convolution fusion | flops 2690646016 | bytes 13631488 | tf_op jit(solution)/shard_map/dot_general | solution.py:202
  108.5 2.6 slice_select_fusion
  125.3 3.6 %fusion.15 = f32[512,1280]{1,0:T(8,128)S(1)} fusion(bf16[512,1280]{1,0:T(8,128)(2,1)S(1)} %add.190, bf16[512,1280]{1,0:T(8,128)(2,1)} %collective-permute-done.3, bf16[512,1280]{1,0:T(8,128)(2,1)S(1)} %copy-done.13, bf16[2048,512]{1,0:T(8,128)(2,1)S(1)} %get-tuple-element.96), kind=kOutput, calls=%fused_computation.36 | convolution fusion | flops 2025062400 | bytes 8126464 | tf_op jit(solution)/shard_map/dot_general | solution.py:198
  128.9 3.6 %fusion.16 = f32[512,1280]{1,0:T(8,128)S(1)} fusion(bf16[512,1280]{1,0:T(8,128)(2,1)S(1)} %add.190, bf16[512,1280]{1,0:T(8,128)(2,1)} %collective-permute-done.3, bf16[512,1280]{1,0:T(8,128)(2,1)S(1)} %copy-done.13, bf16[2048,512]{1,0:T(8,128)(2,1)S(1)} %get-tuple-element.101), kind=kOutput, calls=%fused_computation.37 | convolution fusion | flops 2025062400 | bytes 8126464 | tf_op jit(solution)/shard_map/dot_general | solution.py:198
  132.7 9.7 %collective-permute-done.16 = bf16[512,1280]{1,0:T(8,128)(2,1)S(1)} collective-permute-done((bf16[512,1280]{1,0:T(8,128)(2,1)}, bf16[512,1280]{1,0:T(8,128)(2,1)S(1)}, u32[]{:S(2)}, u32[]{:S(2)}) %collective-permute-start.16) | collective-permute-done | bytes 1310752 | tf_op jit(solution)/shard_map/ppermute | solution.py:153
  142.4 16.5 %collective-permute-start.18 = (bf16[256,1024]{1,0:T(8,128)(2,1)S(1)}, bf16[256,1024]{1,0:T(8,128)(2,1)S(1)}, u32[]{:S(2)}, u32[]{:S(2)}) collective-permute-start(bf16[256,1024]{1,0:T(8,128)(2,1)S(1)} %add_convert_fusion.5), channel_id=1, source_target_pairs={{0,0},{1,8},{4,4},{5,12},{8,9},{9,1},{12,13},{13,5},{16,18},{17,26... | collective-permute-start | bytes 1572872 | tf_op jit(solution)/shard_map/ppermute | solution.py:153
  167.0 3.5 %collective-permute-done.14 = bf16[512,1280]{1,0:T(8,128)(2,1)S(1)} collective-permute-done((bf16[512,1280]{1,0:T(8,128)(2,1)S(1)}, bf16[512,1280]{1,0:T(8,128)(2,1)S(1)}, u32[]{:S(2)}, u32[]{:S(2)}) %collective-permute-start.14) | collective-permute-done | bytes 1310752 | tf_op jit(solution)/shard_map/ppermute | solution.py:153
  170.5 11.2 %collective-permute-done.18 = bf16[256,1024]{1,0:T(8,128)(2,1)S(1)} collective-permute-done((bf16[256,1024]{1,0:T(8,128)(2,1)S(1)}, bf16[256,1024]{1,0:T(8,128)(2,1)S(1)}, u32[]{:S(2)}, u32[]{:S(2)}) %collective-permute-start.18) | collective-permute-done | bytes 524320 | tf_op jit(solution)/shard_map/ppermute | solution.py:153
  185.4 6.1 %collective-permute-start.20 = (bf16[512,1024]{1,0:T(8,128)(2,1)S(1)}, bf16[512,1024]{1,0:T(8,128)(2,1)S(1)}, u32[]{:S(2)}, u32[]{:S(2)}) collective-permute-start(bf16[512,1024]{1,0:T(8,128)(2,1)S(1)} %get-tuple-element.153), channel_id=1, source_target_pairs={{1,0},{3,2},{5,4},{7,6},{9,8},{11,10},{13,12},{15,14},{17,16},{19,... | collective-permute-start | bytes 3145736 | tf_op jit(solution)/shard_map/ppermute | solution.py:153
  193.1 3.6 %fusion.13 = f32[512,1280]{1,0:T(8,128)S(1)} fusion(bf16[512,1280]{1,0:T(8,128)(2,1)S(1)} %add.197, bf16[512,1280]{1,0:T(8,128)(2,1)} %collective-permute-done.8, bf16[512,1280]{1,0:T(8,128)(2,1)S(1)} %copy-done.10, bf16[2048,512]{1,0:T(8,128)(2,1)S(1)} %get-tuple-element.96), kind=kOutput, calls=%fused_computation.34 | convolution fusion | flops 2025062400 | bytes 8126464 | tf_op jit(solution)/shard_map/dot_general | solution.py:198
  196.7 3.6 %fusion.14 = f32[512,1280]{1,0:T(8,128)S(1)} fusion(bf16[512,1280]{1,0:T(8,128)(2,1)S(1)} %add.197, bf16[512,1280]{1,0:T(8,128)(2,1)} %collective-permute-done.8, bf16[512,1280]{1,0:T(8,128)(2,1)S(1)} %copy-done.10, bf16[2048,512]{1,0:T(8,128)(2,1)S(1)} %get-tuple-element.101), kind=kOutput, calls=%fused_computation.35 | convolution fusion | flops 2025062400 | bytes 8126464 | tf_op jit(solution)/shard_map/dot_general | solution.py:198
  206.1 6.7 %collective-permute-done.24 = bf16[512,768]{1,0:T(8,128)(2,1)S(1)} collective-permute-done((bf16[512,768]{1,0:T(8,128)(2,1)S(1)}, bf16[512,768]{1,0:T(8,128)(2,1)S(1)}, u32[]{:S(2)}, u32[]{:S(2)}) %collective-permute-start.24) | collective-permute-done | bytes 786464 | tf_op jit(solution)/shard_map/ppermute | solution.py:153
  212.8 2.3 collective-permute-done.23
  226.6 6.6 %collective-permute-done.28 = bf16[512,768]{1,0:T(8,128)(2,1)S(1)} collective-permute-done((bf16[512,768]{1,0:T(8,128)(2,1)S(1)}, bf16[512,768]{1,0:T(8,128)(2,1)S(1)}, u32[]{:S(2)}, u32[]{:S(2)}) %collective-permute-start.28) | collective-permute-done | bytes 786464 | tf_op jit(solution)/shard_map/ppermute | solution.py:153
  233.2 4.6 %collective-permute-done.27 = bf16[256,1024]{1,0:T(8,128)(2,1)} collective-permute-done((bf16[256,1024]{1,0:T(8,128)(2,1)S(1)}, bf16[256,1024]{1,0:T(8,128)(2,1)}, u32[]{:S(2)}, u32[]{:S(2)}) %collective-permute-start.27) | collective-permute-done | bytes 524320 | tf_op jit(solution)/shard_map/ppermute | solution.py:153
  238.2 3.1 %collective-permute-start.33 = (f32[2,512]{1,0:T(2,128)S(1)}, f32[2,512]{1,0:T(2,128)S(1)}, u32[]{:S(2)}, u32[]{:S(2)}) collective-permute-start(f32[2,512]{1,0:T(2,128)S(1)} %pad_maximum_fusion.12), channel_id=1, source_target_pairs={{0,1},{1,0},{2,3},{3,2},{4,5},{5,4},{6,7},{7,6},{8,9},{9,8},{10,11... | collective-permute-start | bytes 12296 | tf_op jit(solution)/shard_map/ppermute | solution.py:153
  251.2 2.5 collective-permute-start.37
  255.1 4.7 %collective-permute-start.38 = (f32[2,128]{0,1:T(8,128)S(1)}, f32[2,128]{0,1:T(8,128)S(1)}, u32[]{:S(2)}, u32[]{:S(2)}) collective-permute-start(f32[2,128]{0,1:T(8,128)S(1)} %broadcast_in_dim.20), channel_id=1, source_target_pairs={{0,1},{1,0},{2,3},{3,2},{4,5},{5,4},{6,7},{7,6},{8,9},{9,8},{10,11... | collective-permute-start | bytes 3080 | tf_op jit(solution)/shard_map/ppermute | solution.py:153
  261.3 5.0 %collective-permute-start.31 = (bf16[256,1024]{1,0:T(8,128)(2,1)S(1)}, bf16[256,1024]{1,0:T(8,128)(2,1)S(1)}, u32[]{:S(2)}, u32[]{:S(2)}) collective-permute-start(bf16[256,1024]{1,0:T(8,128)(2,1)S(1)} %add_convert_fusion.2), channel_id=1, source_target_pairs={{1,24},{5,28},{9,17},{13,21},{17,10},{21,14},{25,3},{29,7}} | collective-permute-start | bytes 1572872 | tf_op jit(solution)/shard_map/ppermute | solution.py:153
  268.9 4.8 %collective-permute-done.39 = f32[2,128]{0,1:T(8,128)S(1)} collective-permute-done((f32[2,128]{0,1:T(8,128)S(1)}, f32[2,128]{0,1:T(8,128)S(1)}, u32[]{:S(2)}, u32[]{:S(2)}) %collective-permute-start.39) | collective-permute-done | bytes 1056 | tf_op jit(solution)/shard_map/ppermute | solution.py:153
  273.9 4.7 %multiply_multiply_fusion = (f32[512,1280]{1,0:T(8,128)}, f32[512,1280]{1,0:T(8,128)}) fusion(f32[1280]{0:T(1024)S(1)} %get-tuple-element.133, f32[512]{0:T(512)S(1)} %bitcast.52, f32[512,768]{1,0:T(8,128)S(1)} %add_multiply_fusion.1, f32[512,512]{1,0:T(8,128)S(1)} %add_multiply_fusion.2, f32[1280]{0:T(1024)S(1)} %get-tuple-element.134, ...), kind=kLoop, calls=%fused_computation.16 | loop fusion | flops 3276800 | bytes 10500096 | tf_op jit(solution)/shard_map/mul | solution.py:395
  (188 shorter events, 89.7 us)
Async XLA Ops:
  2.3 16.8 %collective-permute-start = (bf16[128,1024]{1,0:T(8,128)(2,1)S(1)}, bf16[128,1024]{1,0:T(8,128)(2,1)S(1)}, u32[]{:S(2)}, u32[]{:S(2)}) collective-permute-start(bf16[128,1024]{1,0:T(8,128)(2,1)S(1)} %get-tuple-element.146), channel_id=1, source_target_pairs={{0,8},{1,9},{2,10},{3,11},{4,12},{5,13},{6,14},{7,15},{8,0},{9,1},... | collective-permute-start | bytes 786440 | tf_op jit(solution)/shard_map/ppermute | solution.py:153
  4.5 14.7 %collective-permute-start.1 = (bf16[128,1024]{1,0:T(8,128)(2,1)S(1)}, bf16[128,1024]{1,0:T(8,128)(2,1)S(1)}, u32[]{:S(2)}, u32[]{:S(2)}) collective-permute-start(bf16[128,1024]{1,0:T(8,128)(2,1)S(1)} %get-tuple-element.145), channel_id=1, source_target_pairs={{0,16},{1,17},{2,18},{3,19},{4,20},{5,21},{6,22},{7,23},{8,24},{9,... | collective-permute-start | bytes 786440 | tf_op jit(solution)/shard_map/ppermute | solution.py:153
  6.8 16.9 %collective-permute-start.2 = (bf16[128,1024]{1,0:T(8,128)(2,1)S(1)}, bf16[128,1024]{1,0:T(8,128)(2,1)S(1)}, u32[]{:S(2)}, u32[]{:S(2)}) collective-permute-start(bf16[128,1024]{1,0:T(8,128)(2,1)S(1)} %get-tuple-element.144), channel_id=1, source_target_pairs={{0,24},{1,25},{2,26},{3,27},{4,28},{5,29},{6,30},{7,31},{8,16},{9,... | collective-permute-start | bytes 786440 | tf_op jit(solution)/shard_map/ppermute | solution.py:153
  23.7 33.4 %collective-permute-start.3 = (bf16[512,1280]{1,0:T(8,128)(2,1)}, bf16[512,1280]{1,0:T(8,128)(2,1)}, u32[]{:S(2)}, u32[]{:S(2)}) collective-permute-start(bf16[512,1280]{1,0:T(8,128)(2,1)} %shard_map.137), channel_id=1, source_target_pairs={{0,8},{1,9},{2,10},{3,11},{4,12},{5,13},{6,14},{7,15},{8,0},{9,1},... | collective-permute-start | bytes 3932168 | tf_op jit(solution)/shard_map/ppermute | solution.py:153
  29.5 27.6 %collective-permute-start.4 = (bf16[512,1280]{1,0:T(8,128)(2,1)}, bf16[512,1280]{1,0:T(8,128)(2,1)}, u32[]{:S(2)}, u32[]{:S(2)}) collective-permute-start(bf16[512,1280]{1,0:T(8,128)(2,1)} %shard_map.137), channel_id=1, source_target_pairs={{8,16},{9,17},{10,18},{11,19},{12,20},{13,21},{14,22},{15,23},{16,... | collective-permute-start | bytes 3932168 | tf_op jit(solution)/shard_map/ppermute | solution.py:153
  31.2 28.5 %collective-permute-start.5 = (bf16[512,1280]{1,0:T(8,128)(2,1)}, bf16[512,1280]{1,0:T(8,128)(2,1)}, u32[]{:S(2)}, u32[]{:S(2)}) collective-permute-start(bf16[512,1280]{1,0:T(8,128)(2,1)} %param.16), channel_id=1, source_target_pairs={{0,4},{1,5},{2,6},{3,7},{4,0},{5,1},{6,2},{7,3},{8,12},{9,13},{10,... | collective-permute-start | bytes 3932168 | tf_op jit(solution)/shard_map/ppermute | solution.py:153
  32.4 52.8 %collective-permute-start.8 = (bf16[512,1280]{1,0:T(8,128)(2,1)S(1)}, bf16[512,1280]{1,0:T(8,128)(2,1)}, u32[]{:S(2)}, u32[]{:S(2)}) collective-permute-start(bf16[512,1280]{1,0:T(8,128)(2,1)S(1)} %copy-done.8), channel_id=1, source_target_pairs={{0,8},{1,9},{2,10},{3,11},{4,12},{5,13},{6,14},{7,15},{8,0},{9,1},... | collective-permute-start | bytes 3932168 | tf_op jit(solution)/shard_map/ppermute | solution.py:153
  34.0 52.9 %collective-permute-start.9 = (bf16[512,1280]{1,0:T(8,128)(2,1)S(1)}, bf16[512,1280]{1,0:T(8,128)(2,1)S(1)}, u32[]{:S(2)}, u32[]{:S(2)}) collective-permute-start(bf16[512,1280]{1,0:T(8,128)(2,1)S(1)} %copy-done.8), channel_id=1, source_target_pairs={{8,16},{9,17},{10,18},{11,19},{12,20},{13,21},{14,22},{15,23},{16,... | collective-permute-start | bytes 3932168 | tf_op jit(solution)/shard_map/ppermute | solution.py:153
  59.7 27.6 %collective-permute-start.10 = (bf16[512,1280]{1,0:T(8,128)(2,1)}, bf16[512,1280]{1,0:T(8,128)(2,1)}, u32[]{:S(2)}, u32[]{:S(2)}) collective-permute-start(bf16[512,1280]{1,0:T(8,128)(2,1)} %param.17), channel_id=1, source_target_pairs={{0,4},{1,5},{2,6},{3,7},{4,0},{5,1},{6,2},{7,3},{8,12},{9,13},{10,... | collective-permute-start | bytes 3932168 | tf_op jit(solution)/shard_map/ppermute | solution.py:153
  60.9 26.0 %collective-permute-start.11 = (bf16[3,128,1024]{2,1,0:T(8,128)(2,1)S(1)}, bf16[3,128,1024]{2,1,0:T(8,128)(2,1)S(1)}, u32[]{:S(2)}, u32[]{:S(2)}) collective-permute-start(bf16[3,128,1024]{2,1,0:T(8,128)(2,1)S(1)} %pad_maximum_fusion.10), channel_id=1, source_target_pairs={{0,2},{1,3},{2,0},{3,1},{4,6},{5,7},{6,4},{7,5},{8,10},{9,11},{10,... | collective-permute-start | bytes 2359304 | tf_op jit(solution)/shard_map/ppermute | solution.py:153
  63.8 49.4 %collective-permute-start.6 = (bf16[512,1280]{1,0:T(8,128)(2,1)}, bf16[512,1280]{1,0:T(8,128)(2,1)}, u32[]{:S(2)}, u32[]{:S(2)}) collective-permute-start(bf16[512,1280]{1,0:T(8,128)(2,1)} %collective-permute-done.4), channel_id=1, source_target_pairs={{8,0},{9,1},{10,2},{11,3},{12,4},{13,5},{14,6},{15,7},{16,24},{17,... | collective-permute-start | bytes 3932168 | tf_op jit(solution)/shard_map/ppermute | solution.py:153
  85.2 28.1 %collective-permute-start.7 = (bf16[512,1280]{1,0:T(8,128)(2,1)}, bf16[512,1280]{1,0:T(8,128)(2,1)}, u32[]{:S(2)}, u32[]{:S(2)}) collective-permute-start(bf16[512,1280]{1,0:T(8,128)(2,1)} %collective-permute-done.3), channel_id=1, source_target_pairs={{8,16},{9,17},{10,18},{11,19},{12,20},{13,21},{14,22},{15,23},{16,... | collective-permute-start | bytes 3932168 | tf_op jit(solution)/shard_map/ppermute | solution.py:153
  87.4 25.9 %collective-permute-start.12 = (bf16[2,3,128,1024]{3,2,1,0:T(8,128)(2,1)S(1)}, bf16[2,3,128,1024]{3,2,1,0:T(8,128)(2,1)}, u32[]{:S(2)}, u32[]{:S(2)}) collective-permute-start(bf16[2,3,128,1024]{3,2,1,0:T(8,128)(2,1)S(1)} %pad_maximum_fusion.8), channel_id=1, source_target_pairs={{0,1},{1,0},{2,3},{3,2},{4,5},{5,4},{6,7},{7,6},{8,9},{9,8},{10,11... | collective-permute-start | bytes 4718600 | tf_op jit(solution)/shard_map/ppermute | solution.py:153
  107.7 25.0 %collective-permute-start.15 = (bf16[512,1280]{1,0:T(8,128)(2,1)}, bf16[512,1280]{1,0:T(8,128)(2,1)S(1)}, u32[]{:S(2)}, u32[]{:S(2)}) collective-permute-start(bf16[512,1280]{1,0:T(8,128)(2,1)} %collective-permute-done.8), channel_id=1, source_target_pairs={{8,16},{9,17},{10,18},{11,19},{12,20},{13,21},{14,22},{15,23},{16,... | collective-permute-start | bytes 3932168 | tf_op jit(solution)/shard_map/ppermute | solution.py:153
  115.0 17.5 %collective-permute-start.17 = (bf16[256,1024]{1,0:T(8,128)(2,1)S(1)}, bf16[256,1024]{1,0:T(8,128)(2,1)S(1)}, u32[]{:S(2)}, u32[]{:S(2)}) collective-permute-start(bf16[256,1024]{1,0:T(8,128)(2,1)S(1)} %dynamic-slice_convert_fusion.2), channel_id=1, source_target_pairs={{0,2},{1,3},{2,0},{3,1},{4,6},{5,7},{6,4},{7,5},{8,10},{9,11},{10,... | collective-permute-start | bytes 1572872 | tf_op jit(solution)/shard_map/ppermute | solution.py:153
  116.3 26.1 %collective-permute-start.16 = (bf16[512,1280]{1,0:T(8,128)(2,1)}, bf16[512,1280]{1,0:T(8,128)(2,1)S(1)}, u32[]{:S(2)}, u32[]{:S(2)}) collective-permute-start(bf16[512,1280]{1,0:T(8,128)(2,1)} %collective-permute-done.7), channel_id=1, source_target_pairs={{8,0},{9,1},{10,2},{11,3},{12,4},{13,5},{14,6},{15,7},{16,24},{17,... | collective-permute-start | bytes 3932168 | tf_op jit(solution)/shard_map/ppermute | solution.py:153
  119.6 50.9 %collective-permute-start.14 = (bf16[512,1280]{1,0:T(8,128)(2,1)S(1)}, bf16[512,1280]{1,0:T(8,128)(2,1)S(1)}, u32[]{:S(2)}, u32[]{:S(2)}) collective-permute-start(bf16[512,1280]{1,0:T(8,128)(2,1)S(1)} %collective-permute-done.9), channel_id=1, source_target_pairs={{8,0},{9,1},{10,2},{11,3},{12,4},{13,5},{14,6},{15,7},{16,24},{17,... | collective-permute-start | bytes 3932168 | tf_op jit(solution)/shard_map/ppermute | solution.py:153
  142.4 39.3 %collective-permute-start.18 = (bf16[256,1024]{1,0:T(8,128)(2,1)S(1)}, bf16[256,1024]{1,0:T(8,128)(2,1)S(1)}, u32[]{:S(2)}, u32[]{:S(2)}) collective-permute-start(bf16[256,1024]{1,0:T(8,128)(2,1)S(1)} %add_convert_fusion.5), channel_id=1, source_target_pairs={{0,0},{1,8},{4,4},{5,12},{8,9},{9,1},{12,13},{13,5},{16,18},{17,26... | collective-permute-start | bytes 1572872 | tf_op jit(solution)/shard_map/ppermute | solution.py:153
  158.9 22.8 %collective-permute-start.19 = (bf16[256,1024]{1,0:T(8,128)(2,1)S(1)}, bf16[256,1024]{1,0:T(8,128)(2,1)S(1)}, u32[]{:S(2)}, u32[]{:S(2)}) collective-permute-start(bf16[256,1024]{1,0:T(8,128)(2,1)S(1)} %add_convert_fusion.5), channel_id=1, source_target_pairs={{2,0},{3,8},{6,4},{7,12},{10,9},{11,1},{14,13},{15,5},{18,18},{19,... | collective-permute-start | bytes 1572872 | tf_op jit(solution)/shard_map/ppermute | solution.py:153
  163.1 37.2 %collective-permute-start.22 = (bf16[512,1280]{1,0:T(8,128)(2,1)S(1)}, bf16[512,1280]{1,0:T(8,128)(2,1)S(1)}, u32[]{:S(2)}, u32[]{:S(2)}) collective-permute-start(bf16[512,1280]{1,0:T(8,128)(2,1)S(1)} %add_convert_fusion), channel_id=1, source_target_pairs={{0,4},{1,5},{2,6},{3,7},{4,0},{5,1},{6,2},{7,3},{8,12},{9,13},{10,... | collective-permute-start | bytes 3932168 | tf_op jit(solution)/shard_map/ppermute | solution.py:153
  164.4 35.9 %collective-permute-start.21 = (bf16[512,512]{1,0:T(8,128)(2,1)S(1)}, bf16[512,512]{1,0:T(8,128)(2,1)S(1)}, u32[]{:S(2)}, u32[]{:S(2)}) collective-permute-start(bf16[512,512]{1,0:T(8,128)(2,1)S(1)} %slice.129), channel_id=1, source_target_pairs={{8,0},{9,1},{10,2},{11,3},{12,4},{13,5},{14,6},{15,7},{16,24},{17,... | collective-permute-start | bytes 1572872 | tf_op jit(solution)/shard_map/ppermute | solution.py:153
  185.4 15.0 %collective-permute-start.20 = (bf16[512,1024]{1,0:T(8,128)(2,1)S(1)}, bf16[512,1024]{1,0:T(8,128)(2,1)S(1)}, u32[]{:S(2)}, u32[]{:S(2)}) collective-permute-start(bf16[512,1024]{1,0:T(8,128)(2,1)S(1)} %get-tuple-element.153), channel_id=1, source_target_pairs={{1,0},{3,2},{5,4},{7,6},{9,8},{11,10},{13,12},{15,14},{17,16},{19,... | collective-permute-start | bytes 3145736 | tf_op jit(solution)/shard_map/ppermute | solution.py:153
  191.5 21.2 %collective-permute-start.24 = (bf16[512,768]{1,0:T(8,128)(2,1)S(1)}, bf16[512,768]{1,0:T(8,128)(2,1)S(1)}, u32[]{:S(2)}, u32[]{:S(2)}) collective-permute-start(bf16[512,768]{1,0:T(8,128)(2,1)S(1)} %slice.134), channel_id=1, source_target_pairs={{8,0},{9,1},{10,2},{11,3},{12,4},{13,5},{14,6},{15,7},{16,24},{17,... | collective-permute-start | bytes 2359304 | tf_op jit(solution)/shard_map/ppermute | solution.py:153
  200.7 12.0 %collective-permute-start.25 = (bf16[256,1024]{1,0:T(8,128)(2,1)S(1)}, bf16[256,1024]{1,0:T(8,128)(2,1)S(1)}, u32[]{:S(2)}, u32[]{:S(2)}) collective-permute-start(bf16[256,1024]{1,0:T(8,128)(2,1)S(1)} %dynamic-slice_convert_fusion.1), channel_id=1, source_target_pairs={{0,2},{2,0},{4,6},{6,4},{8,10},{10,8},{12,14},{14,12},{16,18},{18,... | collective-permute-start | bytes 1572872 | tf_op jit(solution)/shard_map/ppermute | solution.py:153
  202.7 12.4 %collective-permute-start.23 = (bf16[512,512]{1,0:T(8,128)(2,1)S(1)}, bf16[512,512]{1,0:T(8,128)(2,1)S(1)}, u32[]{:S(2)}, u32[]{:S(2)}) collective-permute-start(bf16[512,512]{1,0:T(8,128)(2,1)S(1)} %add_convert_fusion.4), channel_id=1, source_target_pairs={{0,4},{1,5},{2,6},{3,7},{4,0},{5,1},{6,2},{7,3},{8,12},{9,13},{10,... | collective-permute-start | bytes 1572872 | tf_op jit(solution)/shard_map/ppermute | solution.py:153
  218.7 7.8 %collective-permute-start.29 = (bf16[256,1024]{1,0:T(8,128)(2,1)S(1)}, bf16[256,1024]{1,0:T(8,128)(2,1)S(1)}, u32[]{:S(2)}, u32[]{:S(2)}) collective-permute-start(bf16[256,1024]{1,0:T(8,128)(2,1)S(1)} %add_convert_fusion.3), channel_id=1, source_target_pairs={{0,16},{4,20},{8,25},{12,29},{16,2},{20,6},{24,11},{28,15}} | collective-permute-start | bytes 1572872 | tf_op jit(solution)/shard_map/ppermute | solution.py:153
  219.4 7.1 %collective-permute-start.30 = (bf16[256,1024]{1,0:T(8,128)(2,1)S(1)}, bf16[256,1024]{1,0:T(8,128)(2,1)S(1)}, u32[]{:S(2)}, u32[]{:S(2)}) collective-permute-start(bf16[256,1024]{1,0:T(8,128)(2,1)S(1)} %add_convert_fusion.3), channel_id=1, source_target_pairs={{2,16},{6,20},{10,25},{14,29},{18,2},{22,6},{26,11},{30,15}} | collective-permute-start | bytes 1572872 | tf_op jit(solution)/shard_map/ppermute | solution.py:153
  220.8 12.4 %collective-permute-start.28 = (bf16[512,768]{1,0:T(8,128)(2,1)S(1)}, bf16[512,768]{1,0:T(8,128)(2,1)S(1)}, u32[]{:S(2)}, u32[]{:S(2)}) collective-permute-start(bf16[512,768]{1,0:T(8,128)(2,1)S(1)} %add_convert_fusion.1), channel_id=1, source_target_pairs={{0,4},{1,5},{2,6},{3,7},{4,0},{5,1},{6,2},{7,3},{8,12},{9,13},{10,... | collective-permute-start | bytes 2359304 | tf_op jit(solution)/shard_map/ppermute | solution.py:153
  224.2 13.6 %collective-permute-start.27 = (bf16[256,1024]{1,0:T(8,128)(2,1)S(1)}, bf16[256,1024]{1,0:T(8,128)(2,1)}, u32[]{:S(2)}, u32[]{:S(2)}) collective-permute-start(bf16[256,1024]{1,0:T(8,128)(2,1)S(1)} %dynamic-slice_convert_fusion), channel_id=1, source_target_pairs={{1,3},{3,1},{5,7},{7,5},{9,11},{11,9},{13,15},{15,13},{17,19},{19,... | collective-permute-start | bytes 1572872 | tf_op jit(solution)/shard_map/ppermute | solution.py:153
  255.1 12.0 %collective-permute-start.38 = (f32[2,128]{0,1:T(8,128)S(1)}, f32[2,128]{0,1:T(8,128)S(1)}, u32[]{:S(2)}, u32[]{:S(2)}) collective-permute-start(f32[2,128]{0,1:T(8,128)S(1)} %broadcast_in_dim.20), channel_id=1, source_target_pairs={{0,1},{1,0},{2,3},{3,2},{4,5},{5,4},{6,7},{7,6},{8,9},{9,8},{10,11... | collective-permute-start | bytes 3080 | tf_op jit(solution)/shard_map/ppermute | solution.py:153
  261.3 17.2 %collective-permute-start.31 = (bf16[256,1024]{1,0:T(8,128)(2,1)S(1)}, bf16[256,1024]{1,0:T(8,128)(2,1)S(1)}, u32[]{:S(2)}, u32[]{:S(2)}) collective-permute-start(bf16[256,1024]{1,0:T(8,128)(2,1)S(1)} %add_convert_fusion.2), channel_id=1, source_target_pairs={{1,24},{5,28},{9,17},{13,21},{17,10},{21,14},{25,3},{29,7}} | collective-permute-start | bytes 1572872 | tf_op jit(solution)/shard_map/ppermute | solution.py:153
  266.3 12.3 %collective-permute-start.32 = (bf16[256,1024]{1,0:T(8,128)(2,1)S(1)}, bf16[256,1024]{1,0:T(8,128)(2,1)S(1)}, u32[]{:S(2)}, u32[]{:S(2)}) collective-permute-start(bf16[256,1024]{1,0:T(8,128)(2,1)S(1)} %add_convert_fusion.2), channel_id=1, source_target_pairs={{3,24},{7,28},{11,17},{15,21},{19,10},{23,14},{27,3},{31,7}} | collective-permute-start | bytes 1572872 | tf_op jit(solution)/shard_map/ppermute | solution.py:153
  (35 other events, 355.8 us)
